TPU v7x, 256 devices: a whole 4x4x8 slice. The times are simulated.
256 devices in a mesh: gx: 16 (over x, y), gy: 16 (over z, core).
Axes of the slice: x: 4, y: 4, z: 8, core: 2. Of those that a mesh axis runs over, the one named last changes fastest.
Arguments:
- labels: int32 [32, 256, 2048], P(None, 'gx', 'gy'), may hold values from 0 to 2, as said below
- conduct_x: bfloat16 [32, 256, 2048], P(None, 'gx', 'gy'), may hold values from 0.0099487305 to 1
- conduct_y: bfloat16 [32, 256, 2048], P(None, 'gx', 'gy'), may hold values from 0.0099487305 to 1
- conduct_z: bfloat16 [32, 256, 2048], P(None, 'gx', 'gy'), may hold values from 0.0009994507 to 0.099609375
Outputs:
- potential: float32 [32, 256, 2048], P(None, 'gx', 'gy')
Inputs may be any that keep to these rules, and one draw needn't show every extreme that they name: `labels`: 0 marks a free voxel, 1 a seed of the first object, 2 a seed of the second.
All inputs are finite; a program needn't handle non-finite values.
Results may differ from a plain program's by a relative error of at most 0.0003.
Values sent between devices are 32-bit elements; how exact they have to be, the bound alone decides.
No kernel may reach another device: no remote copies, remote signals or barrier semaphores. Data moves between devices by JAX's collectives and lax.ppermute only.
A program may use at most 64 MiB of HBM per device.

v0:
```python
import jax
import jax.numpy as jnp
from jax import lax
from jax.sharding import PartitionSpec as P

NU = 4
COARSE_SWEEPS = 24


OMEGA = 0.8
LEAK = 0.005


def extended(cells, sides, width):
    for axis, dim in sides:
        count = lax.axis_size(axis)
        ends = count - 1
        head = lax.slice_in_dim(cells, 0, width, axis=dim)
        tail = lax.slice_in_dim(cells, cells.shape[dim] - width, cells.shape[dim], axis=dim)
        cells = jnp.concatenate(
            [
                lax.ppermute(tail, axis, [(i, (i + 1) % count) for i in range(ends)]),
                cells,
                lax.ppermute(head, axis, [((i + 1) % count, i) for i in range(ends)]),
            ],
            axis=dim,
        )
    return cells


def from_behind(block, axis, distance):
    devices = range(lax.axis_size(axis))
    route = [(i - distance, i) for i in devices if i - distance in devices]
    return lax.ppermute(block, axis, route)


def below_z(field):
    return jnp.concatenate([jnp.zeros_like(field[:1]), field[:-1]], 0)


def apply_operator(field, padded, operator):
    fwd_x, back_x, fwd_y, back_y, fwd_z, back_z, diagonal, divisor = operator
    beside_all = fwd_x * padded[:, 2:, 1:-1] + back_x * padded[:, :-2, 1:-1]
    beside_all = beside_all + fwd_y * padded[:, 1:-1, 2:] + back_y * padded[:, 1:-1, :-2]
    upper = jnp.concatenate([field[1:], jnp.zeros_like(field[:1])], 0)
    beside_all = beside_all + fwd_z * upper + back_z * below_z(field)
    return diagonal * field - beside_all


def relax(field, padded, rhs, operator):
    return field + OMEGA * (rhs - apply_operator(field, padded, operator)) / operator[7]


def grid_rim(field):
    return extended(field, (("gx", 1), ("gy", 2)), 1)


def back_planes(fwd_x, fwd_y):
    from_x = from_behind(fwd_x[:, -1:, :], "gx", 1)
    from_y = from_behind(fwd_y[:, :, -1:], "gy", 1)
    return (
        jnp.concatenate([from_x, fwd_x[:, :-1, :]], 1),
        jnp.concatenate([from_y, fwd_y[:, :, :-1]], 2),
    )


def make_operator(fwd_x, back_x, fwd_y, back_y, fwd_z, extra, free):
    back_z = below_z(fwd_z)
    diagonal = fwd_x.astype(jnp.float32) + back_x.astype(jnp.float32)
    diagonal = diagonal + fwd_y.astype(jnp.float32) + back_y.astype(jnp.float32)
    diagonal = diagonal + fwd_z.astype(jnp.float32) + back_z.astype(jnp.float32) + extra
    divisor = diagonal + 1.0 - free
    return (fwd_x, back_x, fwd_y, back_y, fwd_z, back_z, diagonal, divisor)


def blocks(field):
    depth, rows, cols = field.shape
    return field.astype(jnp.float32).reshape(depth, rows // 2, 2, cols // 2, 2)


def coarse_solve(rhs, operator):
    first_step = OMEGA * rhs / operator[7]

    def tile_sweep(count, field):
        padded = extended(field, (("gx", 1), ("gy", 2)), 1)
        return relax(field, padded, rhs, operator)

    return lax.fori_loop(0, COARSE_SWEEPS - 1, tile_sweep, first_step)


def vcycle(level, rhs, operators, masks):
    operator = operators[level]
    if level == 3:
        return coarse_solve(rhs, operator)
    field = OMEGA * rhs / operator[7]
    for sweep in range(NU - 1):
        field = relax(field, grid_rim(field), rhs, operator)
    residual = rhs - apply_operator(field, grid_rim(field), operator)
    coarse = vcycle(level + 1, blocks(residual).sum((2, 4)), operators, masks)
    field = field + jnp.repeat(jnp.repeat(coarse, 2, 1), 2, 2) * masks[level]
    for sweep in range(NU):
        field = relax(field, grid_rim(field), rhs, operator)
    return field


def body(labels, conduct_x, conduct_y, conduct_z):
    depth, rows, cols = labels.shape
    rim = extended(labels, (("gx", 1), ("gy", 2)), 1)
    rim = jnp.pad(rim, ((1, 1), (0, 0), (0, 0)), constant_values=2)
    pad_free = (rim == 0).astype(jnp.float32)
    pad_first = (rim == 1).astype(jnp.float32)
    free = pad_free[1:-1, 1:-1, 1:-1]
    zero_bf = jnp.zeros((), jnp.bfloat16)
    row_index = lax.broadcasted_iota(jnp.int32, labels.shape, 1)
    col_index = lax.broadcasted_iota(jnp.int32, labels.shape, 2)
    depth_index = lax.broadcasted_iota(jnp.int32, labels.shape, 0)
    last_x = lax.axis_index("gx") == lax.axis_size("gx") - 1
    last_y = lax.axis_index("gy") == lax.axis_size("gy") - 1
    cond_x = jnp.where(last_x & (row_index == rows - 1), zero_bf, conduct_x)
    cond_y = jnp.where(last_y & (col_index == cols - 1), zero_bf, conduct_y)
    cond_z = jnp.where(depth_index == depth - 1, zero_bf, conduct_z)
    raw_back_x, raw_back_y = back_planes(cond_x.astype(jnp.float32), cond_y.astype(jnp.float32))
    views = [
        (slice(1, -1), slice(2, None), slice(1, -1)),
        (slice(1, -1), slice(None, -2), slice(1, -1)),
        (slice(1, -1), slice(1, -1), slice(2, None)),
        (slice(1, -1), slice(1, -1), slice(None, -2)),
        (slice(2, None), slice(1, -1), slice(1, -1)),
        (slice(None, -2), slice(1, -1), slice(1, -1)),
    ]
    edges = [cond_x, raw_back_x, cond_y, raw_back_y, cond_z, below_z(cond_z)]
    extra = jnp.full(free.shape, LEAK, jnp.float32)
    rhs = jnp.zeros(free.shape, jnp.float32)
    for edge, view in zip(edges, views):
        extra = extra + edge.astype(jnp.float32) * (1.0 - pad_free[view])
        rhs = rhs + edge.astype(jnp.float32) * pad_first[view]
    extra = free * extra
    rhs = free * rhs
    fwd_x = cond_x * (free * pad_free[views[0]]).astype(jnp.bfloat16)
    back_x = raw_back_x.astype(jnp.bfloat16) * (free * pad_free[views[1]]).astype(jnp.bfloat16)
    fwd_y = cond_y * (free * pad_free[views[2]]).astype(jnp.bfloat16)
    back_y = raw_back_y.astype(jnp.bfloat16) * (free * pad_free[views[3]]).astype(jnp.bfloat16)
    fwd_z = cond_z * (free * pad_free[views[4]]).astype(jnp.bfloat16)
    operators = [make_operator(fwd_x, back_x, fwd_y, back_y, fwd_z, extra, free)]
    masks = [free]
    level_x, level_y, level_z, level_extra, level_free = (fwd_x, fwd_y, fwd_z, extra, free)
    for level in range(3):
        level_x = blocks(level_x)[:, :, 1, :, :].sum(3)
        level_y = blocks(level_y)[:, :, :, :, 1].sum(2)
        level_z = blocks(level_z).sum((2, 4))
        level_extra = blocks(level_extra).sum((2, 4))
        level_free = blocks(level_free).max((2, 4))
        coarse_back_x, coarse_back_y = back_planes(level_x, level_y)
        operators.append(
            make_operator(
                level_x, coarse_back_x, level_y, coarse_back_y, level_z, level_extra, level_free
            )
        )
        masks.append(level_free)
    return vcycle(0, rhs, operators, masks)


def solution(mesh):
    in_specs = (P(None, "gx", "gy"), P(None, "gx", "gy"), P(None, "gx", "gy"), P(None, "gx", "gy"))
    out_specs = P(None, "gx", "gy")
    return jax.shard_map(body, mesh=mesh, in_specs=in_specs, out_specs=out_specs, check_vma=False)
```

profile of v0, /device:TPU:152, one launch (start us, length us, event | category | flops | bytes accessed | tf_op | source)
XLA Modules:
  0.0 1055.5 jit_solution(10717009590653365340)
XLA Ops:
  7.1 5.2 collective-permute-start.8
  23.8 5.0 collective-permute-done.6
  49.6 5.0 collective-permute-done.13
  71.5 5.0 collective-permute-done.17
  79.4 6.0 collective-permute-start.19
  94.2 5.0 collective-permute-done.21
  101.5 5.2 collective-permute-start.23
  116.7 6.0 collective-permute-start.26
  150.5 6.0 collective-permute-start.29
  169.3 6.3 collective-permute-start.33
  189.5 6.3 collective-permute-start.37
  209.3 6.3 collective-permute-start.41
  240.4 6.0 collective-permute-start.47
  258.9 6.3 collective-permute-start.51
  278.7 6.3 collective-permute-start.55
  307.7 6.0 collective-permute-start.59
  327.7 481.5 %while.10 = (s32[]{:T(128)}, f32[32,2,16]{0,2,1:T(8,128)}, f32[32,2,16]{0,2,1:T(8,128)}, f32[32,2,16]{0,2,1:T(8,128)}, f32[32,2,16]{0,2,1:T(8,128)}, /*index=5*/...) while((s32[]{:T(128)}, f32[32,2,16]{0,2,1:T(8,128)}, ...), condition=%wide.region_19.20_spmd, body=%wide.region_18.19_spmd.sunk | while | flops 21506 | bytes 246405 | solution.py:88
  328.4 6.2 collective-permute-start
  337.2 5.1 collective-permute-done.1
  812.0 6.0 collective-permute-start.65
  830.5 6.3 collective-permute-start.69
  849.2 6.3 collective-permute-start.73
  867.8 6.3 collective-permute-start.77
  887.5 6.3 collective-permute-start.81
  906.0 6.3 collective-permute-start.85
  924.4 6.3 collective-permute-start.89
  942.9 6.3 collective-permute-start.93
  961.0 6.3 collective-permute-start.97
  969.4 5.7 collective-permute-done.96
  982.9 5.0 collective-permute-done.99
  1026.8 5.0 collective-permute-done.107
  1048.7 5.0 collective-permute-done.111
  (1058 shorter events, 869.7 us)
Async XLA Ops:
  1.0 13.4 %collective-permute-start.4 = (s32[32,1,128]{2,0,1:T(8,128)S(1)}, s32[32,1,128]{2,0,1:T(8,128)S(1)}, u32[]{:S(2)}, u32[]{:S(2)}) collective-permute-start(s32[32,1,128]{2,0,1:T(8,128)S(1)} %copy.332), channel_id=1, source_target_pairs={{0,16},{16,32},{32,48},{48,64},{64,80},{80,96},{96,112},{112,128},... | collective-permute-start | bytes 49160 | tf_op jit(solution)/shard_map/ppermute | solution.py:22
  4.1 10.4 collective-permute-start.5
  7.1 23.6 %collective-permute-start.8 = (f32[32,1,128]{2,1,0:T(1,128)S(1)}, f32[32,1,128]{2,1,0:T(1,128)S(1)}, u32[]{:S(2)}, u32[]{:S(2)}) collective-permute-start(f32[32,1,128]{2,1,0:T(1,128)S(1)} %slice.1279), channel_id=1, source_target_pairs={{0,16},{16,32},{32,48},{48,64},{64,80},{80,96},{96,112},{112,128},... | collective-permute-start | bytes 49160 | tf_op jit(solution)/shard_map/ppermute | solution.py:34
  12.5 18.2 %collective-permute-start.9 = (f32[32,16,1]{2,1,0:T(8,128)S(1)}, f32[32,16,1]{2,1,0:T(8,128)S(1)}, u32[]{:S(2)}, u32[]{:S(2)}) collective-permute-start(f32[32,16,1]{2,1,0:T(8,128)S(1)} %slice.1283), channel_id=1, source_target_pairs={{0,1},{1,2},{2,3},{3,4},{4,5},{5,6},{6,7},{7,8},{8,9},{9,10},{10,1... | collective-permute-start | bytes 6152 | tf_op jit(solution)/shard_map/ppermute | solution.py:34
  14.7 9.1 collective-permute-start.7
  19.6 9.3 collective-permute-start.6
  45.4 9.3 collective-permute-start.13
  67.3 9.3 collective-permute-start.17
  77.5 10.4 collective-permute-start.18
  90.0 9.3 collective-permute-start.21
  101.5 23.3 %collective-permute-start.23 = (f32[32,1,128]{2,1,0:T(1,128)}, f32[32,1,128]{2,1,0:T(1,128)S(1)}, u32[]{:S(2)}, u32[]{:S(2)}) collective-permute-start(f32[32,1,128]{2,1,0:T(1,128)} %get-tuple-element.208), channel_id=1, source_target_pairs={{0,16},{16,32},{32,48},{48,64},{64,80},{80,96},{96,112},{112,128},... | collective-permute-start | bytes 49160 | tf_op jit(solution)/shard_map/ppermute | solution.py:22
  106.8 18.0 %collective-permute-start.22 = (f32[32,1,128]{2,1,0:T(1,128)S(1)}, f32[32,1,128]{2,1,0:T(1,128)S(1)}, u32[]{:S(2)}, u32[]{:S(2)}) collective-permute-start(f32[32,1,128]{2,1,0:T(1,128)S(1)} %get-tuple-element.207), channel_id=1, source_target_pairs={{16,0},{32,16},{48,32},{64,48},{80,64},{96,80},{112,96},{128,112},... | collective-permute-start | bytes 49160 | tf_op jit(solution)/shard_map/ppermute | solution.py:24
  116.7 31.3 %collective-permute-start.26 = (f32[32,1,64]{0,2,1:T(8,128)S(1)}, f32[32,1,64]{0,2,1:T(8,128)S(1)}, u32[]{:S(2)}, u32[]{:S(2)}) collective-permute-start(f32[32,1,64]{0,2,1:T(8,128)S(1)} %slice.1321), channel_id=1, source_target_pairs={{0,16},{16,32},{32,48},{48,64},{64,80},{80,96},{96,112},{112,128},... | collective-permute-start | bytes 24584 | tf_op jit(solution)/shard_map/ppermute | solution.py:34
  122.7 25.2 %collective-permute-start.27 = (f32[32,8,1]{0,2,1:T(1,128)S(1)}, f32[32,8,1]{0,2,1:T(1,128)S(1)}, u32[]{:S(2)}, u32[]{:S(2)}) collective-permute-start(f32[32,8,1]{0,2,1:T(1,128)S(1)} %slice.1324), channel_id=1, source_target_pairs={{0,1},{1,2},{2,3},{3,4},{4,5},{5,6},{6,7},{7,8},{8,9},{9,10},{10,1... | collective-permute-start | bytes 3080 | tf_op jit(solution)/shard_map/ppermute | solution.py:34
  126.4 12.1 %collective-permute-start.24 = (f32[32,18,1]{2,0,1:T(8,128)}, f32[32,18,1]{2,0,1:T(8,128)}, u32[]{:S(2)}, u32[]{:S(2)}) collective-permute-start(f32[32,18,1]{2,0,1:T(8,128)} %get-tuple-element.141), channel_id=1, source_target_pairs={{1,0},{2,1},{3,2},{4,3},{5,4},{6,5},{7,6},{8,7},{9,8},{10,9},{11,1... | collective-permute-start | bytes 6920 | tf_op jit(solution)/shard_map/ppermute | solution.py:24
  131.3 9.6 collective-permute-start.25
  167.4 8.5 collective-permute-start.32
  187.6 8.6 collective-permute-start.36
  207.4 17.4 %collective-permute-start.40 = (f32[32,1,64]{0,2,1:T(8,128)}, f32[32,1,64]{0,2,1:T(8,128)}, u32[]{:S(2)}, u32[]{:S(2)}) collective-permute-start(f32[32,1,64]{0,2,1:T(8,128)} %get-tuple-element.192), channel_id=1, source_target_pairs={{16,0},{32,16},{48,32},{64,48},{80,64},{96,80},{112,96},{128,112},... | collective-permute-start | bytes 24584 | tf_op jit(solution)/shard_map/ppermute | solution.py:24
  209.3 15.5 %collective-permute-start.41 = (f32[32,1,64]{0,2,1:T(8,128)}, f32[32,1,64]{0,2,1:T(8,128)}, u32[]{:S(2)}, u32[]{:S(2)}) collective-permute-start(f32[32,1,64]{0,2,1:T(8,128)} %get-tuple-element.191), channel_id=1, source_target_pairs={{0,16},{16,32},{32,48},{48,64},{64,80},{80,96},{96,112},{112,128},... | collective-permute-start | bytes 24584 | tf_op jit(solution)/shard_map/ppermute | solution.py:22
  217.5 19.9 %collective-permute-start.44 = (f32[32,1,32]{0,2,1:T(8,128)}, f32[32,1,32]{0,2,1:T(8,128)}, u32[]{:S(2)}, u32[]{:S(2)}) collective-permute-start(f32[32,1,32]{0,2,1:T(8,128)} %slice.1344), channel_id=1, source_target_pairs={{0,16},{16,32},{32,48},{48,64},{64,80},{80,96},{96,112},{112,128},... | collective-permute-start | bytes 12296 | tf_op jit(solution)/shard_map/ppermute | solution.py:34
  222.0 15.4 %collective-permute-start.45 = (f32[32,4,1]{0,2,1:T(1,128)}, f32[32,4,1]{0,2,1:T(1,128)}, u32[]{:S(2)}, u32[]{:S(2)}) collective-permute-start(f32[32,4,1]{0,2,1:T(1,128)} %slice.1347), channel_id=1, source_target_pairs={{0,1},{1,2},{2,3},{3,4},{4,5},{5,6},{6,7},{7,8},{8,9},{9,10},{10,1... | collective-permute-start | bytes 1544 | tf_op jit(solution)/shard_map/ppermute | solution.py:34
  256.9 8.9 collective-permute-start.50
  276.8 18.8 %collective-permute-start.54 = (f32[32,1,32]{0,2,1:T(8,128)}, f32[32,1,32]{0,2,1:T(8,128)}, u32[]{:S(2)}, u32[]{:S(2)}) collective-permute-start(f32[32,1,32]{0,2,1:T(8,128)} %get-tuple-element.262), channel_id=1, source_target_pairs={{16,0},{32,16},{48,32},{64,48},{80,64},{96,80},{112,96},{128,112},... | collective-permute-start | bytes 12296 | tf_op jit(solution)/shard_map/ppermute | solution.py:24
  278.7 16.9 %collective-permute-start.55 = (f32[32,1,32]{0,2,1:T(8,128)}, f32[32,1,32]{0,2,1:T(8,128)}, u32[]{:S(2)}, u32[]{:S(2)}) collective-permute-start(f32[32,1,32]{0,2,1:T(8,128)} %get-tuple-element.261), channel_id=1, source_target_pairs={{0,16},{16,32},{32,48},{48,64},{64,80},{80,96},{96,112},{112,128},... | collective-permute-start | bytes 12296 | tf_op jit(solution)/shard_map/ppermute | solution.py:22
  287.0 26.7 %collective-permute-start.62 = (f32[32,1,16]{0,2,1:T(8,128)}, f32[32,1,16]{0,2,1:T(8,128)}, u32[]{:S(2)}, u32[]{:S(2)}) collective-permute-start(f32[32,1,16]{0,2,1:T(8,128)} %get-tuple-element.273), channel_id=1, source_target_pairs={{0,16},{16,32},{32,48},{48,64},{64,80},{80,96},{96,112},{112,128},... | collective-permute-start | bytes 6152 | tf_op jit(solution)/shard_map/ppermute | solution.py:34
  292.2 21.5 %collective-permute-start.63 = (f32[32,2,1]{0,2,1:T(1,128)}, f32[32,2,1]{0,2,1:T(1,128)}, u32[]{:S(2)}, u32[]{:S(2)}) collective-permute-start(f32[32,2,1]{0,2,1:T(1,128)} %slice.1370), channel_id=1, source_target_pairs={{0,1},{1,2},{2,3},{3,4},{4,5},{5,6},{6,7},{7,8},{8,9},{9,10},{10,1... | collective-permute-start | bytes 776 | tf_op jit(solution)/shard_map/ppermute | solution.py:34
  305.6 9.6 collective-permute-start.58
  978.7 9.3 collective-permute-start.99
  1000.6 9.3 collective-permute-start.103
  1022.6 9.3 collective-permute-start.107
  1044.5 9.3 collective-permute-start.111
  (326 other events, 2287.2 us)
where the time goes:
time: 1080 us; the launch traced here: 1060 us
  starting transfers between devices  662 us (61%)
  waiting for transfers between devices  225 us (21%)
  other arithmetic  87.4 us (8%)
  local copies, waits for them, and re-layouts  76.4 us (7%)
    ppermute x96, starting transfers between devices, extended(): lax.ppermute(head, axis, [((i + 1) % count, i) for i in range(ends)])  362 us
    ppermute x96, starting transfers between devices, extended(): lax.ppermute(tail, axis, [(i, (i + 1) % count) for i in range(ends)])  273 us
    ppermute x96, waiting for transfers between devices, extended(): lax.ppermute(head, axis, [((i + 1) % count, i) for i in range(ends)])  163 us
    ppermute x96, waiting for transfers between devices, extended(): lax.ppermute(tail, axis, [(i, (i + 1) % count) for i in range(ends)])  61.3 us
    add x43, other arithmetic, relax(): field + OMEGA * (rhs - apply_operator(field, padded, operator)) / operato...  50 us
    while x253, local copies, waits for them, and re-layouts  29.8 us
    ppermute x8, starting transfers between devices, from_behind(): return lax.ppermute(block, axis, route)  26.7 us
  transfers between devices with their start and end apart: 200, of which 99 were waited for; matrix products, arithmetic and copies ran while one was open for 4% of the time, Pallas kernels for 0%

commit v1 on v0

v1 whole, which is shorter than its diff:
```python
import functools

import jax
import jax.numpy as jnp
from jax import lax
from jax.experimental import pallas as pl
from jax.experimental.pallas import tpu as pltpu
from jax.sharding import PartitionSpec as P

NU = 4
COARSE_SWEEPS = 24
OMEGA = 0.8
LEAK = 0.005

NZ = 32
H0 = 13
R0 = 16
N0 = R0 + 2 * H0
GROUPS = (N0 + 7) // 8
H1 = 6
N1 = 8 + 2 * H1
F32 = jnp.float32


def spec():
    return pl.BlockSpec(memory_space=pltpu.VMEM)


def call(kernel, ins, outs, scratch=(), limit=24, apart=()):
    places = [pl.BlockSpec(memory_space=pl.ANY) if i in apart else spec() for i in range(len(ins))]
    return pl.pallas_call(
        kernel,
        out_shape=[jax.ShapeDtypeStruct(s, F32) for s in outs],
        in_specs=places,
        out_specs=[spec() for _ in outs],
        scratch_shapes=[pltpu.VMEM(s, F32) if isinstance(s, tuple) else s for s in scratch],
        compiler_params=pltpu.CompilerParams(vmem_limit_bytes=limit * 1024 * 1024),
    )(*ins)


def lanes(shape):
    return lax.broadcasted_iota(jnp.int32, shape, len(shape) - 1)


def roll(value, shift, axis):
    size = value.shape[axis]
    shift = shift % size
    return value if shift == 0 else pltpu.roll(value, shift, axis)


def planes(lo, hi, body, step=16):
    whole = (hi - lo) // step

    def chunk(i, carry):
        for k in range(step):
            body(lo + i * step + k)
        return carry

    if whole == 1:
        chunk(0, 0)
    elif whole:
        lax.fori_loop(0, whole, chunk, 0)
    for p in range(lo + whole * step, hi):
        body(p)


def ahead_z(v):
    return jnp.concatenate([v[8:], roll(v[:8], -1, 0)], 0)


def behind_z(v):
    return jnp.concatenate([roll(v[24:], 1, 0), v[:24]], 0)


def neighbours(v_ref, fx, fy, fz, p):
    v = v_ref[p]
    s = fx[p] * v_ref[p + 1] + fx[p - 1] * v_ref[p - 1]
    cy = fy[p]
    s = s + cy * roll(v, -1, 1) + roll(cy * v, 1, 1)
    cz = fz[p]
    s = s + cz * ahead_z(v) + behind_z(cz * v)
    return v, s


def sweep(src, dst, f, g, fx, fy, fz, lo, hi, step=16):
    def body(p):
        v, s = neighbours(src, fx, fy, fz, p)
        dst[p] = (1.0 - OMEGA) * v + g[p] * (f[p] + s)

    planes(lo, hi, body, step)


def residual(src, dst, f, d, fx, fy, fz, lo, hi, step=16):
    def body(p):
        v, s = neighbours(src, fx, fy, fz, p)
        dst[p] = f[p] - d[p] * v + s

    planes(lo, hi, body, step)


def diagonal(extra, fx, fy, fz, p):
    cy, cz = fy[p], fz[p]
    return extra + fx[p] + fx[p - 1] + cy + roll(cy, 1, 1) + cz + behind_z(cz)


def scale_of(d):
    free = d > 0.0
    return jnp.where(free, OMEGA / jnp.where(free, d, 1.0), 0.0)


def selection(rows, cols, target, odd=False):
    row = lax.broadcasted_iota(jnp.int32, (rows, cols), 0)
    col = lax.broadcasted_iota(jnp.int32, (rows, cols), 1)
    hit = col == target(row)
    if odd:
        hit = hit & (row % 2 == 1)
    return hit.astype(F32)


def dot(a, matrix):
    matrix = matrix.astype(jnp.bfloat16)
    total = None
    for _ in range(3):
        part = a.astype(jnp.bfloat16)
        a = a - part.astype(F32)
        product = jnp.dot(part, matrix, preferred_element_type=F32)
        total = product if total is None else total + product
    return total


def fetch(pairs, sems):
    copies = [pltpu.make_async_copy(src, dst, sems.at[i]) for i, (src, dst) in enumerate(pairs)]
    for copy in copies:
        copy.start()
    return copies


def stage_kernel(
    in0, in1, in2, in3, own, to_right, to_left, labels, cond_x, cond_y, cond_z, sems
):
    copies = fetch(((in0, labels), (in1, cond_x), (in2, cond_y), (in3, cond_z)), sems)
    last_x = lax.axis_index("gx") == lax.axis_size("gx") - 1
    last_y = lax.axis_index("gy") == lax.axis_size("gy") - 1
    shape = (R0, 8, 128)
    row = lax.broadcasted_iota(jnp.int32, shape, 0)
    for a, ref in enumerate((labels, cond_x, cond_y, cond_z)):
        copies[a].wait()
        for b in range(4):
            value = jnp.stack([ref[4 * s + b].astype(F32) for s in range(8)])
            value = jnp.swapaxes(value, 0, 1)
            if a == 1:
                value = jnp.where(last_x & (row == R0 - 1), 0.0, value)
            if a == 2:
                value = jnp.where(last_y & (lanes(shape) == 127), 0.0, value)
            if a == 3 and b == 3:
                last = lax.broadcasted_iota(jnp.int32, shape, 1) == 7
                value = jnp.where(last, 0.0, value)
            part = slice(8 * b, 8 * b + 8)
            own[a, :, part] = value
            to_right[a, :, part] = value[R0 - H0 :]
            to_left[a, :, part] = value[:H0]


def edge_kernel(own, behind, ahead, to_right, to_left):
    lane = lanes((NZ, 128))

    def plane(a, p):
        if p < H0:
            return behind[a, p]
        if p < H0 + R0:
            return own[a, p - H0]
        return ahead[a, p - H0 - R0]

    for a in range(4):
        for c in range(GROUPS):
            right = left = jnp.zeros((NZ, 128), F32)
            for k in range(8):
                if 8 * c + k < N0:
                    value = roll(plane(a, 8 * c + k), 16 * k + 16, 1)
                    right = jnp.where(lane // 16 == k, value, right)
                    left = jnp.where(lane // 16 == (k + 1) % 8, value, left)
            to_right[a, c] = right
            to_left[a, c] = left


def down_kernel(
    own, behind, ahead, from_left, from_right,
    keep0, ops1, own1, kept_f1, to_right, to_left, own3,
    ext, fx, fy, fz, d, g, f, va, vb, t, t1, d1, f1, va1, vb1, x2, y2, z2, e2,
):
    lane = lanes((NZ, 128))
    for a in range(4):
        ext[a, 0:H0, :, 0:128] = behind[a]
        ext[a, H0 : H0 + R0, :, 0:128] = own[a]
        ext[a, H0 + R0 : N0, :, 0:128] = ahead[a]
        for c in range(GROUPS):
            left, right = from_left[a, c], from_right[a, c]
            for k in range(8):
                if 8 * c + k < N0:
                    both = jnp.where(lane // 16 == k, left, right)
                    ext[a, 8 * c + k, :, 128:256] = roll(both, -16 * k - 16, 1)

    def cut(value, *kinds):
        for kind in kinds:
            value = jnp.where(kind, value, 0.0)
        return value

    fx[0] = cut(ext[1, 0], ext[0, 0] == 0.0, ext[0, 1] == 0.0)

    def operator0(p):
        label, label_up, label_down = ext[0, p], ext[0, p + 1], ext[0, p - 1]
        cx, cx_back, cy, cz = ext[1, p], ext[1, p - 1], ext[2, p], ext[3, p]
        cy_back, cz_back = roll(cy, 1, 1), behind_z(cz)
        y_up, y_down = roll(label, -1, 1), roll(label, 1, 1)
        z_up, z_down = ahead_z(label), behind_z(label)
        free = label == 0.0
        extra, rhs, diag = LEAK, 0.0, LEAK
        edges = (
            (cx, label_up), (cx_back, label_down), (cy, y_up), (cy_back, y_down), (cz, z_up), (cz_back, z_down),
        )
        for edge, across in edges:
            extra = extra + jnp.where(across == 0.0, 0.0, edge)
            rhs = rhs + jnp.where(across == 1.0, edge, 0.0)
            diag = diag + edge
        rhs, diag = cut(rhs, free), cut(diag, free)
        scale = scale_of(diag)
        fx[p] = cut(cx, free, label_up == 0.0)
        fy[p] = cut(cy, free, y_up == 0.0)
        fz[p] = cut(cz, free, z_up == 0.0)
        d[p], g[p], f[p] = diag, scale, rhs
        va[p] = scale * rhs
        t[p] = cut(extra, free)

    planes(1, N0 - 1, operator0, 4)
    src, dst = va, vb
    for s in range(NU - 1):
        sweep(src, dst, f, g, fx, fy, fz, 2 + s, N0 - 2 - s)
        src, dst = dst, src

    lo = H0 - 4
    for i, ref in enumerate((src, f, g, fx, fy, fz)):
        keep0[i] = ref[lo : lo + 24]

    def to1(row):
        return jnp.where(row < 192, row // 2, row // 2 - 128) + 32

    pick, pick_odd = selection(256, 128, to1), selection(256, 128, to1, True)

    def coarsen1(q):
        p = 2 * q + 1
        t1[0, q] = fx[p + 1]
        t1[1, q] = fy[p] + fy[p + 1]
        t1[2, q] = fz[p] + fz[p + 1]
        t1[3, q] = t[p] + t[p + 1]

    planes(0, N1, coarsen1, 4)
    for a in range(4):
        for c in range(0, N1, 4):
            value = t1[a, c : c + 4].reshape(4 * NZ, 256)
            ops1[a, c : c + 4] = dot(value, pick_odd if a == 1 else pick).reshape(4, NZ, 128)

    residual(src, dst, f, d, fx, fy, fz, H0 - 8, H0 + R0 + 8)
    f1[0:2] = jnp.zeros((2, NZ, 128), F32)
    f1[N1 - 2 : N1] = jnp.zeros((2, NZ, 128), F32)
    for c in range(2, N1 - 2, 4):
        value = jnp.stack([dst[2 * q + 1] + dst[2 * q + 2] for q in range(c, c + 4)])
        f1[c : c + 4] = dot(value.reshape(4 * NZ, 256), pick).reshape(4, NZ, 128)

    x1, y1, z1, e1, g1 = (ops1.at[a] for a in range(5))
    g1[0] = jnp.where(e1[0] > 0.0, 1.0, 0.0)

    def operator1(q):
        diag = diagonal(e1[q], x1, y1, z1, q)
        d1[q] = diag
        scale = scale_of(diag)
        g1[q] = scale
        va1[q] = scale * f1[q]

    planes(1, N1, operator1)
    src, dst = va1, vb1
    for s in range(NU - 1):
        sweep(src, dst, f1, g1, x1, y1, z1, 3 + s, N1 - 3 - s)
        src, dst = dst, src
    own1[...] = src[H1 : H1 + 8]
    kept_f1[...] = f1[...]
    residual(src, dst, f1, d1, x1, y1, z1, H1, H1 + 8)

    half, half_odd = (selection(128, 128, lambda row: row // 2, odd) for odd in (False, True))
    q = [H1 + 2 * k for k in range(4)]
    f2 = dot(jnp.concatenate([dst[i] + dst[i + 1] for i in q]), half).reshape(4, NZ, 128)
    x2[...] = dot(jnp.concatenate([x1[i + 1] for i in [H1 - 2] + q]), half).reshape(5, NZ, 128)
    y2[...] = dot(jnp.concatenate([y1[i] + y1[i + 1] for i in q]), half_odd).reshape(4, NZ, 128)
    z2[...] = dot(jnp.concatenate([z1[i] + z1[i + 1] for i in q]), half).reshape(4, NZ, 128)
    e2[...] = dot(jnp.concatenate([e1[i] + e1[i + 1] for i in q]), half).reshape(4, NZ, 128)

    def around(x, x_back, y, z, extra):
        return extra + x + x_back + y + roll(y, 1, 1) + z + behind_z(z)

    for a in range(5):
        for h in range(2):
            pair = []
            for k in (2 * h, 2 * h + 1):
                if a == 4:
                    pair.append(around(x2[k + 1], x2[k], y2[k], z2[k], e2[k]))
                else:
                    pair.append((f2, x2[1:], y2, z2)[a][k])
            both = pair[0] + roll(pair[1], 64, 1)
            to_right[2 * a + h] = both
            to_left[2 * a + h] = both

    right = left = jnp.zeros((NZ, 128), F32)
    for k in range(8):
        here = lane // 8 == k
        right = jnp.where(here, roll(own1[k], 8 * k - 88, 1), right)
        left = jnp.where(here, roll(own1[k], 8 * k - 32, 1), left)
    to_right[10] = right
    to_left[10] = left

    x3 = dot(jnp.concatenate([x2[0], x2[2], x2[4]]), half).reshape(3, NZ, 128)
    y3 = dot(jnp.concatenate([y2[0] + y2[1], y2[2] + y2[3]]), half_odd).reshape(2, NZ, 128)
    z3 = dot(jnp.concatenate([z2[0] + z2[1], z2[2] + z2[3]]), half).reshape(2, NZ, 128)
    e3 = dot(jnp.concatenate([e2[0] + e2[1], e2[2] + e2[3]]), half).reshape(2, NZ, 128)
    total = jnp.zeros((NZ, 128), F32)
    for i in range(2):
        d3 = around(x3[i + 1], x3[i], y3[i], z3[i], e3[i])
        for a, value in enumerate((x3[i + 1], y3[i], z3[i], d3)):
            spot = 32 * a + 16 * i
            total = jnp.where(lane // 16 == spot // 16, roll(value, spot - 8, 1), total)
    own3[...] = total
    to_right[11] = total
    to_left[11] = total


def join_kernel(
    own2, own1, f1, left, right, left3, right3,
    joined2, first2, last2, joined1, to_right, to_left, near3,
):
    lane = lanes((NZ, 128))
    low, high = lane % 64 < 16, lane % 64 >= 48
    for a in range(10):
        value = jnp.where(high, roll(right[a], 32, 1), own2[a])
        value = jnp.where(low, roll(left[a], -32, 1), value)
        joined2[a] = value
        to_right[a] = value
        to_left[a] = value
        (last2 if a % 2 else first2)[a // 2] = value
    low, high = lane // 8 == 3, lane // 8 == 12
    for k in range(8):
        value = jnp.where(low, roll(left[10], 24 - 8 * k, 1), own1[k])
        value = jnp.where(high, roll(right[10], 96 - 8 * k, 1), value)
        joined1[k] = value
        if k >= 8 - H1:
            to_right[10 + k - 8 + H1] = value
        if k < H1:
            to_left[10 + k] = value
    to_right[10 + H1] = f1[H1 + 8 - 5]
    to_left[10 + H1] = f1[H1 + 4]
    for s, value in enumerate((left3[...], left[11], own2[11], right[11], right3[...])):
        near3[s] = value


def rows_of(value, odd):
    return roll(value, 64, 1) if odd else value


def middle_kernel(behind, own, ahead, out, f, fx, fy, fz, d, g, va, vb):
    for j in range(12):
        source = (behind, own, ahead)[j // 4]
        for a, ref in enumerate((f, fx, fy, fz, d)):
            ref[j] = rows_of(source[2 * a + j % 4 // 2], j % 2)
        g[j] = scale_of(d[j])
        va[j] = g[j] * f[j]
    src, dst = va, vb
    for s in range(NU - 1):
        sweep(src, dst, f, g, fx, fy, fz, 1 + s, 11 - s)
        src, dst = dst, src
    residual(src, dst, f, d, fx, fy, fz, 4, 8)
    total = None
    for i in range(2):
        matrix = selection(
            128, 128, lambda row: jnp.where((row >= 16) & (row < 48), (row - 16) // 2 + 16 * i, -99)
        )
        part = dot(dst[4 + 2 * i] + dst[5 + 2 * i], matrix)
        total = part if total is None else total + part
    value = total[:8]
    for b in range(1, 4):
        value = value + roll(total[8 * b : 8 * b + 8], 32 * b, 1)
    out[...] = value


def near_kernel(count, *refs):
    for c in range(count):
        for s in range(5):
            refs[5][c, s] = refs[s][...]


PAD3 = 8


def spread3_kernel(count, gathered, ops3):
    rows = 2 * count
    lo, hi = PAD3, PAD3 + rows
    lane = lanes((NZ, 128))
    for a in range(4):
        ops3[a, 0:lo] = jnp.zeros((PAD3, NZ, 128), F32)
        ops3[a, hi : hi + PAD3] = jnp.zeros((PAD3, NZ, 128), F32)

    def unpack(i, carry):
        for a in range(4):
            for r in range(2):
                total = jnp.zeros((NZ, 128), F32)
                for s in range(5):
                    value = roll(gathered[i, s], 16 * s - 32 * a - 16 * r, 1)
                    total = jnp.where(lane // 16 == s, value, total)
                ops3[a, lo + 2 * i + r] = scale_of(total) if a == 3 else total
        return carry

    lax.fori_loop(0, count, unpack, 0)


def solve_kernel(count, rhs3, ops3, out, f3, va3, vb3):
    rows = 2 * count
    lo, hi = PAD3, PAD3 + rows
    lane8 = lanes((8, 128))
    x3, y3, z3, g3 = (ops3.at[a] for a in range(4))
    for ref in (va3, vb3):
        ref[0:lo] = jnp.zeros((PAD3, NZ, 128), F32)
        ref[hi : hi + PAD3] = jnp.zeros((PAD3, NZ, 128), F32)

    def unpack(i, carry):
        for r in range(2):
            p = lo + 2 * i + r
            for b in range(4):
                total = jnp.zeros((8, 128), F32)
                for s in range(5):
                    value = roll(rhs3[i, s], 16 * s - 32 * b - 16 * r, 1)
                    total = jnp.where(lane8 // 16 == s, value, total)
                f3[p, 8 * b : 8 * b + 8] = total
                va3[p, 8 * b : 8 * b + 8] = total * g3[p, 8 * b : 8 * b + 8]
        return carry

    lax.fori_loop(0, count, unpack, 0)

    def two(i, carry):
        sweep(va3, vb3, f3, g3, x3, y3, z3, lo, hi, 32)
        sweep(vb3, va3, f3, g3, x3, y3, z3, lo, hi, 32)
        return carry

    lax.fori_loop(0, (COARSE_SWEEPS - 1) // 2, two, 0)
    sweep(va3, vb3, f3, g3, x3, y3, z3, lo, hi, 32)
    start = lo + 2 * lax.axis_index("gx") - 4
    out[...] = vb3[pl.ds(start, 10)]


def up_kernel(
    e3, behind3, behind2, behind, joined2, ahead, ahead2, ahead3, joined1, kept_f1, in_ops1, in_keep0,
    out,
    f2, x2, y2, z2, d2, g2, va2, vb2, f1, va1, vb1, va0, vb0, ops1, keep0, sems,
):
    copies = fetch(((in_ops1, ops1), (in_keep0, keep0)), sems)
    sources = [(behind3, None)]
    sources += [(ref, h) for ref in (behind2, behind, joined2, ahead, ahead2) for h in range(2)]
    sources += [(ahead3, None)]
    for n, (source, h) in enumerate(sources):
        for a, ref in enumerate((f2, x2, y2, z2, d2)):
            value = source[a if h is None else 2 * a + h]
            ref[2 * n] = value
            ref[2 * n + 1] = roll(value, 64, 1)

    def operator2(j):
        g2[j] = scale_of(d2[j])
        va2[j] = g2[j] * f2[j]

    planes(0, 24, operator2, 24)
    src, dst = va2, vb2
    for s in range(NU - 1):
        sweep(src, dst, f2, g2, x2, y2, z2, 1 + s, 23 - s, 32)
        src, dst = dst, src
    col = lax.broadcasted_iota(jnp.int32, (128, 128), 1)
    row = lax.broadcasted_iota(jnp.int32, (128, 128), 0)
    spread = ((row == (col + 128 - 16) // 2 - 64 + 32) & (col < 64)).astype(F32)
    coarse = dot(e3[...].reshape(10 * NZ, 128), spread).reshape(10, NZ, 128)
    for r in range(-7, 11):
        j = r + 10
        src[j] = src[j] + jnp.where(g2[j] > 0.0, coarse[r // 2 + 4], 0.0)
    for s in range(NU):
        sweep(src, dst, f2, g2, x2, y2, z2, 4 + s, 20 - s, 32)
        src, dst = dst, src

    copies[0].wait()
    x1, y1, z1, g1 = ops1.at[0], ops1.at[1], ops1.at[2], ops1.at[4]
    f1[...] = kept_f1[...]
    f1[1] = behind[10 + H1]
    f1[N1 - 2] = ahead[10 + H1]
    spread = (row == (col - 32 + 128) // 2 - 64 + 16).astype(F32)
    coarse = dot(src[7:17].reshape(10 * NZ, 128), spread).reshape(10, NZ, 128)
    for q in range(N1):
        if q < H1:
            value = behind[10 + q]
        elif q < H1 + 8:
            value = joined1[q - H1]
        else:
            value = ahead[10 + q - H1 - 8]
        va1[q] = value + jnp.where(g1[q] > 0.0, coarse[q // 2], 0.0)
    src, dst = va1, vb1
    for s in range(NU):
        sweep(src, dst, f1, g1, x1, y1, z1, 1 + s, N1 - 1 - s, 32)
        src, dst = dst, src

    copies[1].wait()
    v0, f0, g0, x0, y0, z0 = (keep0.at[a] for a in range(6))
    col = lax.broadcasted_iota(jnp.int32, (128, 256), 1)
    row = lax.broadcasted_iota(jnp.int32, (128, 256), 0)
    spread = (row == jnp.where(col < 192, col // 2, col // 2 - 128) + 32).astype(F32)
    for c in range(0, 12, 4):
        coarse = dot(src[4 + c : 8 + c].reshape(4 * NZ, 128), spread).reshape(4, NZ, 256)
        for k in range(8):
            i = 2 * c + k
            va0[i] = v0[i] + jnp.where(g0[i] > 0.0, coarse[k // 2], 0.0)
    src, dst = va0, vb0
    for s in range(NU):
        sweep(src, dst, f0, g0, x0, y0, z0, 1 + s, 23 - s)
        src, dst = dst, src
    for b in range(4):
        value = jnp.swapaxes(src[4:20, 8 * b : 8 * b + 8, 0:128], 0, 1)
        for s in range(8):
            out[4 * s + b] = value[s]


def shift(value, axis, distance):
    count = lax.axis_size(axis)
    route = [(i, i + distance) for i in range(count) if 0 <= i + distance < count]
    return lax.ppermute(value, axis, route)


def body(labels, conduct_x, conduct_y, conduct_z):
    count = lax.axis_size("gx")
    side = (NZ, 128)
    wide = (N0, NZ, 256)
    own, to_right, to_left = call(
        stage_kernel,
        (labels, conduct_x, conduct_y, conduct_z),
        [(4, R0, *side), (4, H0, *side), (4, H0, *side)],
        [pltpu.VMEM(labels.shape, labels.dtype)]
        + [pltpu.VMEM(labels.shape, conduct_x.dtype)] * 3
        + [pltpu.SemaphoreType.DMA((4,))],
        apart=(0, 1, 2, 3),
    )
    behind = shift(to_right, "gx", 1)
    ahead = shift(to_left, "gx", -1)
    to_right, to_left = call(edge_kernel, (own, behind, ahead), [(4, GROUPS, *side)] * 2)
    from_left = shift(to_right, "gy", 1)
    from_right = shift(to_left, "gy", -1)
    keep0, ops1, own1, kept_f1, to_right, to_left, own3 = call(
        down_kernel,
        (own, behind, ahead, from_left, from_right),
        [(6, 24, NZ, 256), (5, N1, *side), (8, *side), (N1, *side), (12, *side), (12, *side), side],
        [(4, N0, NZ, 256)]
        + [wide] * 9
        + [(4, N1, NZ, 256)]
        + [(N1, *side)] * 4
        + [(5, *side)]
        + [(4, *side)] * 3,
        limit=44,
    )
    left, right = shift(to_right, "gy", 1), shift(to_left, "gy", -1)
    left3, right3 = shift(own3, "gy", 2), shift(own3, "gy", -2)
    joined2, first2, last2, joined1, to_right, to_left, near3 = call(
        join_kernel,
        (to_right, own1, kept_f1, left, right, left3, right3),
        [(10, *side), (5, *side), (5, *side), (8, *side)]
        + [(11 + H1, *side)] * 2
        + [(5, *side)],
    )
    all3 = lax.all_gather(near3, "gx")
    behind, ahead = shift(to_right, "gx", 1), shift(to_left, "gx", -1)
    (rhs3,) = call(middle_kernel, (behind, joined2, ahead), [(8, 128)], [(12, *side)] * 8)
    rhs3, joined2, first2, last2 = lax.optimization_barrier((rhs3, joined2, first2, last2))
    around = [shift(rhs3, "gy", distance) for distance in (2, 1, -1, -2)]
    behind2, ahead2 = shift(joined2, "gx", 2), shift(joined2, "gx", -2)
    behind3, ahead3 = shift(last2, "gx", 3), shift(first2, "gx", -3)
    (rhs3,) = call(
        functools.partial(near_kernel, count),
        (around[0], around[1], rhs3, around[2], around[3]),
        [(count, 5, 8, 128)],
    )
    rhs3 = lax.all_to_all(rhs3, "gx", 0, 0)
    rows3 = 2 * count + 2 * PAD3
    (ops3,) = call(functools.partial(spread3_kernel, count), (all3,), [(4, rows3, *side)])
    (e3,) = call(
        functools.partial(solve_kernel, count), (rhs3, ops3), [(10, *side)], [(rows3, *side)] * 3
    )
    (out,) = call(
        up_kernel,
        (e3, behind3, behind2, behind, joined2, ahead, ahead2, ahead3, joined1, kept_f1, ops1, keep0),
        [(NZ, R0, 128)],
        [(24, *side)] * 8
        + [(N1, *side)] * 3
        + [(24, NZ, 256)] * 2
        + [(5, N1, *side), (6, 24, NZ, 256)]
        + [pltpu.SemaphoreType.DMA((2,))],
        limit=30,
        apart=(10, 11),
    )
    return out


def solution(mesh):
    in_specs = (P(None, "gx", "gy"),) * 4
    out_specs = P(None, "gx", "gy")
    return jax.shard_map(body, mesh=mesh, in_specs=in_specs, out_specs=out_specs, check_vma=False)
```

time: 1080 us -> 173 us (0.16)
  the two profiles are of different devices: /device:TPU:152 before, /device:TPU:6 now
where the time goes in v1:
time: 173 us; the launch traced here: 172 us
  starting transfers between devices  67.7 us (39%)
  waiting for transfers between devices  42.6 us (25%)
  Pallas kernels  38.4 us (22%)
  between operations  13.7 us (8%)
  local copies, waits for them, and re-layouts  9.98 us (6%)
    ppermute x18, starting transfers between devices, shift(): return lax.ppermute(value, axis, route)  59.1 us
    ppermute x18, waiting for transfers between devices, shift(): return lax.ppermute(value, axis, route)  38.9 us
    pallas_call x9, Pallas kernels, call(): pl.pallas_call(kernel, out_shape=[jax.ShapeDtypeStruct(s, F32) for s in o...  38.4 us
    unnamed x28, local copies, waits for them, and re-layouts  9.98 us
    all_to_all x1, starting transfers between devices, body(): rhs3 = lax.all_to_all(rhs3, 'gx', 0, 0)  8.56 us
    all_gather x1, waiting for transfers between devices, body(): all3 = lax.all_gather(near3, 'gx')  3.7 us
  transfers between devices with their start and end apart: 20, of which 10 were waited for; matrix products, arithmetic and copies ran while one was open for 0% of the time, Pallas kernels for 9%

profile of v1, /device:TPU:6, one launch (start us, length us, event | category | flops | bytes accessed | tf_op | source)
XLA Modules:
  0.0 172.4 jit_solution(2172113326347393743)
XLA Ops:
  11.2 3.5 %collective-permute-start = (f32[4,13,32,128]{3,2,1,0:T(8,128)S(1)}, f32[4,13,32,128]{3,2,1,0:T(8,128)S(1)}, u32[]{:S(2)}, u32[]{:S(2)}) collective-permute-start(f32[4,13,32,128]{3,2,1,0:T(8,128)S(1)} %get-tuple-element.29), channel_id=1, source_target_pairs={{0,16},{16,32},{32,48},{48,64},{64,80},{80,96},{96,112},{112,128},... | collective-permute-start | bytes 2555912 | tf_op jit(solution)/shard_map/ppermute | solution.py:533
  14.7 4.5 %collective-permute-start.1 = (f32[4,13,32,128]{3,2,1,0:T(8,128)S(1)}, f32[4,13,32,128]{3,2,1,0:T(8,128)S(1)}, u32[]{:S(2)}, u32[]{:S(2)}) collective-permute-start(f32[4,13,32,128]{3,2,1,0:T(8,128)S(1)} %get-tuple-element.30), channel_id=1, source_target_pairs={{16,0},{32,16},{48,32},{64,48},{80,64},{96,80},{112,96},{128,112},... | collective-permute-start | bytes 2555912 | tf_op jit(solution)/shard_map/ppermute | solution.py:533
  19.1 16.7 %collective-permute-done.behind = f32[4,13,32,128]{3,2,1,0:T(8,128)S(1)} collective-permute-done((f32[4,13,32,128]{3,2,1,0:T(8,128)S(1)}, f32[4,13,32,128]{3,2,1,0:T(8,128)S(1)}, u32[]{:S(2)}, u32[]{:S(2)}) %collective-permute-start) | collective-permute-done | bytes 852000 | tf_op jit(solution)/shard_map/ppermute | solution.py:533
  37.7 1.3 collective-permute-start.2
  39.1 1.3 collective-permute-start.3
  40.4 4.4 %collective-permute-done.3.from_right = f32[4,6,32,128]{3,2,1,0:T(8,128)S(1)} collective-permute-done((f32[4,6,32,128]{3,2,1,0:T(8,128)S(1)}, f32[4,6,32,128]{3,2,1,0:T(8,128)S(1)}, u32[]{:S(2)}, u32[]{:S(2)}) %collective-permute-start.3) | collective-permute-done | bytes 393248 | tf_op jit(solution)/shard_map/ppermute | solution.py:533
  44.8 12.9 %shard_map.48 = (f32[6,24,32,256]{3,2,1,0:T(8,128)}, f32[5,20,32,128]{3,2,1,0:T(8,128)S(1)}, f32[8,32,128]{2,1,0:T(8,128)S(1)}, f32[20,32,128]{2,1,0:T(8,128)S(1...) custom-call(f32[4,16,32,128]{3,2,1,0:T(8,128)S(1)} %get-tuple-element.28.own, ...), custom_call_target="tpu_custom_call" | custom-call | tf_op jit(solution)/shard_map/pallas_call | solution.py:31
  58.9 7.9 %collective-permute-start.4 = (f32[12,32,128]{2,1,0:T(8,128)S(1)}, f32[12,32,128]{2,1,0:T(8,128)S(1)}, u32[]{:S(2)}, u32[]{:S(2)}) collective-permute-start(f32[12,32,128]{2,1,0:T(8,128)S(1)} %get-tuple-element.33.own2), channel_id=1, source_target_pairs={{0,1},{1,2},{2,3},{3,4},{4,5},{5,6},{6,7},{7,8},{8,9},{9,10},{10,1... | collective-permute-start | bytes 589832 | tf_op jit(solution)/shard_map/ppermute | solution.py:533
  66.8 1.3 collective-permute-start.5
  68.1 4.4 %collective-permute-start.6 = (f32[32,128]{1,0:T(8,128)S(1)}, f32[32,128]{1,0:T(8,128)S(1)}, u32[]{:S(2)}, u32[]{:S(2)}) collective-permute-start(f32[32,128]{1,0:T(8,128)S(1)} %get-tuple-element.37), channel_id=1, source_target_pairs={{0,2},{1,3},{2,4},{3,5},{4,6},{5,7},{6,8},{7,9},{8,10},{9,11},{10,... | collective-permute-start | bytes 49160 | tf_op jit(solution)/shard_map/ppermute | solution.py:533
  72.5 1.3 collective-permute-start.7
  74.0 4.2 %collective-permute-done.7.right3 = f32[32,128]{1,0:T(8,128)S(1)} collective-permute-done((f32[32,128]{1,0:T(8,128)S(1)}, f32[32,128]{1,0:T(8,128)S(1)}, u32[]{:S(2)}, u32[]{:S(2)}) %collective-permute-start.7) | collective-permute-done | bytes 16416 | tf_op jit(solution)/shard_map/ppermute | solution.py:533
  79.8 3.4 %collective-permute-start.8 = (f32[17,32,128]{2,1,0:T(8,128)S(1)}, f32[17,32,128]{2,1,0:T(8,128)S(1)}, u32[]{:S(2)}, u32[]{:S(2)}) collective-permute-start(f32[17,32,128]{2,1,0:T(8,128)S(1)} %get-tuple-element.38), channel_id=1, source_target_pairs={{0,16},{16,32},{32,48},{48,64},{64,80},{80,96},{96,112},{112,128},... | collective-permute-start | bytes 835592 | tf_op jit(solution)/shard_map/ppermute | solution.py:533
  83.2 5.0 %collective-permute-start.9 = (f32[17,32,128]{2,1,0:T(8,128)S(1)}, f32[17,32,128]{2,1,0:T(8,128)S(1)}, u32[]{:S(2)}, u32[]{:S(2)}) collective-permute-start(f32[17,32,128]{2,1,0:T(8,128)S(1)} %get-tuple-element.40), channel_id=1, source_target_pairs={{16,0},{32,16},{48,32},{64,48},{80,64},{96,80},{112,96},{128,112},... | collective-permute-start | bytes 835592 | tf_op jit(solution)/shard_map/ppermute | solution.py:533
  88.2 4.1 %collective-permute-done.8.behind = f32[17,32,128]{2,1,0:T(8,128)S(1)} collective-permute-done((f32[17,32,128]{2,1,0:T(8,128)S(1)}, f32[17,32,128]{2,1,0:T(8,128)S(1)}, u32[]{:S(2)}, u32[]{:S(2)}) %collective-permute-start.8) | collective-permute-done | bytes 278560 | tf_op jit(solution)/shard_map/ppermute | solution.py:533
  93.5 1.7 shard_map.50.refs_2_
  96.0 6.2 %collective-permute-start.10 = (f32[8,128]{1,0:T(8,128)S(1)}, f32[8,128]{1,0:T(8,128)S(1)}, u32[]{:S(2)}, u32[]{:S(2)}) collective-permute-start(f32[8,128]{1,0:T(8,128)S(1)} %shard_map.50.refs_2_), channel_id=1, source_target_pairs={{0,2},{1,3},{2,4},{3,5},{4,6},{5,7},{6,8},{7,9},{8,10},{9,11},{10,... | collective-permute-start | bytes 12296 | tf_op jit(solution)/shard_map/ppermute | solution.py:533
  103.5 1.3 collective-permute-start.12
  104.8 1.3 collective-permute-start.13
  106.1 2.4 %collective-permute-done.12.refs_3_ = f32[8,128]{1,0:T(8,128)S(1)} collective-permute-done((f32[8,128]{1,0:T(8,128)S(1)}, f32[8,128]{1,0:T(8,128)S(1)}, u32[]{:S(2)}, u32[]{:S(2)}) %collective-permute-start.12) | collective-permute-done | bytes 4128 | tf_op jit(solution)/shard_map/ppermute | solution.py:533
  108.5 4.5 %collective-permute-done.13.refs_4_ = f32[8,128]{1,0:T(8,128)S(1)} collective-permute-done((f32[8,128]{1,0:T(8,128)S(1)}, f32[8,128]{1,0:T(8,128)S(1)}, u32[]{:S(2)}, u32[]{:S(2)}) %collective-permute-start.13) | collective-permute-done | bytes 4128 | tf_op jit(solution)/shard_map/ppermute | solution.py:533
  113.8 8.6 %all-to-all-start = ((f32[16,5,8,128]{3,2,1,0:T(8,128)}), f32[16,5,8,128]{3,2,1,0:T(8,128)}, u32[]{:S(2)}, u32[]{:S(2)}) async-start(f32[16,5,8,128]{3,2,1,0:T(8,128)} %shard_map.51), calls=%async_computation | async-start | bytes 655360 | tf_op jit(solution)/shard_map/all_to_all | solution.py:587
  122.3 4.9 %collective-permute-start.15 = (f32[10,32,128]{2,1,0:T(8,128)}, f32[10,32,128]{2,1,0:T(8,128)}, u32[]{:S(2)}, u32[]{:S(2)}) collective-permute-start(f32[10,32,128]{2,1,0:T(8,128)} %get-tuple-element.46.own.joined2), channel_id=1, source_target_pairs={{0,32},{16,48},{32,64},{48,80},{64,96},{80,112},{96,128},{112,144}... | collective-permute-start | bytes 491528 | tf_op jit(solution)/shard_map/ppermute | solution.py:533
  127.2 3.4 %collective-permute-start.16 = (f32[10,32,128]{2,1,0:T(8,128)}, f32[10,32,128]{2,1,0:T(8,128)}, u32[]{:S(2)}, u32[]{:S(2)}) collective-permute-start(f32[10,32,128]{2,1,0:T(8,128)} %get-tuple-element.46.own.joined2), channel_id=1, source_target_pairs={{32,0},{48,16},{64,32},{80,48},{96,64},{112,80},{128,96},{144,112}... | collective-permute-start | bytes 491528 | tf_op jit(solution)/shard_map/ppermute | solution.py:533
  130.6 4.3 %collective-permute-start.14 = (f32[5,32,128]{2,1,0:T(8,128)}, f32[5,32,128]{2,1,0:T(8,128)S(1)}, u32[]{:S(2)}, u32[]{:S(2)}) collective-permute-start(f32[5,32,128]{2,1,0:T(8,128)} %get-tuple-element.45), channel_id=1, source_target_pairs={{0,48},{16,64},{32,80},{48,96},{64,112},{80,128},{96,144},{112,160... | collective-permute-start | bytes 245768 | tf_op jit(solution)/shard_map/ppermute | solution.py:533
  134.9 2.6 %collective-permute-start.17 = (f32[5,32,128]{2,1,0:T(8,128)}, f32[5,32,128]{2,1,0:T(8,128)}, u32[]{:S(2)}, u32[]{:S(2)}) collective-permute-start(f32[5,32,128]{2,1,0:T(8,128)} %get-tuple-element.47), channel_id=1, source_target_pairs={{48,0},{64,16},{80,32},{96,48},{112,64},{128,80},{144,96},{160,112... | collective-permute-start | bytes 245768 | tf_op jit(solution)/shard_map/ppermute | solution.py:533
  137.5 3.7 %all-gather.3.cloned.1.call-done = f32[80,32,128]{2,1,0:T(8,128)} async-done(((f32[5,32,128]{2,1,0:T(8,128)}), f32[80,32,128]{2,1,0:T(8,128)}) %all-gather.3.cloned.1.call-update) | async-done | bytes 1310736 | tf_op jit(solution)/shard_map/all_gather | solution.py:575
  141.2 1.3 copy-done.3
  142.5 3.6 %shard_map.52.ops3 = f32[4,48,32,128]{3,2,1,0:T(8,128)S(1)} custom-call(f32[16,5,32,128]{3,2,1,0:T(8,128)S(1)} %bitcast.1), custom_call_target="tpu_custom_call" | custom-call | tf_op jit(solution)/shard_map/pallas_call | solution.py:31
  146.2 10.0 %shard_map.53.e3 = f32[10,32,128]{2,1,0:T(8,128)S(1)} custom-call(f32[16,5,8,128]{3,2,1,0:T(8,128)} %all-to-all-done.rhs3, f32[4,48,32,128]{3,2,1,0:T(8,128)S(1)} %shard_map.52.ops3), custom_call_target="tpu_custom_call" | custom-call | tf_op jit(solution)/shard_map/pallas_call | solution.py:31
  156.3 2.3 %copy-done = f32[6,24,32,256]{3,2,1,0:T(8,128)S(1)} copy-done((f32[6,24,32,256]{3,2,1,0:T(8,128)S(1)}, f32[6,24,32,256]{3,2,1,0:T(8,128)}, u32[]{:S(2)}) %copy-start) | copy-done | bytes 4718616
  158.7 6.9 %shard_map.54 = f32[32,16,128]{2,1,0:T(8,128)} custom-call(f32[10,32,128]{2,1,0:T(8,128)S(1)} %shard_map.53.e3, f32[5,32,128]{2,1,0:T(8,128)S(1)} %collective-permute-done.14.behind3, f32[10,32,128]{2,1,0:T(8,128)} %collective-permute-done.15.behind2, f32[17,32,128]{2,1,0:T(8,128)S(1)} %copy-done.5, f32[10,32,128]{2,1,0:T(8,128)} %get-tuple-element.46.own.joined2, ...), custom_call_target="tpu_custom_call" | custom-call | tf_op jit(solution)/shard_map/pallas_call | solution.py:31
  (46 shorter events, 13.5 us)
Async XLA Ops:
  6.5 134.7 %all-gather.3.cloned.1.call-start = ((), (), s32[]{:S(2)}) async-start(), calls=%async_computation.1 | async-start | bytes 1392640 | tf_op jit(solution)/shard_map/all_gather | solution.py:575
  6.5 0.9 copy-start.8
  7.5 0.9 copy-start.11
  8.4 0.9 copy-start.12
  9.3 0.9 copy-start.13
  11.2 24.7 %collective-permute-start = (f32[4,13,32,128]{3,2,1,0:T(8,128)S(1)}, f32[4,13,32,128]{3,2,1,0:T(8,128)S(1)}, u32[]{:S(2)}, u32[]{:S(2)}) collective-permute-start(f32[4,13,32,128]{3,2,1,0:T(8,128)S(1)} %get-tuple-element.29), channel_id=1, source_target_pairs={{0,16},{16,32},{32,48},{48,64},{64,80},{80,96},{96,112},{112,128},... | collective-permute-start | bytes 2555912 | tf_op jit(solution)/shard_map/ppermute | solution.py:533
  14.7 22.4 %collective-permute-start.1 = (f32[4,13,32,128]{3,2,1,0:T(8,128)S(1)}, f32[4,13,32,128]{3,2,1,0:T(8,128)S(1)}, u32[]{:S(2)}, u32[]{:S(2)}) collective-permute-start(f32[4,13,32,128]{3,2,1,0:T(8,128)S(1)} %get-tuple-element.30), channel_id=1, source_target_pairs={{16,0},{32,16},{48,32},{64,48},{80,64},{96,80},{112,96},{128,112},... | collective-permute-start | bytes 2555912 | tf_op jit(solution)/shard_map/ppermute | solution.py:533
  37.7 2.6 %collective-permute-start.2 = (f32[4,6,32,128]{3,2,1,0:T(8,128)S(1)}, f32[4,6,32,128]{3,2,1,0:T(8,128)S(1)}, u32[]{:S(2)}, u32[]{:S(2)}) collective-permute-start(f32[4,6,32,128]{3,2,1,0:T(8,128)S(1)} %get-tuple-element.31), channel_id=1, source_target_pairs={{0,1},{1,2},{2,3},{3,4},{4,5},{5,6},{6,7},{7,8},{8,9},{9,10},{10,1... | collective-permute-start | bytes 1179656 | tf_op jit(solution)/shard_map/ppermute | solution.py:533
  39.1 5.7 %collective-permute-start.3 = (f32[4,6,32,128]{3,2,1,0:T(8,128)S(1)}, f32[4,6,32,128]{3,2,1,0:T(8,128)S(1)}, u32[]{:S(2)}, u32[]{:S(2)}) collective-permute-start(f32[4,6,32,128]{3,2,1,0:T(8,128)S(1)} %get-tuple-element.32), channel_id=1, source_target_pairs={{1,0},{2,1},{3,2},{4,3},{5,4},{6,5},{7,6},{8,7},{9,8},{10,9},{11,1... | collective-permute-start | bytes 1179656 | tf_op jit(solution)/shard_map/ppermute | solution.py:533
  57.7 1.2 copy-start.1
  58.9 19.3 %collective-permute-start.4 = (f32[12,32,128]{2,1,0:T(8,128)S(1)}, f32[12,32,128]{2,1,0:T(8,128)S(1)}, u32[]{:S(2)}, u32[]{:S(2)}) collective-permute-start(f32[12,32,128]{2,1,0:T(8,128)S(1)} %get-tuple-element.33.own2), channel_id=1, source_target_pairs={{0,1},{1,2},{2,3},{3,4},{4,5},{5,6},{6,7},{7,8},{8,9},{9,10},{10,1... | collective-permute-start | bytes 589832 | tf_op jit(solution)/shard_map/ppermute | solution.py:533
  66.8 11.4 %collective-permute-start.5 = (f32[12,32,128]{2,1,0:T(8,128)S(1)}, f32[12,32,128]{2,1,0:T(8,128)S(1)}, u32[]{:S(2)}, u32[]{:S(2)}) collective-permute-start(f32[12,32,128]{2,1,0:T(8,128)S(1)} %get-tuple-element.36), channel_id=1, source_target_pairs={{1,0},{2,1},{3,2},{4,3},{5,4},{6,5},{7,6},{8,7},{9,8},{10,9},{11,1... | collective-permute-start | bytes 589832 | tf_op jit(solution)/shard_map/ppermute | solution.py:533
  68.1 5.9 %collective-permute-start.6 = (f32[32,128]{1,0:T(8,128)S(1)}, f32[32,128]{1,0:T(8,128)S(1)}, u32[]{:S(2)}, u32[]{:S(2)}) collective-permute-start(f32[32,128]{1,0:T(8,128)S(1)} %get-tuple-element.37), channel_id=1, source_target_pairs={{0,2},{1,3},{2,4},{3,5},{4,6},{5,7},{6,8},{7,9},{8,10},{9,11},{10,... | collective-permute-start | bytes 49160 | tf_op jit(solution)/shard_map/ppermute | solution.py:533
  72.5 5.6 %collective-permute-start.7 = (f32[32,128]{1,0:T(8,128)S(1)}, f32[32,128]{1,0:T(8,128)S(1)}, u32[]{:S(2)}, u32[]{:S(2)}) collective-permute-start(f32[32,128]{1,0:T(8,128)S(1)} %get-tuple-element.37), channel_id=1, source_target_pairs={{2,0},{3,1},{4,2},{5,3},{6,4},{7,5},{8,6},{9,7},{10,8},{11,9},{12,... | collective-permute-start | bytes 49160 | tf_op jit(solution)/shard_map/ppermute | solution.py:533
  79.8 12.6 %collective-permute-start.8 = (f32[17,32,128]{2,1,0:T(8,128)S(1)}, f32[17,32,128]{2,1,0:T(8,128)S(1)}, u32[]{:S(2)}, u32[]{:S(2)}) collective-permute-start(f32[17,32,128]{2,1,0:T(8,128)S(1)} %get-tuple-element.38), channel_id=1, source_target_pairs={{0,16},{16,32},{32,48},{48,64},{64,80},{80,96},{96,112},{112,128},... | collective-permute-start | bytes 835592 | tf_op jit(solution)/shard_map/ppermute | solution.py:533
  83.2 10.3 %collective-permute-start.9 = (f32[17,32,128]{2,1,0:T(8,128)S(1)}, f32[17,32,128]{2,1,0:T(8,128)S(1)}, u32[]{:S(2)}, u32[]{:S(2)}) collective-permute-start(f32[17,32,128]{2,1,0:T(8,128)S(1)} %get-tuple-element.40), channel_id=1, source_target_pairs={{16,0},{32,16},{48,32},{64,48},{80,64},{96,80},{112,96},{128,112},... | collective-permute-start | bytes 835592 | tf_op jit(solution)/shard_map/ppermute | solution.py:533
  93.5 1.7 copy-start.6
  96.0 10.1 %collective-permute-start.10 = (f32[8,128]{1,0:T(8,128)S(1)}, f32[8,128]{1,0:T(8,128)S(1)}, u32[]{:S(2)}, u32[]{:S(2)}) collective-permute-start(f32[8,128]{1,0:T(8,128)S(1)} %shard_map.50.refs_2_), channel_id=1, source_target_pairs={{0,2},{1,3},{2,4},{3,5},{4,6},{5,7},{6,8},{7,9},{8,10},{9,11},{10,... | collective-permute-start | bytes 12296 | tf_op jit(solution)/shard_map/ppermute | solution.py:533
  102.2 3.9 %collective-permute-start.11 = (f32[8,128]{1,0:T(8,128)S(1)}, f32[8,128]{1,0:T(8,128)S(1)}, u32[]{:S(2)}, u32[]{:S(2)}) collective-permute-start(f32[8,128]{1,0:T(8,128)S(1)} %shard_map.50.refs_2_), channel_id=1, source_target_pairs={{0,1},{1,2},{2,3},{3,4},{4,5},{5,6},{6,7},{7,8},{8,9},{9,10},{10,1... | collective-permute-start | bytes 12296 | tf_op jit(solution)/shard_map/ppermute | solution.py:533
  103.5 5.0 %collective-permute-start.12 = (f32[8,128]{1,0:T(8,128)S(1)}, f32[8,128]{1,0:T(8,128)S(1)}, u32[]{:S(2)}, u32[]{:S(2)}) collective-permute-start(f32[8,128]{1,0:T(8,128)S(1)} %shard_map.50.refs_2_), channel_id=1, source_target_pairs={{1,0},{2,1},{3,2},{4,3},{5,4},{6,5},{7,6},{8,7},{9,8},{10,9},{11,1... | collective-permute-start | bytes 12296 | tf_op jit(solution)/shard_map/ppermute | solution.py:533
  104.8 8.2 %collective-permute-start.13 = (f32[8,128]{1,0:T(8,128)S(1)}, f32[8,128]{1,0:T(8,128)S(1)}, u32[]{:S(2)}, u32[]{:S(2)}) collective-permute-start(f32[8,128]{1,0:T(8,128)S(1)} %shard_map.50.refs_2_), channel_id=1, source_target_pairs={{2,0},{3,1},{4,2},{5,3},{6,4},{7,5},{8,6},{9,7},{10,8},{11,9},{12,... | collective-permute-start | bytes 12296 | tf_op jit(solution)/shard_map/ppermute | solution.py:533
  113.8 32.4 %all-to-all-start = ((f32[16,5,8,128]{3,2,1,0:T(8,128)}), f32[16,5,8,128]{3,2,1,0:T(8,128)}, u32[]{:S(2)}, u32[]{:S(2)}) async-start(f32[16,5,8,128]{3,2,1,0:T(8,128)} %shard_map.51), calls=%async_computation | async-start | bytes 655360 | tf_op jit(solution)/shard_map/all_to_all | solution.py:587
  122.3 33.9 %collective-permute-start.15 = (f32[10,32,128]{2,1,0:T(8,128)}, f32[10,32,128]{2,1,0:T(8,128)}, u32[]{:S(2)}, u32[]{:S(2)}) collective-permute-start(f32[10,32,128]{2,1,0:T(8,128)} %get-tuple-element.46.own.joined2), channel_id=1, source_target_pairs={{0,32},{16,48},{32,64},{48,80},{64,96},{80,112},{96,128},{112,144}... | collective-permute-start | bytes 491528 | tf_op jit(solution)/shard_map/ppermute | solution.py:533
  127.2 29.1 %collective-permute-start.16 = (f32[10,32,128]{2,1,0:T(8,128)}, f32[10,32,128]{2,1,0:T(8,128)}, u32[]{:S(2)}, u32[]{:S(2)}) collective-permute-start(f32[10,32,128]{2,1,0:T(8,128)} %get-tuple-element.46.own.joined2), channel_id=1, source_target_pairs={{32,0},{48,16},{64,32},{80,48},{96,64},{112,80},{128,96},{144,112}... | collective-permute-start | bytes 491528 | tf_op jit(solution)/shard_map/ppermute | solution.py:533
  130.6 25.6 %collective-permute-start.14 = (f32[5,32,128]{2,1,0:T(8,128)}, f32[5,32,128]{2,1,0:T(8,128)S(1)}, u32[]{:S(2)}, u32[]{:S(2)}) collective-permute-start(f32[5,32,128]{2,1,0:T(8,128)} %get-tuple-element.45), channel_id=1, source_target_pairs={{0,48},{16,64},{32,80},{48,96},{64,112},{80,128},{96,144},{112,160... | collective-permute-start | bytes 245768 | tf_op jit(solution)/shard_map/ppermute | solution.py:533
  134.9 21.3 %collective-permute-start.17 = (f32[5,32,128]{2,1,0:T(8,128)}, f32[5,32,128]{2,1,0:T(8,128)}, u32[]{:S(2)}, u32[]{:S(2)}) collective-permute-start(f32[5,32,128]{2,1,0:T(8,128)} %get-tuple-element.47), channel_id=1, source_target_pairs={{48,0},{64,16},{80,32},{96,48},{112,64},{128,80},{144,96},{160,112... | collective-permute-start | bytes 245768 | tf_op jit(solution)/shard_map/ppermute | solution.py:533
  141.2 1.3 copy-start.3
  146.2 10.1 %copy-start.2 = (f32[5,20,32,128]{3,2,1,0:T(8,128)S(1)}, f32[5,20,32,128]{3,2,1,0:T(8,128)}, u32[]{:S(2)}) copy-start(f32[5,20,32,128]{3,2,1,0:T(8,128)} %copy-done.1) | copy-start | bytes 4915204
  146.2 10.1 %copy-start.5 = (f32[17,32,128]{2,1,0:T(8,128)S(1)}, f32[17,32,128]{2,1,0:T(8,128)}, u32[]{:S(2)}) copy-start(f32[17,32,128]{2,1,0:T(8,128)} %copy-done.4) | copy-start | bytes 835588
  146.2 10.1 %copy-start.7 = (f32[17,32,128]{2,1,0:T(8,128)S(1)}, f32[17,32,128]{2,1,0:T(8,128)}, u32[]{:S(2)}) copy-start(f32[17,32,128]{2,1,0:T(8,128)} %copy-done.6) | copy-start | bytes 835588
  146.2 10.1 %copy-start.10 = (f32[8,32,128]{2,1,0:T(8,128)S(1)}, f32[8,32,128]{2,1,0:T(8,128)}, u32[]{:S(2)}) copy-start(f32[8,32,128]{2,1,0:T(8,128)} %copy-done.9) | copy-start | bytes 393220
  156.3 2.3 %copy-start = (f32[6,24,32,256]{3,2,1,0:T(8,128)S(1)}, f32[6,24,32,256]{3,2,1,0:T(8,128)}, u32[]{:S(2)}) copy-start(f32[6,24,32,256]{3,2,1,0:T(8,128)} %get-tuple-element.50.in_keep0) | copy-start | bytes 14155780
  (2 other events, 1.4 us)
Sparse Core Ops, SparseCore 0:
  79.9 61.2 all-gather.2

commit v2 on v1

--- a/solution.py
+++ b/solution.py
@@ -26,13 +26,15 @@
     return pl.BlockSpec(memory_space=pltpu.VMEM)
 
 
-def call(kernel, ins, outs, scratch=(), limit=24, apart=()):
-    places = [pl.BlockSpec(memory_space=pl.ANY) if i in apart else spec() for i in range(len(ins))]
+def call(kernel, ins, outs, scratch=(), limit=24, apart=(), apart_outs=()):
+    def places(count, left):
+        return [pl.BlockSpec(memory_space=pl.ANY) if i in left else spec() for i in range(count)]
+
     return pl.pallas_call(
         kernel,
         out_shape=[jax.ShapeDtypeStruct(s, F32) for s in outs],
-        in_specs=places,
-        out_specs=[spec() for _ in outs],
+        in_specs=places(len(ins), apart),
+        out_specs=places(len(outs), apart_outs),
         scratch_shapes=[pltpu.VMEM(s, F32) if isinstance(s, tuple) else s for s in scratch],
         compiler_params=pltpu.CompilerParams(vmem_limit_bytes=limit * 1024 * 1024),
     )(*ins)
@@ -126,6 +128,10 @@
         product = jnp.dot(part, matrix, preferred_element_type=F32)
         total = product if total is None else total + product
     return total
+
+
+BEHIND = (0, H0, 2 * H0, 3 * H0 - 1)
+AHEAD = (0, H0, 2 * H0 - 1, 3 * H0 - 2)
 
 
 def fetch(pairs, sems):
@@ -157,8 +163,10 @@
                 value = jnp.where(last, 0.0, value)
             part = slice(8 * b, 8 * b + 8)
             own[a, :, part] = value
-            to_right[a, :, part] = value[R0 - H0 :]
-            to_left[a, :, part] = value[:H0]
+            first, count = R0 - H0 + (a > 1), H0 - (a > 1)
+            to_right[BEHIND[a] : BEHIND[a] + count, part] = value[first:]
+            count = H0 - (a > 0)
+            to_left[AHEAD[a] : AHEAD[a] + count, part] = value[:count]
 
 
 def edge_kernel(own, behind, ahead, to_right, to_left):
@@ -166,17 +174,18 @@
 
     def plane(a, p):
         if p < H0:
-            return behind[a, p]
+            return behind[BEHIND[a] + p - (a > 1)] if p or a < 2 else None
         if p < H0 + R0:
             return own[a, p - H0]
-        return ahead[a, p - H0 - R0]
+        return ahead[AHEAD[a] + p - H0 - R0] if p < N0 - 1 or a == 0 else None
 
     for a in range(4):
         for c in range(GROUPS):
             right = left = jnp.zeros((NZ, 128), F32)
             for k in range(8):
-                if 8 * c + k < N0:
-                    value = roll(plane(a, 8 * c + k), 16 * k + 16, 1)
+                value = plane(a, 8 * c + k) if 8 * c + k < N0 else None
+                if value is not None:
+                    value = roll(value, 16 * k + 16, 1)
                     right = jnp.where(lane // 16 == k, value, right)
                     left = jnp.where(lane // 16 == (k + 1) % 8, value, left)
             to_right[a, c] = right
@@ -185,14 +194,15 @@
 
 def down_kernel(
     own, behind, ahead, from_left, from_right,
-    keep0, ops1, own1, kept_f1, to_right, to_left, own3,
-    ext, fx, fy, fz, d, g, f, va, vb, t, t1, d1, f1, va1, vb1, x2, y2, z2, e2,
+    keep0, out_ops1, out_f1, own1, edge_f1, to_right, to_left,
+    ext, fx, fy, fz, d, g, f, va, vb, t, t1, ops1, d1, f1, va1, vb1, x2, y2, z2, e2, sems,
 ):
     lane = lanes((NZ, 128))
     for a in range(4):
-        ext[a, 0:H0, :, 0:128] = behind[a]
+        skip, count = int(a > 1), H0 - (a > 0)
+        ext[a, skip:H0, :, 0:128] = behind[BEHIND[a] : BEHIND[a] + H0 - skip]
         ext[a, H0 : H0 + R0, :, 0:128] = own[a]
-        ext[a, H0 + R0 : N0, :, 0:128] = ahead[a]
+        ext[a, H0 + R0 : H0 + R0 + count, :, 0:128] = ahead[AHEAD[a] : AHEAD[a] + count]
         for c in range(GROUPS):
             left, right = from_left[a, c], from_right[a, c]
             for k in range(8):
@@ -237,9 +247,9 @@
         sweep(src, dst, f, g, fx, fy, fz, 2 + s, N0 - 2 - s)
         src, dst = dst, src
 
-    lo = H0 - 4
-    for i, ref in enumerate((src, f, g, fx, fy, fz)):
-        keep0[i] = ref[lo : lo + 24]
+    part = pl.ds(H0 - 4, 24)
+    pairs = [(ref.at[part], keep0.at[i]) for i, ref in enumerate((src, f, g, fx, fy, fz))]
+    copies = fetch(pairs, sems)
 
     def to1(row):
         return jnp.where(row < 192, row // 2, row // 2 - 128) + 32
@@ -277,12 +287,14 @@
         va1[q] = scale * f1[q]
 
     planes(1, N1, operator1)
+    copies += fetch(((ops1, out_ops1), (f1, out_f1)), sems.at[pl.ds(6, 2)])
     src, dst = va1, vb1
     for s in range(NU - 1):
         sweep(src, dst, f1, g1, x1, y1, z1, 3 + s, N1 - 3 - s)
         src, dst = dst, src
     own1[...] = src[H1 : H1 + 8]
-    kept_f1[...] = f1[...]
+    edge_f1[0] = f1[H1 + 4]
+    edge_f1[1] = f1[H1 + 8 - 5]
     residual(src, dst, f1, d1, x1, y1, z1, H1, H1 + 8)
 
     half, half_odd = (selection(128, 128, lambda row: row // 2, odd) for odd in (False, True))
@@ -326,15 +338,13 @@
         for a, value in enumerate((x3[i + 1], y3[i], z3[i], d3)):
             spot = 32 * a + 16 * i
             total = jnp.where(lane // 16 == spot // 16, roll(value, spot - 8, 1), total)
-    own3[...] = total
     to_right[11] = total
     to_left[11] = total
-
-
-def join_kernel(
-    own2, own1, f1, left, right, left3, right3,
-    joined2, first2, last2, joined1, to_right, to_left, near3,
-):
+    for copy in copies:
+        copy.wait()
+
+
+def join_kernel(own2, own1, edge_f1, left, right, joined2, joined1, to_right, to_left):
     lane = lanes((NZ, 128))
     low, high = lane % 64 < 16, lane % 64 >= 48
     for a in range(10):
@@ -343,7 +353,6 @@
         joined2[a] = value
         to_right[a] = value
         to_left[a] = value
-        (last2 if a % 2 else first2)[a // 2] = value
     low, high = lane // 8 == 3, lane // 8 == 12
     for k in range(8):
         value = jnp.where(low, roll(left[10], 24 - 8 * k, 1), own1[k])
@@ -353,17 +362,17 @@
             to_right[10 + k - 8 + H1] = value
         if k < H1:
             to_left[10 + k] = value
-    to_right[10 + H1] = f1[H1 + 8 - 5]
-    to_left[10 + H1] = f1[H1 + 4]
-    for s, value in enumerate((left3[...], left[11], own2[11], right[11], right3[...])):
-        near3[s] = value
+    to_right[10 + H1] = edge_f1[1]
+    to_left[10 + H1] = edge_f1[0]
 
 
 def rows_of(value, odd):
     return roll(value, 64, 1) if odd else value
 
 
-def middle_kernel(behind, own, ahead, out, f, fx, fy, fz, d, g, va, vb):
+def middle_kernel(
+    behind, own, ahead, left, right, to_right, to_left, f, fx, fy, fz, d, g, va, vb
+):
     for j in range(12):
         source = (behind, own, ahead)[j // 4]
         for a, ref in enumerate((f, fx, fy, fz, d)):
@@ -385,58 +394,52 @@
     value = total[:8]
     for b in range(1, 4):
         value = value + roll(total[8 * b : 8 * b + 8], 32 * b, 1)
-    out[...] = value
-
-
-def near_kernel(count, *refs):
+    to_right[0:8] = value
+    to_right[8:40] = left[11]
+    to_left[0:8] = value
+    to_left[8:40] = right[11]
+
+
+def near_kernel(count, own2, own, left2, right2, left, right, left_far, right_far, out):
+    rhs = (left_far[0:8], left[0:8], own[0:8], right[0:8], right_far[0:8])
+    ops = (left[8:40], left2[11], own2[11], right2[11], right[8:40])
     for c in range(count):
         for s in range(5):
-            refs[5][c, s] = refs[s][...]
+            out[c, s, 0:8] = rhs[s]
+            out[c, s, 8:40] = ops[s]
 
 
 PAD3 = 8
 
 
-def spread3_kernel(count, gathered, ops3):
+def turned(parts):
+    slot = lanes(parts[0].shape) // 16
+    rolled = [roll(part, 16 * s, 1) for s, part in enumerate(parts)]
+    results = []
+    for m in range(8):
+        total = jnp.zeros_like(parts[0])
+        for s, value in enumerate(rolled):
+            total = jnp.where(slot == (m + s) % 8, value, total)
+        results.append(roll(total, -16 * m, 1))
+    return results
+
+
+def solve_kernel(count, gathered, out, ops3, f3, va3, vb3):
     rows = 2 * count
     lo, hi = PAD3, PAD3 + rows
-    lane = lanes((NZ, 128))
-    for a in range(4):
-        ops3[a, 0:lo] = jnp.zeros((PAD3, NZ, 128), F32)
-        ops3[a, hi : hi + PAD3] = jnp.zeros((PAD3, NZ, 128), F32)
-
-    def unpack(i, carry):
-        for a in range(4):
-            for r in range(2):
-                total = jnp.zeros((NZ, 128), F32)
-                for s in range(5):
-                    value = roll(gathered[i, s], 16 * s - 32 * a - 16 * r, 1)
-                    total = jnp.where(lane // 16 == s, value, total)
-                ops3[a, lo + 2 * i + r] = scale_of(total) if a == 3 else total
-        return carry
-
-    lax.fori_loop(0, count, unpack, 0)
-
-
-def solve_kernel(count, rhs3, ops3, out, f3, va3, vb3):
-    rows = 2 * count
-    lo, hi = PAD3, PAD3 + rows
-    lane8 = lanes((8, 128))
     x3, y3, z3, g3 = (ops3.at[a] for a in range(4))
-    for ref in (va3, vb3):
+    for ref in (va3, vb3, x3):
         ref[0:lo] = jnp.zeros((PAD3, NZ, 128), F32)
         ref[hi : hi + PAD3] = jnp.zeros((PAD3, NZ, 128), F32)
 
     def unpack(i, carry):
-        for r in range(2):
-            p = lo + 2 * i + r
-            for b in range(4):
-                total = jnp.zeros((8, 128), F32)
-                for s in range(5):
-                    value = roll(rhs3[i, s], 16 * s - 32 * b - 16 * r, 1)
-                    total = jnp.where(lane8 // 16 == s, value, total)
-                f3[p, 8 * b : 8 * b + 8] = total
-                va3[p, 8 * b : 8 * b + 8] = total * g3[p, 8 * b : 8 * b + 8]
+        p = lo + 2 * i
+        for m, value in enumerate(turned([gathered[i, s, 8:40] for s in range(5)])):
+            ops3[m // 2, p + m % 2] = scale_of(value) if m >= 6 else value
+        for m, value in enumerate(turned([gathered[i, s, 0:8] for s in range(5)])):
+            part = slice(8 * (m // 2), 8 * (m // 2) + 8)
+            f3[p + m % 2, part] = value
+            va3[p + m % 2, part] = value * g3[p + m % 2, part]
         return carry
 
     lax.fori_loop(0, count, unpack, 0)
@@ -453,19 +456,27 @@
 
 
 def up_kernel(
-    e3, behind3, behind2, behind, joined2, ahead, ahead2, ahead3, joined1, kept_f1, in_ops1, in_keep0,
+    e3, all2, in_behind, in_ahead, in_joined1, in_f1, in_ops1, in_keep0,
     out,
-    f2, x2, y2, z2, d2, g2, va2, vb2, f1, va1, vb1, va0, vb0, ops1, keep0, sems,
+    f2, x2, y2, z2, d2, g2, va2, vb2, f1, va1, vb1, va0, vb0,
+    wide2, behind, ahead, joined1, ops1, keep0, sems,
 ):
-    copies = fetch(((in_ops1, ops1), (in_keep0, keep0)), sems)
-    sources = [(behind3, None)]
-    sources += [(ref, h) for ref in (behind2, behind, joined2, ahead, ahead2) for h in range(2)]
-    sources += [(ahead3, None)]
-    for n, (source, h) in enumerate(sources):
-        for a, ref in enumerate((f2, x2, y2, z2, d2)):
-            value = source[a if h is None else 2 * a + h]
-            ref[2 * n] = value
-            ref[2 * n + 1] = roll(value, 64, 1)
+    me, ends = lax.axis_index("gx"), lax.axis_size("gx") - 1
+    pairs = [(all2.at[jnp.clip(me + n - 3, 0, ends)], wide2.at[n]) for n in range(7)]
+    rows1 = pl.ds(10, 1 + H1)
+    pairs += [(in_behind.at[rows1], behind), (in_ahead.at[rows1], ahead), (in_joined1, joined1)]
+    pairs += [(in_f1, f1), (in_ops1, ops1), (in_keep0, keep0)]
+    copies = fetch(pairs, sems)
+    for n in range(7):
+        copies[n].wait()
+        inside = (me + n - 3 >= 0) & (me + n - 3 <= ends)
+        for h in range(2):
+            j = 4 * n + 2 * h - 2
+            if 0 <= j < 24:
+                for a, ref in enumerate((f2, x2, y2, z2, d2)):
+                    value = jnp.where(inside, wide2[n, 2 * a + h], 0.0)
+                    ref[j] = value
+                    ref[j + 1] = roll(value, 64, 1)
 
     def operator2(j):
         g2[j] = scale_of(d2[j])
@@ -487,27 +498,27 @@
         sweep(src, dst, f2, g2, x2, y2, z2, 4 + s, 20 - s, 32)
         src, dst = dst, src
 
-    copies[0].wait()
+    for copy in copies[7:12]:
+        copy.wait()
     x1, y1, z1, g1 = ops1.at[0], ops1.at[1], ops1.at[2], ops1.at[4]
-    f1[...] = kept_f1[...]
-    f1[1] = behind[10 + H1]
-    f1[N1 - 2] = ahead[10 + H1]
+    f1[1] = behind[H1]
+    f1[N1 - 2] = ahead[H1]
     spread = (row == (col - 32 + 128) // 2 - 64 + 16).astype(F32)
     coarse = dot(src[7:17].reshape(10 * NZ, 128), spread).reshape(10, NZ, 128)
     for q in range(N1):
         if q < H1:
-            value = behind[10 + q]
+            value = behind[q]
         elif q < H1 + 8:
             value = joined1[q - H1]
         else:
-            value = ahead[10 + q - H1 - 8]
+            value = ahead[q - H1 - 8]
         va1[q] = value + jnp.where(g1[q] > 0.0, coarse[q // 2], 0.0)
     src, dst = va1, vb1
     for s in range(NU):
         sweep(src, dst, f1, g1, x1, y1, z1, 1 + s, N1 - 1 - s, 32)
         src, dst = dst, src
 
-    copies[1].wait()
+    copies[12].wait()
     v0, f0, g0, x0, y0, z0 = (keep0.at[a] for a in range(6))
     col = lax.broadcasted_iota(jnp.int32, (128, 256), 1)
     row = lax.broadcasted_iota(jnp.int32, (128, 256), 0)
@@ -540,10 +551,11 @@
     own, to_right, to_left = call(
         stage_kernel,
         (labels, conduct_x, conduct_y, conduct_z),
-        [(4, R0, *side), (4, H0, *side), (4, H0, *side)],
+        [(4, R0, *side), (4 * H0 - 2, *side), (4 * H0 - 3, *side)],
         [pltpu.VMEM(labels.shape, labels.dtype)]
         + [pltpu.VMEM(labels.shape, conduct_x.dtype)] * 3
         + [pltpu.SemaphoreType.DMA((4,))],
+        limit=58,
         apart=(0, 1, 2, 3),
     )
     behind = shift(to_right, "gx", 1)
@@ -551,56 +563,62 @@
     to_right, to_left = call(edge_kernel, (own, behind, ahead), [(4, GROUPS, *side)] * 2)
     from_left = shift(to_right, "gy", 1)
     from_right = shift(to_left, "gy", -1)
-    keep0, ops1, own1, kept_f1, to_right, to_left, own3 = call(
+    keep0, ops1, f1, own1, edge_f1, to_right2, to_left2 = call(
         down_kernel,
         (own, behind, ahead, from_left, from_right),
-        [(6, 24, NZ, 256), (5, N1, *side), (8, *side), (N1, *side), (12, *side), (12, *side), side],
+        [(6, 24, NZ, 256), (5, N1, *side), (N1, *side), (8, *side), (2, *side)]
+        + [(12, *side)] * 2,
         [(4, N0, NZ, 256)]
         + [wide] * 9
-        + [(4, N1, NZ, 256)]
+        + [(4, N1, NZ, 256), (5, N1, *side)]
         + [(N1, *side)] * 4
         + [(5, *side)]
-        + [(4, *side)] * 3,
+        + [(4, *side)] * 3
+        + [pltpu.SemaphoreType.DMA((8,))],
         limit=44,
+        apart_outs=(0, 1, 2),
+    )
+    left2, right2 = shift(to_right2, "gy", 1), shift(to_left2, "gy", -1)
+    joined2, joined1, to_right, to_left = call(
+        join_kernel,
+        (to_right2, own1, edge_f1, left2, right2),
+        [(10, *side), (8, *side)] + [(11 + H1, *side)] * 2,
+    )
+    all2 = lax.all_gather(joined2, "gx")
+    behind, ahead = shift(to_right, "gx", 1), shift(to_left, "gx", -1)
+    to_right, to_left = call(
+        middle_kernel,
+        (behind, joined2, ahead, left2, right2),
+        [(40, 128)] * 2,
+        [(12, *side)] * 8,
     )
     left, right = shift(to_right, "gy", 1), shift(to_left, "gy", -1)
-    left3, right3 = shift(own3, "gy", 2), shift(own3, "gy", -2)
-    joined2, first2, last2, joined1, to_right, to_left, near3 = call(
-        join_kernel,
-        (to_right, own1, kept_f1, left, right, left3, right3),
-        [(10, *side), (5, *side), (5, *side), (8, *side)]
-        + [(11 + H1, *side)] * 2
-        + [(5, *side)],
-    )
-    all3 = lax.all_gather(near3, "gx")
-    behind, ahead = shift(to_right, "gx", 1), shift(to_left, "gx", -1)
-    (rhs3,) = call(middle_kernel, (behind, joined2, ahead), [(8, 128)], [(12, *side)] * 8)
-    rhs3, joined2, first2, last2 = lax.optimization_barrier((rhs3, joined2, first2, last2))
-    around = [shift(rhs3, "gy", distance) for distance in (2, 1, -1, -2)]
-    behind2, ahead2 = shift(joined2, "gx", 2), shift(joined2, "gx", -2)
-    behind3, ahead3 = shift(last2, "gx", 3), shift(first2, "gx", -3)
+    left_far, right_far = shift(left, "gy", 1), shift(right, "gy", -1)
     (rhs3,) = call(
         functools.partial(near_kernel, count),
-        (around[0], around[1], rhs3, around[2], around[3]),
-        [(count, 5, 8, 128)],
+        (to_right2, to_right, left2, right2, left, right, left_far, right_far),
+        [(count, 5, 40, 128)],
     )
     rhs3 = lax.all_to_all(rhs3, "gx", 0, 0)
     rows3 = 2 * count + 2 * PAD3
-    (ops3,) = call(functools.partial(spread3_kernel, count), (all3,), [(4, rows3, *side)])
     (e3,) = call(
-        functools.partial(solve_kernel, count), (rhs3, ops3), [(10, *side)], [(rows3, *side)] * 3
+        functools.partial(solve_kernel, count),
+        (rhs3,),
+        [(10, *side)],
+        [(4, rows3, *side)] + [(rows3, *side)] * 3,
     )
     (out,) = call(
         up_kernel,
-        (e3, behind3, behind2, behind, joined2, ahead, ahead2, ahead3, joined1, kept_f1, ops1, keep0),
+        (e3, all2, behind, ahead, joined1, f1, ops1, keep0),
         [(NZ, R0, 128)],
         [(24, *side)] * 8
         + [(N1, *side)] * 3
         + [(24, NZ, 256)] * 2
+        + [(7, 10, *side), (1 + H1, *side), (1 + H1, *side), (8, *side)]
         + [(5, N1, *side), (6, 24, NZ, 256)]
-        + [pltpu.SemaphoreType.DMA((2,))],
-        limit=30,
-        apart=(10, 11),
+        + [pltpu.SemaphoreType.DMA((13,))],
+        limit=58,
+        apart=range(1, 8),
     )
     return out
 

time: 173 us -> 172 us (level)
  the two profiles are of different devices: /device:TPU:6 before, /device:TPU:97 now
where the time goes in v2:
time: 172 us; the launch traced here: 171 us
  waiting for transfers between devices  44.9 us (26%)
  blocking collectives  39.9 us (23%)
  Pallas kernels  35.1 us (20%)
  starting transfers between devices  33.1 us (19%)
  between operations  13.6 us (8%)
  local copies, waits for them, and re-layouts  4.51 us (3%)
    ppermute x12, waiting for transfers between devices, shift(): return lax.ppermute(value, axis, route)  44.9 us
    all_to_all x1, blocking collectives, body(): rhs3 = lax.all_to_all(rhs3, 'gx', 0, 0)  39.9 us
    pallas_call x8, Pallas kernels, call(): pl.pallas_call(kernel, out_shape=[jax.ShapeDtypeStruct(s, F32) for s in o...  35.1 us
    ppermute x12, starting transfers between devices, shift(): return lax.ppermute(value, axis, route)  33.1 us
    unnamed x16, local copies, waits for them, and re-layouts  4.51 us
  transfers between devices with their start and end apart: 13, of which 8 were waited for; matrix products, arithmetic and copies ran while one was open for 0% of the time, Pallas kernels for 7%

profile of v2, /device:TPU:97, one launch (start us, length us, event | category | flops | bytes accessed | tf_op | source)
XLA Modules:
  0.0 171.2 jit_solution(1892559406138901356)
XLA Ops:
  6.5 2.9 %shard_map.46 = (f32[4,16,32,128]{3,2,1,0:T(8,128)}, f32[50,32,128]{2,1,0:T(8,128)}, f32[49,32,128]{2,1,0:T(8,128)}) custom-call(s32[32,16,128]{2,1,0:T(8,128)} %in0.1, bf16[32,16,128]{2,1,0:T(8,128)(2,1)} %in1.1, bf16[32,16,128]{2,1,0:T(8,128)(2,1)} %in2.1, bf16[32,16,128]{2,1,0:T(8,128)(2,1)} %in3.1), custom_call_target="tpu_custom_call" | custom-call | tf_op jit(solution)/shard_map/pallas_call | solution.py:33
  9.4 3.3 %collective-permute-start = (f32[50,32,128]{2,1,0:T(8,128)}, f32[50,32,128]{2,1,0:T(8,128)S(1)}, u32[]{:S(2)}, u32[]{:S(2)}) collective-permute-start(f32[50,32,128]{2,1,0:T(8,128)} %get-tuple-element.24), channel_id=1, source_target_pairs={{0,16},{16,32},{32,48},{48,64},{64,80},{80,96},{96,112},{112,128},... | collective-permute-start | bytes 2457608 | tf_op jit(solution)/shard_map/ppermute | solution.py:544
  12.7 1.3 collective-permute-start.1
  14.0 19.2 %collective-permute-done.1.ahead = f32[49,32,128]{2,1,0:T(8,128)S(1)} collective-permute-done((f32[49,32,128]{2,1,0:T(8,128)}, f32[49,32,128]{2,1,0:T(8,128)S(1)}, u32[]{:S(2)}, u32[]{:S(2)}) %collective-permute-start.1) | collective-permute-done | bytes 802848 | tf_op jit(solution)/shard_map/ppermute | solution.py:544
  33.2 1.2 copy-done
  34.5 0.7 shard_map.47
  35.1 6.5 %collective-permute-start.2 = (f32[4,6,32,128]{3,2,1,0:T(8,128)S(1)}, f32[4,6,32,128]{3,2,1,0:T(8,128)S(1)}, u32[]{:S(2)}, u32[]{:S(2)}) collective-permute-start(f32[4,6,32,128]{3,2,1,0:T(8,128)S(1)} %get-tuple-element.26), channel_id=1, source_target_pairs={{0,1},{1,2},{2,3},{3,4},{4,5},{5,6},{6,7},{7,8},{8,9},{9,10},{10,1... | collective-permute-start | bytes 1179656 | tf_op jit(solution)/shard_map/ppermute | solution.py:544
  41.7 1.9 %collective-permute-start.3 = (f32[4,6,32,128]{3,2,1,0:T(8,128)S(1)}, f32[4,6,32,128]{3,2,1,0:T(8,128)S(1)}, u32[]{:S(2)}, u32[]{:S(2)}) collective-permute-start(f32[4,6,32,128]{3,2,1,0:T(8,128)S(1)} %get-tuple-element.27), channel_id=1, source_target_pairs={{1,0},{2,1},{3,2},{4,3},{5,4},{6,5},{7,6},{8,7},{9,8},{10,9},{11,1... | collective-permute-start | bytes 1179656 | tf_op jit(solution)/shard_map/ppermute | solution.py:544
  43.6 2.8 %collective-permute-done.2.from_left = f32[4,6,32,128]{3,2,1,0:T(8,128)S(1)} collective-permute-done((f32[4,6,32,128]{3,2,1,0:T(8,128)S(1)}, f32[4,6,32,128]{3,2,1,0:T(8,128)S(1)}, u32[]{:S(2)}, u32[]{:S(2)}) %collective-permute-start.2) | collective-permute-done | bytes 393248 | tf_op jit(solution)/shard_map/ppermute | solution.py:544
  46.4 5.6 %collective-permute-done.3.from_right = f32[4,6,32,128]{3,2,1,0:T(8,128)S(1)} collective-permute-done((f32[4,6,32,128]{3,2,1,0:T(8,128)S(1)}, f32[4,6,32,128]{3,2,1,0:T(8,128)S(1)}, u32[]{:S(2)}, u32[]{:S(2)}) %collective-permute-start.3) | collective-permute-done | bytes 393248 | tf_op jit(solution)/shard_map/ppermute | solution.py:544
  52.0 11.1 %shard_map.48 = (f32[6,24,32,256]{3,2,1,0:T(8,128)}, f32[5,20,32,128]{3,2,1,0:T(8,128)S(1)}, f32[20,32,128]{2,1,0:T(8,128)S(1)}, f32[8,32,128]{2,1,0:T(8,128)S(1...) custom-call(f32[4,16,32,128]{3,2,1,0:T(8,128)S(1)} %copy-done.1, ...), custom_call_target="tpu_custom_call" | custom-call | tf_op jit(solution)/shard_map/pallas_call | solution.py:33
  63.1 1.2 copy-done.2
  64.3 0.7 copy-done.6
  65.1 1.9 %collective-permute-start.4 = (f32[12,32,128]{2,1,0:T(8,128)S(1)}, f32[12,32,128]{2,1,0:T(8,128)S(1)}, u32[]{:S(2)}, u32[]{:S(2)}) collective-permute-start(f32[12,32,128]{2,1,0:T(8,128)S(1)} %get-tuple-element.28.own2), channel_id=1, source_target_pairs={{0,1},{1,2},{2,3},{3,4},{4,5},{5,6},{6,7},{7,8},{8,9},{9,10},{10,1... | collective-permute-start | bytes 589832 | tf_op jit(solution)/shard_map/ppermute | solution.py:544
  67.0 2.4 %collective-permute-start.5 = (f32[12,32,128]{2,1,0:T(8,128)S(1)}, f32[12,32,128]{2,1,0:T(8,128)S(1)}, u32[]{:S(2)}, u32[]{:S(2)}) collective-permute-start(f32[12,32,128]{2,1,0:T(8,128)S(1)} %get-tuple-element.31), channel_id=1, source_target_pairs={{1,0},{2,1},{3,2},{4,3},{5,4},{6,5},{7,6},{8,7},{9,8},{10,9},{11,1... | collective-permute-start | bytes 589832 | tf_op jit(solution)/shard_map/ppermute | solution.py:544
  69.6 5.6 %collective-permute-done.5.right.right2 = f32[12,32,128]{2,1,0:T(8,128)S(1)} collective-permute-done((f32[12,32,128]{2,1,0:T(8,128)S(1)}, f32[12,32,128]{2,1,0:T(8,128)S(1)}, u32[]{:S(2)}, u32[]{:S(2)}) %collective-permute-start.5) | collective-permute-done | bytes 196640 | tf_op jit(solution)/shard_map/ppermute | solution.py:544
  75.2 0.8 shard_map.49
  76.0 0.6 copy-done.7
  76.7 3.2 %collective-permute-start.6 = (f32[17,32,128]{2,1,0:T(8,128)S(1)}, f32[17,32,128]{2,1,0:T(8,128)S(1)}, u32[]{:S(2)}, u32[]{:S(2)}) collective-permute-start(f32[17,32,128]{2,1,0:T(8,128)S(1)} %get-tuple-element.32), channel_id=1, source_target_pairs={{0,16},{16,32},{32,48},{48,64},{64,80},{80,96},{96,112},{112,128},... | collective-permute-start | bytes 835592 | tf_op jit(solution)/shard_map/ppermute | solution.py:544
  79.8 1.3 collective-permute-start.7
  81.1 3.0 %collective-permute-done.6.behind.in_behind = f32[17,32,128]{2,1,0:T(8,128)S(1)} collective-permute-done((f32[17,32,128]{2,1,0:T(8,128)S(1)}, f32[17,32,128]{2,1,0:T(8,128)S(1)}, u32[]{:S(2)}, u32[]{:S(2)}) %collective-permute-start.6) | collective-permute-done | bytes 278560 | tf_op jit(solution)/shard_map/ppermute | solution.py:544
  84.1 4.1 %collective-permute-done.7.ahead.in_ahead = f32[17,32,128]{2,1,0:T(8,128)S(1)} collective-permute-done((f32[17,32,128]{2,1,0:T(8,128)S(1)}, f32[17,32,128]{2,1,0:T(8,128)S(1)}, u32[]{:S(2)}, u32[]{:S(2)}) %collective-permute-start.7) | collective-permute-done | bytes 278560 | tf_op jit(solution)/shard_map/ppermute | solution.py:544
  88.3 1.7 shard_map.50
  89.9 2.7 %collective-permute-start.8 = (f32[40,128]{1,0:T(8,128)S(1)}, f32[40,128]{1,0:T(8,128)S(1)}, u32[]{:S(2)}, u32[]{:S(2)}) collective-permute-start(f32[40,128]{1,0:T(8,128)S(1)} %get-tuple-element.35.own), channel_id=1, source_target_pairs={{0,1},{1,2},{2,3},{3,4},{4,5},{5,6},{6,7},{7,8},{8,9},{9,10},{10,1... | collective-permute-start | bytes 61448 | tf_op jit(solution)/shard_map/ppermute | solution.py:544
  92.6 1.9 %collective-permute-start.9 = (f32[40,128]{1,0:T(8,128)S(1)}, f32[40,128]{1,0:T(8,128)S(1)}, u32[]{:S(2)}, u32[]{:S(2)}) collective-permute-start(f32[40,128]{1,0:T(8,128)S(1)} %get-tuple-element.36), channel_id=1, source_target_pairs={{1,0},{2,1},{3,2},{4,3},{5,4},{6,5},{7,6},{8,7},{9,8},{10,9},{11,1... | collective-permute-start | bytes 61448 | tf_op jit(solution)/shard_map/ppermute | solution.py:544
  94.5 4.9 %collective-permute-start.10 = (f32[40,128]{1,0:T(8,128)S(1)}, f32[40,128]{1,0:T(8,128)S(1)}, u32[]{:S(2)}, u32[]{:S(2)}) collective-permute-start(f32[40,128]{1,0:T(8,128)S(1)} %collective-permute-done.8.left), channel_id=1, source_target_pairs={{0,1},{1,2},{2,3},{3,4},{4,5},{5,6},{6,7},{7,8},{8,9},{9,10},{10,1... | collective-permute-start | bytes 61448 | tf_op jit(solution)/shard_map/ppermute | solution.py:544
  99.4 1.9 %collective-permute-start.11 = (f32[40,128]{1,0:T(8,128)S(1)}, f32[40,128]{1,0:T(8,128)S(1)}, u32[]{:S(2)}, u32[]{:S(2)}) collective-permute-start(f32[40,128]{1,0:T(8,128)S(1)} %collective-permute-done.9.right), channel_id=1, source_target_pairs={{1,0},{2,1},{3,2},{4,3},{5,4},{6,5},{7,6},{8,7},{9,8},{10,9},{11,1... | collective-permute-start | bytes 61448 | tf_op jit(solution)/shard_map/ppermute | solution.py:544
  101.4 4.4 %collective-permute-done.11.right_far = f32[40,128]{1,0:T(8,128)S(1)} collective-permute-done((f32[40,128]{1,0:T(8,128)S(1)}, f32[40,128]{1,0:T(8,128)S(1)}, u32[]{:S(2)}, u32[]{:S(2)}) %collective-permute-start.11) | collective-permute-done | bytes 20512 | tf_op jit(solution)/shard_map/ppermute | solution.py:544
  105.9 39.9 %all_to_all.5.gathered = f32[16,5,40,128]{3,2,1,0:T(8,128)S(1)} all-to-all(f32[16,5,40,128]{3,2,1,0:T(8,128)S(1)} %shard_map.51), channel_id=1, replica_groups=mesh['gx'=16,'gy'=16] {'gx'}, dimensions={0} | all-to-all | bytes 3276800 | tf_op jit(solution)/shard_map/all_to_all | solution.py:602
  145.8 10.1 %shard_map.52.e3 = f32[10,32,128]{2,1,0:T(8,128)S(1)} custom-call(f32[16,5,40,128]{3,2,1,0:T(8,128)S(1)} %all_to_all.5.gathered), custom_call_target="tpu_custom_call" | custom-call | tf_op jit(solution)/shard_map/pallas_call | solution.py:33
  155.9 0.7 copy-done.5
  156.6 7.8 %shard_map.53 = f32[32,16,128]{2,1,0:T(8,128)} custom-call(f32[10,32,128]{2,1,0:T(8,128)} %copy-done.5, f32[16,10,32,128]{3,2,1,0:T(8,128)} %bitcast.1, f32[17,32,128]{2,1,0:T(8,128)} %copy-done.3, f32[17,32,128]{2,1,0:T(8,128)} %copy-done.4, f32[8,32,128]{2,1,0:T(8,128)} %copy-done.7, f32[20,32,128]{2,1,0:T(8,128)} %copy-done.6, ...), custom_call_target="tpu_custom_call" | custom-call | tf_op jit(solution)/shard_map/pallas_call | solution.py:33
  (20 shorter events, 0.3 us)
Async XLA Ops:
  6.5 150.0 %all-gather.3.cloned.1.call-start = ((), (), s32[]{:S(2)}) async-start(), calls=%async_computation.1 | async-start | bytes 2785280 | tf_op jit(solution)/shard_map/all_gather | solution.py:587
  9.4 23.8 %collective-permute-start = (f32[50,32,128]{2,1,0:T(8,128)}, f32[50,32,128]{2,1,0:T(8,128)S(1)}, u32[]{:S(2)}, u32[]{:S(2)}) collective-permute-start(f32[50,32,128]{2,1,0:T(8,128)} %get-tuple-element.24), channel_id=1, source_target_pairs={{0,16},{16,32},{32,48},{48,64},{64,80},{80,96},{96,112},{112,128},... | collective-permute-start | bytes 2457608 | tf_op jit(solution)/shard_map/ppermute | solution.py:544
  12.7 20.5 %collective-permute-start.1 = (f32[49,32,128]{2,1,0:T(8,128)}, f32[49,32,128]{2,1,0:T(8,128)S(1)}, u32[]{:S(2)}, u32[]{:S(2)}) collective-permute-start(f32[49,32,128]{2,1,0:T(8,128)} %get-tuple-element.25), channel_id=1, source_target_pairs={{16,0},{32,16},{48,32},{64,48},{80,64},{96,80},{112,96},{128,112},... | collective-permute-start | bytes 2408456 | tf_op jit(solution)/shard_map/ppermute | solution.py:544
  33.2 1.2 copy-start
  34.5 17.5 %copy-start.1 = (f32[4,16,32,128]{3,2,1,0:T(8,128)S(1)}, f32[4,16,32,128]{3,2,1,0:T(8,128)}, u32[]{:S(2)}) copy-start(f32[4,16,32,128]{3,2,1,0:T(8,128)} %get-tuple-element.23.own) | copy-start | bytes 3145732
  35.1 11.2 %collective-permute-start.2 = (f32[4,6,32,128]{3,2,1,0:T(8,128)S(1)}, f32[4,6,32,128]{3,2,1,0:T(8,128)S(1)}, u32[]{:S(2)}, u32[]{:S(2)}) collective-permute-start(f32[4,6,32,128]{3,2,1,0:T(8,128)S(1)} %get-tuple-element.26), channel_id=1, source_target_pairs={{0,1},{1,2},{2,3},{3,4},{4,5},{5,6},{6,7},{7,8},{8,9},{9,10},{10,1... | collective-permute-start | bytes 1179656 | tf_op jit(solution)/shard_map/ppermute | solution.py:544
  41.7 10.3 %collective-permute-start.3 = (f32[4,6,32,128]{3,2,1,0:T(8,128)S(1)}, f32[4,6,32,128]{3,2,1,0:T(8,128)S(1)}, u32[]{:S(2)}, u32[]{:S(2)}) collective-permute-start(f32[4,6,32,128]{3,2,1,0:T(8,128)S(1)} %get-tuple-element.27), channel_id=1, source_target_pairs={{1,0},{2,1},{3,2},{4,3},{5,4},{6,5},{7,6},{8,7},{9,8},{10,9},{11,1... | collective-permute-start | bytes 1179656 | tf_op jit(solution)/shard_map/ppermute | solution.py:544
  63.1 1.2 copy-start.2
  64.3 0.7 copy-start.6
  65.1 4.5 %collective-permute-start.4 = (f32[12,32,128]{2,1,0:T(8,128)S(1)}, f32[12,32,128]{2,1,0:T(8,128)S(1)}, u32[]{:S(2)}, u32[]{:S(2)}) collective-permute-start(f32[12,32,128]{2,1,0:T(8,128)S(1)} %get-tuple-element.28.own2), channel_id=1, source_target_pairs={{0,1},{1,2},{2,3},{3,4},{4,5},{5,6},{6,7},{7,8},{8,9},{9,10},{10,1... | collective-permute-start | bytes 589832 | tf_op jit(solution)/shard_map/ppermute | solution.py:544
  67.0 8.2 %collective-permute-start.5 = (f32[12,32,128]{2,1,0:T(8,128)S(1)}, f32[12,32,128]{2,1,0:T(8,128)S(1)}, u32[]{:S(2)}, u32[]{:S(2)}) collective-permute-start(f32[12,32,128]{2,1,0:T(8,128)S(1)} %get-tuple-element.31), channel_id=1, source_target_pairs={{1,0},{2,1},{3,2},{4,3},{5,4},{6,5},{7,6},{8,7},{9,8},{10,9},{11,1... | collective-permute-start | bytes 589832 | tf_op jit(solution)/shard_map/ppermute | solution.py:544
  76.0 0.6 copy-start.7
  76.7 7.5 %collective-permute-start.6 = (f32[17,32,128]{2,1,0:T(8,128)S(1)}, f32[17,32,128]{2,1,0:T(8,128)S(1)}, u32[]{:S(2)}, u32[]{:S(2)}) collective-permute-start(f32[17,32,128]{2,1,0:T(8,128)S(1)} %get-tuple-element.32), channel_id=1, source_target_pairs={{0,16},{16,32},{32,48},{48,64},{64,80},{80,96},{96,112},{112,128},... | collective-permute-start | bytes 835592 | tf_op jit(solution)/shard_map/ppermute | solution.py:544
  79.8 8.4 %collective-permute-start.7 = (f32[17,32,128]{2,1,0:T(8,128)S(1)}, f32[17,32,128]{2,1,0:T(8,128)S(1)}, u32[]{:S(2)}, u32[]{:S(2)}) collective-permute-start(f32[17,32,128]{2,1,0:T(8,128)S(1)} %get-tuple-element.34), channel_id=1, source_target_pairs={{16,0},{32,16},{48,32},{64,48},{80,64},{96,80},{112,96},{128,112},... | collective-permute-start | bytes 835592 | tf_op jit(solution)/shard_map/ppermute | solution.py:544
  84.1 21.7 %copy-start.3 = (f32[17,32,128]{2,1,0:T(8,128)}, f32[17,32,128]{2,1,0:T(8,128)S(1)}, u32[]{:S(2)}) copy-start(f32[17,32,128]{2,1,0:T(8,128)S(1)} %collective-permute-done.6.behind.in_behind) | copy-start | bytes 835588
  88.3 17.6 %copy-start.4 = (f32[17,32,128]{2,1,0:T(8,128)}, f32[17,32,128]{2,1,0:T(8,128)S(1)}, u32[]{:S(2)}) copy-start(f32[17,32,128]{2,1,0:T(8,128)S(1)} %collective-permute-done.7.ahead.in_ahead) | copy-start | bytes 835588
  89.9 4.6 %collective-permute-start.8 = (f32[40,128]{1,0:T(8,128)S(1)}, f32[40,128]{1,0:T(8,128)S(1)}, u32[]{:S(2)}, u32[]{:S(2)}) collective-permute-start(f32[40,128]{1,0:T(8,128)S(1)} %get-tuple-element.35.own), channel_id=1, source_target_pairs={{0,1},{1,2},{2,3},{3,4},{4,5},{5,6},{6,7},{7,8},{8,9},{9,10},{10,1... | collective-permute-start | bytes 61448 | tf_op jit(solution)/shard_map/ppermute | solution.py:544
  92.6 6.8 %collective-permute-start.9 = (f32[40,128]{1,0:T(8,128)S(1)}, f32[40,128]{1,0:T(8,128)S(1)}, u32[]{:S(2)}, u32[]{:S(2)}) collective-permute-start(f32[40,128]{1,0:T(8,128)S(1)} %get-tuple-element.36), channel_id=1, source_target_pairs={{1,0},{2,1},{3,2},{4,3},{5,4},{6,5},{7,6},{8,7},{9,8},{10,9},{11,1... | collective-permute-start | bytes 61448 | tf_op jit(solution)/shard_map/ppermute | solution.py:544
  94.5 6.8 %collective-permute-start.10 = (f32[40,128]{1,0:T(8,128)S(1)}, f32[40,128]{1,0:T(8,128)S(1)}, u32[]{:S(2)}, u32[]{:S(2)}) collective-permute-start(f32[40,128]{1,0:T(8,128)S(1)} %collective-permute-done.8.left), channel_id=1, source_target_pairs={{0,1},{1,2},{2,3},{3,4},{4,5},{5,6},{6,7},{7,8},{8,9},{9,10},{10,1... | collective-permute-start | bytes 61448 | tf_op jit(solution)/shard_map/ppermute | solution.py:544
  99.4 6.3 %collective-permute-start.11 = (f32[40,128]{1,0:T(8,128)S(1)}, f32[40,128]{1,0:T(8,128)S(1)}, u32[]{:S(2)}, u32[]{:S(2)}) collective-permute-start(f32[40,128]{1,0:T(8,128)S(1)} %collective-permute-done.9.right), channel_id=1, source_target_pairs={{1,0},{2,1},{3,2},{4,3},{5,4},{6,5},{7,6},{8,7},{9,8},{10,9},{11,1... | collective-permute-start | bytes 61448 | tf_op jit(solution)/shard_map/ppermute | solution.py:544
  155.9 0.7 copy-start.5
Sparse Core Ops, SparseCore 0:
  76.8 65.5 all-gather.2

commit v3 on v2

--- a/solution.py
+++ b/solution.py
@@ -194,7 +194,7 @@
 
 def down_kernel(
     own, behind, ahead, from_left, from_right,
-    keep0, out_ops1, out_f1, own1, edge_f1, to_right, to_left,
+    keep0, out_ops1, out_f1, own1, edge_f1, to_right, to_left, own3,
     ext, fx, fy, fz, d, g, f, va, vb, t, t1, ops1, d1, f1, va1, vb1, x2, y2, z2, e2, sems,
 ):
     lane = lanes((NZ, 128))
@@ -338,8 +338,7 @@
         for a, value in enumerate((x3[i + 1], y3[i], z3[i], d3)):
             spot = 32 * a + 16 * i
             total = jnp.where(lane // 16 == spot // 16, roll(value, spot - 8, 1), total)
-    to_right[11] = total
-    to_left[11] = total
+    own3[...] = total
     for copy in copies:
         copy.wait()
 
@@ -371,7 +370,7 @@
 
 
 def middle_kernel(
-    behind, own, ahead, left, right, to_right, to_left, f, fx, fy, fz, d, g, va, vb
+    count, behind, own, ahead, ops3, message, further, nearer, f, fx, fy, fz, d, g, va, vb
 ):
     for j in range(12):
         source = (behind, own, ahead)[j // 4]
@@ -394,19 +393,22 @@
     value = total[:8]
     for b in range(1, 4):
         value = value + roll(total[8 * b : 8 * b + 8], 32 * b, 1)
-    to_right[0:8] = value
-    to_right[8:40] = left[11]
-    to_left[0:8] = value
-    to_left[8:40] = right[11]
-
-
-def near_kernel(count, own2, own, left2, right2, left, right, left_far, right_far, out):
-    rhs = (left_far[0:8], left[0:8], own[0:8], right[0:8], right_far[0:8])
-    ops = (left[8:40], left2[11], own2[11], right2[11], right[8:40])
+    message[count, 0:8] = value
+    message[count, 8:] = jnp.zeros((NZ - 8, 128), F32)
+    for i in range(count):
+        message[i] = ops3[i]
+    further[...] = behind[0:10]
+    nearer[...] = ahead[0:10]
+
+
+def near_kernel(count, own, left, right, left_far, right_far, behind2, ahead2, out, further, nearer):
+    rhs = [ref[count, 0:8] for ref in (left_far, left, own, right, right_far)]
     for c in range(count):
         for s in range(5):
-            out[c, s, 0:8] = rhs[s]
-            out[c, s, 8:40] = ops[s]
+            out[c, s] = rhs[s]
+    for a in range(5):
+        further[a] = behind2[2 * a + 1]
+        nearer[a] = ahead2[2 * a]
 
 
 PAD3 = 8
@@ -424,7 +426,9 @@
     return results
 
 
-def solve_kernel(count, gathered, out, ops3, f3, va3, vb3):
+def solve_kernel(
+    count, gathered, own, left, right, left_far, right_far, out, ops3, f3, va3, vb3
+):
     rows = 2 * count
     lo, hi = PAD3, PAD3 + rows
     x3, y3, z3, g3 = (ops3.at[a] for a in range(4))
@@ -434,9 +438,9 @@
 
     def unpack(i, carry):
         p = lo + 2 * i
-        for m, value in enumerate(turned([gathered[i, s, 8:40] for s in range(5)])):
+        for m, value in enumerate(turned([ref[i] for ref in (left_far, left, own, right, right_far)])):
             ops3[m // 2, p + m % 2] = scale_of(value) if m >= 6 else value
-        for m, value in enumerate(turned([gathered[i, s, 0:8] for s in range(5)])):
+        for m, value in enumerate(turned([gathered[i, s] for s in range(5)])):
             part = slice(8 * (m // 2), 8 * (m // 2) + 8)
             f3[p + m % 2, part] = value
             va3[p + m % 2, part] = value * g3[p + m % 2, part]
@@ -456,27 +460,28 @@
 
 
 def up_kernel(
-    e3, all2, in_behind, in_ahead, in_joined1, in_f1, in_ops1, in_keep0,
+    e3, in_behind3, in_behind2, in_behind, in_own, in_ahead, in_ahead2, in_ahead3,
+    in_joined1, in_f1, in_ops1, in_keep0,
     out,
     f2, x2, y2, z2, d2, g2, va2, vb2, f1, va1, vb1, va0, vb0,
-    wide2, behind, ahead, joined1, ops1, keep0, sems,
+    behind3, behind2, behind, own, ahead, ahead2, ahead3, joined1, ops1, keep0, sems,
 ):
-    me, ends = lax.axis_index("gx"), lax.axis_size("gx") - 1
-    pairs = [(all2.at[jnp.clip(me + n - 3, 0, ends)], wide2.at[n]) for n in range(7)]
-    rows1 = pl.ds(10, 1 + H1)
-    pairs += [(in_behind.at[rows1], behind), (in_ahead.at[rows1], ahead), (in_joined1, joined1)]
-    pairs += [(in_f1, f1), (in_ops1, ops1), (in_keep0, keep0)]
+    pairs = [
+        (in_behind3, behind3), (in_behind2, behind2), (in_behind, behind), (in_own, own),
+        (in_ahead, ahead), (in_ahead2, ahead2), (in_ahead3, ahead3),
+        (in_joined1, joined1), (in_f1, f1), (in_ops1, ops1), (in_keep0, keep0),
+    ]
     copies = fetch(pairs, sems)
-    for n in range(7):
-        copies[n].wait()
-        inside = (me + n - 3 >= 0) & (me + n - 3 <= ends)
-        for h in range(2):
-            j = 4 * n + 2 * h - 2
-            if 0 <= j < 24:
-                for a, ref in enumerate((f2, x2, y2, z2, d2)):
-                    value = jnp.where(inside, wide2[n, 2 * a + h], 0.0)
-                    ref[j] = value
-                    ref[j + 1] = roll(value, 64, 1)
+    sources = [(behind3, None)]
+    sources += [(ref, h) for ref in (behind2, behind, own, ahead, ahead2) for h in range(2)]
+    sources += [(ahead3, None)]
+    for n, (source, h) in enumerate(sources):
+        if n % 2 or n == 0:
+            copies[(n + 1) // 2].wait()
+        for a, ref in enumerate((f2, x2, y2, z2, d2)):
+            value = source[a if h is None else 2 * a + h]
+            ref[2 * n] = value
+            ref[2 * n + 1] = roll(value, 64, 1)
 
     def operator2(j):
         g2[j] = scale_of(d2[j])
@@ -498,27 +503,27 @@
         sweep(src, dst, f2, g2, x2, y2, z2, 4 + s, 20 - s, 32)
         src, dst = dst, src
 
-    for copy in copies[7:12]:
+    for copy in copies[7:10]:
         copy.wait()
     x1, y1, z1, g1 = ops1.at[0], ops1.at[1], ops1.at[2], ops1.at[4]
-    f1[1] = behind[H1]
-    f1[N1 - 2] = ahead[H1]
+    f1[1] = behind[10 + H1]
+    f1[N1 - 2] = ahead[10 + H1]
     spread = (row == (col - 32 + 128) // 2 - 64 + 16).astype(F32)
     coarse = dot(src[7:17].reshape(10 * NZ, 128), spread).reshape(10, NZ, 128)
     for q in range(N1):
         if q < H1:
-            value = behind[q]
+            value = behind[10 + q]
         elif q < H1 + 8:
             value = joined1[q - H1]
         else:
-            value = ahead[q - H1 - 8]
+            value = ahead[10 + q - H1 - 8]
         va1[q] = value + jnp.where(g1[q] > 0.0, coarse[q // 2], 0.0)
     src, dst = va1, vb1
     for s in range(NU):
         sweep(src, dst, f1, g1, x1, y1, z1, 1 + s, N1 - 1 - s, 32)
         src, dst = dst, src
 
-    copies[12].wait()
+    copies[10].wait()
     v0, f0, g0, x0, y0, z0 = (keep0.at[a] for a in range(6))
     col = lax.broadcasted_iota(jnp.int32, (128, 256), 1)
     row = lax.broadcasted_iota(jnp.int32, (128, 256), 0)
@@ -563,11 +568,12 @@
     to_right, to_left = call(edge_kernel, (own, behind, ahead), [(4, GROUPS, *side)] * 2)
     from_left = shift(to_right, "gy", 1)
     from_right = shift(to_left, "gy", -1)
-    keep0, ops1, f1, own1, edge_f1, to_right2, to_left2 = call(
+    keep0, ops1, f1, own1, edge_f1, to_right2, to_left2, own3 = call(
         down_kernel,
         (own, behind, ahead, from_left, from_right),
         [(6, 24, NZ, 256), (5, N1, *side), (N1, *side), (8, *side), (2, *side)]
-        + [(12, *side)] * 2,
+        + [(11, *side)] * 2
+        + [side],
         [(4, N0, NZ, 256)]
         + [wide] * 9
         + [(4, N1, NZ, 256), (5, N1, *side)]
@@ -578,47 +584,51 @@
         limit=44,
         apart_outs=(0, 1, 2),
     )
-    left2, right2 = shift(to_right2, "gy", 1), shift(to_left2, "gy", -1)
+    all3 = lax.all_gather(own3, "gx")
+    left, right = shift(to_right2, "gy", 1), shift(to_left2, "gy", -1)
     joined2, joined1, to_right, to_left = call(
         join_kernel,
-        (to_right2, own1, edge_f1, left2, right2),
+        (to_right2, own1, edge_f1, left, right),
         [(10, *side), (8, *side)] + [(11 + H1, *side)] * 2,
     )
-    all2 = lax.all_gather(joined2, "gx")
     behind, ahead = shift(to_right, "gx", 1), shift(to_left, "gx", -1)
-    to_right, to_left = call(
-        middle_kernel,
-        (behind, joined2, ahead, left2, right2),
-        [(40, 128)] * 2,
+    message, further, nearer = call(
+        functools.partial(middle_kernel, count),
+        (behind, joined2, ahead, all3),
+        [(count + 1, *side)] + [(10, *side)] * 2,
         [(12, *side)] * 8,
     )
-    left, right = shift(to_right, "gy", 1), shift(to_left, "gy", -1)
+    left, right = shift(message, "gy", 1), shift(message, "gy", -1)
+    behind2, ahead2 = shift(further, "gx", 1), shift(nearer, "gx", -1)
     left_far, right_far = shift(left, "gy", 1), shift(right, "gy", -1)
-    (rhs3,) = call(
+    near = (message, left, right, left_far, right_far)
+    rhs3, further, nearer = call(
         functools.partial(near_kernel, count),
-        (to_right2, to_right, left2, right2, left, right, left_far, right_far),
-        [(count, 5, 40, 128)],
+        (*near, behind2, ahead2),
+        [(count, 5, 8, 128), (5, *side), (5, *side)],
     )
     rhs3 = lax.all_to_all(rhs3, "gx", 0, 0)
+    behind3, ahead3 = shift(further, "gx", 1), shift(nearer, "gx", -1)
     rows3 = 2 * count + 2 * PAD3
     (e3,) = call(
         functools.partial(solve_kernel, count),
-        (rhs3,),
+        (rhs3, *near),
         [(10, *side)],
         [(4, rows3, *side)] + [(rows3, *side)] * 3,
     )
     (out,) = call(
         up_kernel,
-        (e3, all2, behind, ahead, joined1, f1, ops1, keep0),
+        (e3, behind3, behind2, behind, joined2, ahead, ahead2, ahead3, joined1, f1, ops1, keep0),
         [(NZ, R0, 128)],
         [(24, *side)] * 8
         + [(N1, *side)] * 3
         + [(24, NZ, 256)] * 2
-        + [(7, 10, *side), (1 + H1, *side), (1 + H1, *side), (8, *side)]
+        + [(5, *side), (10, *side), (11 + H1, *side), (10, *side)]
+        + [(11 + H1, *side), (10, *side), (5, *side), (8, *side)]
         + [(5, N1, *side), (6, 24, NZ, 256)]
-        + [pltpu.SemaphoreType.DMA((13,))],
+        + [pltpu.SemaphoreType.DMA((11,))],
         limit=58,
-        apart=range(1, 8),
+        apart=range(1, 12),
     )
     return out
 

time: 172 us -> 163 us (0.948)
  the two profiles are of different devices: /device:TPU:97 before, /device:TPU:130 now
where the time goes in v3:
time: 163 us; the launch traced here: 160 us
  starting transfers between devices  64.6 us (40%)
  Pallas kernels  33.8 us (21%)
  waiting for transfers between devices  33 us (20%)
  blocking collectives  22.9 us (14%)
  local copies, waits for them, and re-layouts  4.96 us (3%)
    ppermute x16, starting transfers between devices, shift(): return lax.ppermute(value, axis, route)  57.3 us
    pallas_call x8, Pallas kernels, call(): pl.pallas_call(kernel, out_shape=[jax.ShapeDtypeStruct(s, F32) for s in o...  33.8 us
    ppermute x16, waiting for transfers between devices, shift(): return lax.ppermute(value, axis, route)  33 us
    all_gather x1, blocking collectives, body(): all3 = lax.all_gather(own3, 'gx')  22.9 us
    all_to_all x1, starting transfers between devices, body(): rhs3 = lax.all_to_all(rhs3, 'gx', 0, 0)  7.34 us
    unnamed x26, local copies, waits for them, and re-layouts  4.96 us
  transfers between devices with their start and end apart: 17, of which 8 were waited for; matrix products, arithmetic and copies ran while one was open for 0% of the time, Pallas kernels for 6%

profile of v3, /device:TPU:130, one launch (start us, length us, event | category | flops | bytes accessed | tf_op | source)
XLA Modules:
  0.0 159.8 jit_solution(2110701908169603198)
XLA Ops:
  0.0 2.9 %shard_map.46 = (f32[4,16,32,128]{3,2,1,0:T(8,128)}, f32[50,32,128]{2,1,0:T(8,128)}, f32[49,32,128]{2,1,0:T(8,128)}) custom-call(s32[32,16,128]{2,1,0:T(8,128)} %in0.1, bf16[32,16,128]{2,1,0:T(8,128)(2,1)} %in1.1, bf16[32,16,128]{2,1,0:T(8,128)(2,1)} %in2.1, bf16[32,16,128]{2,1,0:T(8,128)(2,1)} %in3.1), custom_call_target="tpu_custom_call" | custom-call | tf_op jit(solution)/shard_map/pallas_call | solution.py:33
  2.9 3.5 %collective-permute-start = (f32[50,32,128]{2,1,0:T(8,128)}, f32[50,32,128]{2,1,0:T(8,128)S(1)}, u32[]{:S(2)}, u32[]{:S(2)}) collective-permute-start(f32[50,32,128]{2,1,0:T(8,128)} %get-tuple-element.29), channel_id=1, source_target_pairs={{0,16},{16,32},{32,48},{48,64},{64,80},{80,96},{96,112},{112,128},... | collective-permute-start | bytes 2457608 | tf_op jit(solution)/shard_map/ppermute | solution.py:549
  6.4 4.5 %collective-permute-start.1 = (f32[49,32,128]{2,1,0:T(8,128)}, f32[49,32,128]{2,1,0:T(8,128)S(1)}, u32[]{:S(2)}, u32[]{:S(2)}) collective-permute-start(f32[49,32,128]{2,1,0:T(8,128)} %get-tuple-element.30), channel_id=1, source_target_pairs={{16,0},{32,16},{48,32},{64,48},{80,64},{96,80},{112,96},{128,112},... | collective-permute-start | bytes 2408456 | tf_op jit(solution)/shard_map/ppermute | solution.py:549
  10.9 17.2 %collective-permute-done.1.ahead = f32[49,32,128]{2,1,0:T(8,128)S(1)} collective-permute-done((f32[49,32,128]{2,1,0:T(8,128)}, f32[49,32,128]{2,1,0:T(8,128)S(1)}, u32[]{:S(2)}, u32[]{:S(2)}) %collective-permute-start.1) | collective-permute-done | bytes 802848 | tf_op jit(solution)/shard_map/ppermute | solution.py:549
  28.0 1.2 copy-done
  29.9 1.9 %collective-permute-start.2 = (f32[4,6,32,128]{3,2,1,0:T(8,128)S(1)}, f32[4,6,32,128]{3,2,1,0:T(8,128)S(1)}, u32[]{:S(2)}, u32[]{:S(2)}) collective-permute-start(f32[4,6,32,128]{3,2,1,0:T(8,128)S(1)} %get-tuple-element.31), channel_id=1, source_target_pairs={{0,1},{1,2},{2,3},{3,4},{4,5},{5,6},{6,7},{7,8},{8,9},{9,10},{10,1... | collective-permute-start | bytes 1179656 | tf_op jit(solution)/shard_map/ppermute | solution.py:549
  31.8 4.9 %collective-permute-start.3 = (f32[4,6,32,128]{3,2,1,0:T(8,128)S(1)}, f32[4,6,32,128]{3,2,1,0:T(8,128)S(1)}, u32[]{:S(2)}, u32[]{:S(2)}) collective-permute-start(f32[4,6,32,128]{3,2,1,0:T(8,128)S(1)} %get-tuple-element.32), channel_id=1, source_target_pairs={{1,0},{2,1},{3,2},{4,3},{5,4},{6,5},{7,6},{8,7},{9,8},{10,9},{11,1... | collective-permute-start | bytes 1179656 | tf_op jit(solution)/shard_map/ppermute | solution.py:549
  36.7 3.5 %collective-permute-done.2.from_left = f32[4,6,32,128]{3,2,1,0:T(8,128)S(1)} collective-permute-done((f32[4,6,32,128]{3,2,1,0:T(8,128)S(1)}, f32[4,6,32,128]{3,2,1,0:T(8,128)S(1)}, u32[]{:S(2)}, u32[]{:S(2)}) %collective-permute-start.2) | collective-permute-done | bytes 393248 | tf_op jit(solution)/shard_map/ppermute | solution.py:549
  40.2 1.8 %collective-permute-done.3.from_right = f32[4,6,32,128]{3,2,1,0:T(8,128)S(1)} collective-permute-done((f32[4,6,32,128]{3,2,1,0:T(8,128)S(1)}, f32[4,6,32,128]{3,2,1,0:T(8,128)S(1)}, u32[]{:S(2)}, u32[]{:S(2)}) %collective-permute-start.3) | collective-permute-done | bytes 393248 | tf_op jit(solution)/shard_map/ppermute | solution.py:549
  42.0 1.2 copy-done.1
  43.2 11.1 %shard_map.48 = (f32[6,24,32,256]{3,2,1,0:T(8,128)}, f32[5,20,32,128]{3,2,1,0:T(8,128)S(1)}, f32[20,32,128]{2,1,0:T(8,128)S(1)}, f32[8,32,128]{2,1,0:T(8,128)S(1...) custom-call(f32[4,16,32,128]{3,2,1,0:T(8,128)S(1)} %copy-done.1, ...), custom_call_target="tpu_custom_call" | custom-call | tf_op jit(solution)/shard_map/pallas_call | solution.py:33
  54.3 1.2 copy-done.2
  55.6 5.0 %collective-permute-start.5 = (f32[11,32,128]{2,1,0:T(8,128)S(1)}, f32[11,32,128]{2,1,0:T(8,128)S(1)}, u32[]{:S(2)}, u32[]{:S(2)}) collective-permute-start(f32[11,32,128]{2,1,0:T(8,128)S(1)} %get-tuple-element.36), channel_id=1, source_target_pairs={{1,0},{2,1},{3,2},{4,3},{5,4},{6,5},{7,6},{8,7},{9,8},{10,9},{11,1... | collective-permute-start | bytes 540680 | tf_op jit(solution)/shard_map/ppermute | solution.py:549
  60.6 1.9 %collective-permute-start.4 = (f32[11,32,128]{2,1,0:T(8,128)S(1)}, f32[11,32,128]{2,1,0:T(8,128)S(1)}, u32[]{:S(2)}, u32[]{:S(2)}) collective-permute-start(f32[11,32,128]{2,1,0:T(8,128)S(1)} %get-tuple-element.33.own2), channel_id=1, source_target_pairs={{0,1},{1,2},{2,3},{3,4},{4,5},{5,6},{6,7},{7,8},{8,9},{9,10},{10,1... | collective-permute-start | bytes 540680 | tf_op jit(solution)/shard_map/ppermute | solution.py:549
  63.6 5.0 %collective-permute-done.4.left = f32[11,32,128]{2,1,0:T(8,128)S(1)} collective-permute-done((f32[11,32,128]{2,1,0:T(8,128)S(1)}, f32[11,32,128]{2,1,0:T(8,128)S(1)}, u32[]{:S(2)}, u32[]{:S(2)}) %collective-permute-start.4) | collective-permute-done | bytes 180256 | tf_op jit(solution)/shard_map/ppermute | solution.py:549
  68.8 3.3 %collective-permute-start.6 = (f32[17,32,128]{2,1,0:T(8,128)S(1)}, f32[17,32,128]{2,1,0:T(8,128)S(1)}, u32[]{:S(2)}, u32[]{:S(2)}) collective-permute-start(f32[17,32,128]{2,1,0:T(8,128)S(1)} %get-tuple-element.37), channel_id=1, source_target_pairs={{0,16},{16,32},{32,48},{48,64},{64,80},{80,96},{96,112},{112,128},... | collective-permute-start | bytes 835592 | tf_op jit(solution)/shard_map/ppermute | solution.py:549
  72.2 5.0 %collective-permute-start.7 = (f32[17,32,128]{2,1,0:T(8,128)S(1)}, f32[17,32,128]{2,1,0:T(8,128)S(1)}, u32[]{:S(2)}, u32[]{:S(2)}) collective-permute-start(f32[17,32,128]{2,1,0:T(8,128)S(1)} %get-tuple-element.39), channel_id=1, source_target_pairs={{16,0},{32,16},{48,32},{64,48},{80,64},{96,80},{112,96},{128,112},... | collective-permute-start | bytes 835592 | tf_op jit(solution)/shard_map/ppermute | solution.py:549
  77.2 22.9 %all-gather = f32[512,128]{1,0:T(8,128)S(1)} all-gather(f32[32,128]{1,0:T(8,128)S(1)} %get-tuple-element.40), channel_id=2, replica_groups=mesh['gx'=16,'gy'=16] {'gx'}, dimensions={0}, use_global_device_ids=true | all-gather | bytes 278528 | tf_op jit(solution)/shard_map/all_gather | solution.py:587
  100.8 1.9 %collective-permute-start.9 = (f32[17,32,128]{2,1,0:T(8,128)S(1)}, f32[17,32,128]{2,1,0:T(8,128)S(1)}, u32[]{:S(2)}, u32[]{:S(2)}) collective-permute-start(f32[17,32,128]{2,1,0:T(8,128)S(1)} %get-tuple-element.41.own), channel_id=1, source_target_pairs={{1,0},{2,1},{3,2},{4,3},{5,4},{6,5},{7,6},{8,7},{9,8},{10,9},{11,1... | collective-permute-start | bytes 835592 | tf_op jit(solution)/shard_map/ppermute | solution.py:549
  102.7 2.4 %collective-permute-start.8 = (f32[17,32,128]{2,1,0:T(8,128)S(1)}, f32[17,32,128]{2,1,0:T(8,128)S(1)}, u32[]{:S(2)}, u32[]{:S(2)}) collective-permute-start(f32[17,32,128]{2,1,0:T(8,128)S(1)} %get-tuple-element.41.own), channel_id=1, source_target_pairs={{0,1},{1,2},{2,3},{3,4},{4,5},{5,6},{6,7},{7,8},{8,9},{9,10},{10,1... | collective-permute-start | bytes 835592 | tf_op jit(solution)/shard_map/ppermute | solution.py:549
  105.2 1.6 %collective-permute-done.9.right = f32[17,32,128]{2,1,0:T(8,128)S(1)} collective-permute-done((f32[17,32,128]{2,1,0:T(8,128)S(1)}, f32[17,32,128]{2,1,0:T(8,128)S(1)}, u32[]{:S(2)}, u32[]{:S(2)}) %collective-permute-start.9) | collective-permute-done | bytes 278560 | tf_op jit(solution)/shard_map/ppermute | solution.py:549
  106.8 5.0 %collective-permute-start.11 = (f32[17,32,128]{2,1,0:T(8,128)S(1)}, f32[17,32,128]{2,1,0:T(8,128)S(1)}, u32[]{:S(2)}, u32[]{:S(2)}) collective-permute-start(f32[17,32,128]{2,1,0:T(8,128)S(1)} %collective-permute-done.9.right), channel_id=1, source_target_pairs={{1,0},{2,1},{3,2},{4,3},{5,4},{6,5},{7,6},{8,7},{9,8},{10,9},{11,1... | collective-permute-start | bytes 835592 | tf_op jit(solution)/shard_map/ppermute | solution.py:549
  111.8 1.9 %collective-permute-start.10 = (f32[17,32,128]{2,1,0:T(8,128)S(1)}, f32[17,32,128]{2,1,0:T(8,128)S(1)}, u32[]{:S(2)}, u32[]{:S(2)}) collective-permute-start(f32[17,32,128]{2,1,0:T(8,128)S(1)} %collective-permute-done.8.left), channel_id=1, source_target_pairs={{0,1},{1,2},{2,3},{3,4},{4,5},{5,6},{6,7},{7,8},{8,9},{9,10},{10,1... | collective-permute-start | bytes 835592 | tf_op jit(solution)/shard_map/ppermute | solution.py:549
  113.7 1.9 %collective-permute-start.12 = (f32[10,32,128]{2,1,0:T(8,128)S(1)}, f32[10,32,128]{2,1,0:T(8,128)S(1)}, u32[]{:S(2)}, u32[]{:S(2)}) collective-permute-start(f32[10,32,128]{2,1,0:T(8,128)S(1)} %get-tuple-element.42), channel_id=1, source_target_pairs={{0,16},{16,32},{32,48},{48,64},{64,80},{80,96},{96,112},{112,128},... | collective-permute-start | bytes 491528 | tf_op jit(solution)/shard_map/ppermute | solution.py:549
  115.7 6.0 %collective-permute-start.13 = (f32[10,32,128]{2,1,0:T(8,128)S(1)}, f32[10,32,128]{2,1,0:T(8,128)S(1)}, u32[]{:S(2)}, u32[]{:S(2)}) collective-permute-start(f32[10,32,128]{2,1,0:T(8,128)S(1)} %get-tuple-element.43), channel_id=1, source_target_pairs={{16,0},{32,16},{48,32},{64,48},{80,64},{96,80},{112,96},{128,112},... | collective-permute-start | bytes 491528 | tf_op jit(solution)/shard_map/ppermute | solution.py:549
  121.7 1.4 collective-permute-done.12.behind2.in_behind2
  123.1 1.4 collective-permute-done.13.ahead2.in_ahead2
  125.3 7.3 %all-to-all-start = ((f32[16,5,8,128]{3,2,1,0:T(8,128)}), f32[16,5,8,128]{3,2,1,0:T(8,128)S(1)}, u32[]{:S(2)}, u32[]{:S(2)}) async-start(f32[16,5,8,128]{3,2,1,0:T(8,128)} %get-tuple-element.44), calls=%async_computation | async-start | bytes 655360 | tf_op jit(solution)/shard_map/all_to_all | solution.py:610
  132.7 3.4 %collective-permute-start.14 = (f32[5,32,128]{2,1,0:T(8,128)S(1)}, f32[5,32,128]{2,1,0:T(8,128)S(1)}, u32[]{:S(2)}, u32[]{:S(2)}) collective-permute-start(f32[5,32,128]{2,1,0:T(8,128)S(1)} %get-tuple-element.45), channel_id=1, source_target_pairs={{0,16},{16,32},{32,48},{48,64},{64,80},{80,96},{96,112},{112,128},... | collective-permute-start | bytes 245768 | tf_op jit(solution)/shard_map/ppermute | solution.py:549
  136.0 4.8 %collective-permute-start.15 = (f32[5,32,128]{2,1,0:T(8,128)S(1)}, f32[5,32,128]{2,1,0:T(8,128)S(1)}, u32[]{:S(2)}, u32[]{:S(2)}) collective-permute-start(f32[5,32,128]{2,1,0:T(8,128)S(1)} %get-tuple-element.46), channel_id=1, source_target_pairs={{16,0},{32,16},{48,32},{64,48},{80,64},{96,80},{112,96},{128,112},... | collective-permute-start | bytes 245768 | tf_op jit(solution)/shard_map/ppermute | solution.py:549
  140.8 10.1 %shard_map.52.e3 = f32[10,32,128]{2,1,0:T(8,128)S(1)} custom-call(f32[16,5,8,128]{3,2,1,0:T(8,128)S(1)} %all-to-all-done.gathered, f32[17,32,128]{2,1,0:T(8,128)S(1)} %get-tuple-element.41.own, f32[17,32,128]{2,1,0:T(8,128)S(1)} %collective-permute-done.8.left, f32[17,32,128]{2,1,0:T(8,128)S(1)} %collective-permute-done.9.right, ...), custom_call_target="tpu_custom_call" | custom-call | tf_op jit(solution)/shard_map/pallas_call | solution.py:33
  152.3 7.4 %shard_map.53 = f32[32,16,128]{2,1,0:T(8,128)} custom-call(f32[10,32,128]{2,1,0:T(8,128)} %copy-done.5, f32[5,32,128]{2,1,0:T(8,128)} %copy-done.11, f32[10,32,128]{2,1,0:T(8,128)} %copy-done.7, f32[17,32,128]{2,1,0:T(8,128)} %copy-done.3, f32[10,32,128]{2,1,0:T(8,128)} %copy-done.6, f32[17,32,128]{2,1,0:T(8,128)} %copy-done.4, f32[10,32,128]{2,1,0:T(8,128)} %copy-done.8, ...), custom_call_target="tpu_custom_call" | custom-call | tf_op jit(solution)/shard_map/pallas_call | solution.py:33
  (37 shorter events, 4.7 us)
Async XLA Ops:
  2.9 25.1 %collective-permute-start = (f32[50,32,128]{2,1,0:T(8,128)}, f32[50,32,128]{2,1,0:T(8,128)S(1)}, u32[]{:S(2)}, u32[]{:S(2)}) collective-permute-start(f32[50,32,128]{2,1,0:T(8,128)} %get-tuple-element.29), channel_id=1, source_target_pairs={{0,16},{16,32},{32,48},{48,64},{64,80},{80,96},{96,112},{112,128},... | collective-permute-start | bytes 2457608 | tf_op jit(solution)/shard_map/ppermute | solution.py:549
  6.4 21.6 %collective-permute-start.1 = (f32[49,32,128]{2,1,0:T(8,128)}, f32[49,32,128]{2,1,0:T(8,128)S(1)}, u32[]{:S(2)}, u32[]{:S(2)}) collective-permute-start(f32[49,32,128]{2,1,0:T(8,128)} %get-tuple-element.30), channel_id=1, source_target_pairs={{16,0},{32,16},{48,32},{64,48},{80,64},{96,80},{112,96},{128,112},... | collective-permute-start | bytes 2408456 | tf_op jit(solution)/shard_map/ppermute | solution.py:549
  28.0 1.2 copy-start
  29.9 10.3 %collective-permute-start.2 = (f32[4,6,32,128]{3,2,1,0:T(8,128)S(1)}, f32[4,6,32,128]{3,2,1,0:T(8,128)S(1)}, u32[]{:S(2)}, u32[]{:S(2)}) collective-permute-start(f32[4,6,32,128]{3,2,1,0:T(8,128)S(1)} %get-tuple-element.31), channel_id=1, source_target_pairs={{0,1},{1,2},{2,3},{3,4},{4,5},{5,6},{6,7},{7,8},{8,9},{9,10},{10,1... | collective-permute-start | bytes 1179656 | tf_op jit(solution)/shard_map/ppermute | solution.py:549
  31.8 10.1 %collective-permute-start.3 = (f32[4,6,32,128]{3,2,1,0:T(8,128)S(1)}, f32[4,6,32,128]{3,2,1,0:T(8,128)S(1)}, u32[]{:S(2)}, u32[]{:S(2)}) collective-permute-start(f32[4,6,32,128]{3,2,1,0:T(8,128)S(1)} %get-tuple-element.32), channel_id=1, source_target_pairs={{1,0},{2,1},{3,2},{4,3},{5,4},{6,5},{7,6},{8,7},{9,8},{10,9},{11,1... | collective-permute-start | bytes 1179656 | tf_op jit(solution)/shard_map/ppermute | solution.py:549
  42.0 1.2 copy-start.1
  54.3 1.2 copy-start.2
  55.6 69.0 %copy-start.9 = (f32[20,32,128]{2,1,0:T(8,128)}, f32[20,32,128]{2,1,0:T(8,128)S(1)}, u32[]{:S(2)}) copy-start(f32[20,32,128]{2,1,0:T(8,128)S(1)} %get-tuple-element.48.in_f1) | copy-start | bytes 983044
  55.6 8.0 %collective-permute-start.5 = (f32[11,32,128]{2,1,0:T(8,128)S(1)}, f32[11,32,128]{2,1,0:T(8,128)S(1)}, u32[]{:S(2)}, u32[]{:S(2)}) collective-permute-start(f32[11,32,128]{2,1,0:T(8,128)S(1)} %get-tuple-element.36), channel_id=1, source_target_pairs={{1,0},{2,1},{3,2},{4,3},{5,4},{6,5},{7,6},{8,7},{9,8},{10,9},{11,1... | collective-permute-start | bytes 540680 | tf_op jit(solution)/shard_map/ppermute | solution.py:549
  60.6 8.0 %collective-permute-start.4 = (f32[11,32,128]{2,1,0:T(8,128)S(1)}, f32[11,32,128]{2,1,0:T(8,128)S(1)}, u32[]{:S(2)}, u32[]{:S(2)}) collective-permute-start(f32[11,32,128]{2,1,0:T(8,128)S(1)} %get-tuple-element.33.own2), channel_id=1, source_target_pairs={{0,1},{1,2},{2,3},{3,4},{4,5},{5,6},{6,7},{7,8},{8,9},{9,10},{10,1... | collective-permute-start | bytes 540680 | tf_op jit(solution)/shard_map/ppermute | solution.py:549
  68.8 56.5 %copy-start.10 = (f32[8,32,128]{2,1,0:T(8,128)}, f32[8,32,128]{2,1,0:T(8,128)S(1)}, u32[]{:S(2)}) copy-start(f32[8,32,128]{2,1,0:T(8,128)S(1)} %get-tuple-element.47.in_joined1) | copy-start | bytes 393220
  68.8 82.8 %copy-start.6 = (f32[10,32,128]{2,1,0:T(8,128)}, f32[10,32,128]{2,1,0:T(8,128)S(1)}, u32[]{:S(2)}) copy-start(f32[10,32,128]{2,1,0:T(8,128)S(1)} %get-tuple-element.38.own.in_own) | copy-start | bytes 491524
  68.8 31.3 %collective-permute-start.6 = (f32[17,32,128]{2,1,0:T(8,128)S(1)}, f32[17,32,128]{2,1,0:T(8,128)S(1)}, u32[]{:S(2)}, u32[]{:S(2)}) collective-permute-start(f32[17,32,128]{2,1,0:T(8,128)S(1)} %get-tuple-element.37), channel_id=1, source_target_pairs={{0,16},{16,32},{32,48},{48,64},{64,80},{80,96},{96,112},{112,128},... | collective-permute-start | bytes 835592 | tf_op jit(solution)/shard_map/ppermute | solution.py:549
  72.2 28.0 %collective-permute-start.7 = (f32[17,32,128]{2,1,0:T(8,128)S(1)}, f32[17,32,128]{2,1,0:T(8,128)S(1)}, u32[]{:S(2)}, u32[]{:S(2)}) collective-permute-start(f32[17,32,128]{2,1,0:T(8,128)S(1)} %get-tuple-element.39), channel_id=1, source_target_pairs={{16,0},{32,16},{48,32},{64,48},{80,64},{96,80},{112,96},{128,112},... | collective-permute-start | bytes 835592 | tf_op jit(solution)/shard_map/ppermute | solution.py:549
  100.1 51.5 %copy-start.3 = (f32[17,32,128]{2,1,0:T(8,128)}, f32[17,32,128]{2,1,0:T(8,128)S(1)}, u32[]{:S(2)}) copy-start(f32[17,32,128]{2,1,0:T(8,128)S(1)} %collective-permute-done.6.behind.in_behind) | copy-start | bytes 835588
  100.1 51.5 %copy-start.4 = (f32[17,32,128]{2,1,0:T(8,128)}, f32[17,32,128]{2,1,0:T(8,128)S(1)}, u32[]{:S(2)}) copy-start(f32[17,32,128]{2,1,0:T(8,128)S(1)} %collective-permute-done.7.ahead.in_ahead) | copy-start | bytes 835588
  100.8 6.0 %collective-permute-start.9 = (f32[17,32,128]{2,1,0:T(8,128)S(1)}, f32[17,32,128]{2,1,0:T(8,128)S(1)}, u32[]{:S(2)}, u32[]{:S(2)}) collective-permute-start(f32[17,32,128]{2,1,0:T(8,128)S(1)} %get-tuple-element.41.own), channel_id=1, source_target_pairs={{1,0},{2,1},{3,2},{4,3},{5,4},{6,5},{7,6},{8,7},{9,8},{10,9},{11,1... | collective-permute-start | bytes 835592 | tf_op jit(solution)/shard_map/ppermute | solution.py:549
  102.7 9.1 %collective-permute-start.8 = (f32[17,32,128]{2,1,0:T(8,128)S(1)}, f32[17,32,128]{2,1,0:T(8,128)S(1)}, u32[]{:S(2)}, u32[]{:S(2)}) collective-permute-start(f32[17,32,128]{2,1,0:T(8,128)S(1)} %get-tuple-element.41.own), channel_id=1, source_target_pairs={{0,1},{1,2},{2,3},{3,4},{4,5},{5,6},{6,7},{7,8},{8,9},{9,10},{10,1... | collective-permute-start | bytes 835592 | tf_op jit(solution)/shard_map/ppermute | solution.py:549
  106.8 17.7 %collective-permute-start.11 = (f32[17,32,128]{2,1,0:T(8,128)S(1)}, f32[17,32,128]{2,1,0:T(8,128)S(1)}, u32[]{:S(2)}, u32[]{:S(2)}) collective-permute-start(f32[17,32,128]{2,1,0:T(8,128)S(1)} %collective-permute-done.9.right), channel_id=1, source_target_pairs={{1,0},{2,1},{3,2},{4,3},{5,4},{6,5},{7,6},{8,7},{9,8},{10,9},{11,1... | collective-permute-start | bytes 835592 | tf_op jit(solution)/shard_map/ppermute | solution.py:549
  111.8 12.7 %collective-permute-start.10 = (f32[17,32,128]{2,1,0:T(8,128)S(1)}, f32[17,32,128]{2,1,0:T(8,128)S(1)}, u32[]{:S(2)}, u32[]{:S(2)}) collective-permute-start(f32[17,32,128]{2,1,0:T(8,128)S(1)} %collective-permute-done.8.left), channel_id=1, source_target_pairs={{0,1},{1,2},{2,3},{3,4},{4,5},{5,6},{6,7},{7,8},{8,9},{9,10},{10,1... | collective-permute-start | bytes 835592 | tf_op jit(solution)/shard_map/ppermute | solution.py:549
  113.7 9.4 %collective-permute-start.12 = (f32[10,32,128]{2,1,0:T(8,128)S(1)}, f32[10,32,128]{2,1,0:T(8,128)S(1)}, u32[]{:S(2)}, u32[]{:S(2)}) collective-permute-start(f32[10,32,128]{2,1,0:T(8,128)S(1)} %get-tuple-element.42), channel_id=1, source_target_pairs={{0,16},{16,32},{32,48},{48,64},{64,80},{80,96},{96,112},{112,128},... | collective-permute-start | bytes 491528 | tf_op jit(solution)/shard_map/ppermute | solution.py:549
  115.7 8.9 %collective-permute-start.13 = (f32[10,32,128]{2,1,0:T(8,128)S(1)}, f32[10,32,128]{2,1,0:T(8,128)S(1)}, u32[]{:S(2)}, u32[]{:S(2)}) collective-permute-start(f32[10,32,128]{2,1,0:T(8,128)S(1)} %get-tuple-element.43), channel_id=1, source_target_pairs={{16,0},{32,16},{48,32},{64,48},{80,64},{96,80},{112,96},{128,112},... | collective-permute-start | bytes 491528 | tf_op jit(solution)/shard_map/ppermute | solution.py:549
  123.1 28.5 %copy-start.7 = (f32[10,32,128]{2,1,0:T(8,128)}, f32[10,32,128]{2,1,0:T(8,128)S(1)}, u32[]{:S(2)}) copy-start(f32[10,32,128]{2,1,0:T(8,128)S(1)} %collective-permute-done.12.behind2.in_behind2) | copy-start | bytes 491524
  124.5 27.1 %copy-start.8 = (f32[10,32,128]{2,1,0:T(8,128)}, f32[10,32,128]{2,1,0:T(8,128)S(1)}, u32[]{:S(2)}) copy-start(f32[10,32,128]{2,1,0:T(8,128)S(1)} %collective-permute-done.13.ahead2.in_ahead2) | copy-start | bytes 491524
  125.3 15.5 %all-to-all-start = ((f32[16,5,8,128]{3,2,1,0:T(8,128)}), f32[16,5,8,128]{3,2,1,0:T(8,128)S(1)}, u32[]{:S(2)}, u32[]{:S(2)}) async-start(f32[16,5,8,128]{3,2,1,0:T(8,128)} %get-tuple-element.44), calls=%async_computation | async-start | bytes 655360 | tf_op jit(solution)/shard_map/all_to_all | solution.py:610
  132.7 18.9 %collective-permute-start.14 = (f32[5,32,128]{2,1,0:T(8,128)S(1)}, f32[5,32,128]{2,1,0:T(8,128)S(1)}, u32[]{:S(2)}, u32[]{:S(2)}) collective-permute-start(f32[5,32,128]{2,1,0:T(8,128)S(1)} %get-tuple-element.45), channel_id=1, source_target_pairs={{0,16},{16,32},{32,48},{48,64},{64,80},{80,96},{96,112},{112,128},... | collective-permute-start | bytes 245768 | tf_op jit(solution)/shard_map/ppermute | solution.py:549
  136.0 15.6 %collective-permute-start.15 = (f32[5,32,128]{2,1,0:T(8,128)S(1)}, f32[5,32,128]{2,1,0:T(8,128)S(1)}, u32[]{:S(2)}, u32[]{:S(2)}) collective-permute-start(f32[5,32,128]{2,1,0:T(8,128)S(1)} %get-tuple-element.46), channel_id=1, source_target_pairs={{16,0},{32,16},{48,32},{64,48},{80,64},{96,80},{112,96},{128,112},... | collective-permute-start | bytes 245768 | tf_op jit(solution)/shard_map/ppermute | solution.py:549
  150.9 0.7 copy-start.5
  151.6 0.6 copy-start.11
  151.6 0.7 copy-start.12

commit v4 on v3

--- a/solution.py
+++ b/solution.py
@@ -26,7 +26,7 @@
     return pl.BlockSpec(memory_space=pltpu.VMEM)
 
 
-def call(kernel, ins, outs, scratch=(), limit=24, apart=(), apart_outs=()):
+def call(kernel, ins, outs, scratch=(), limit=10, apart=(), apart_outs=()):
     def places(count, left):
         return [pl.BlockSpec(memory_space=pl.ANY) if i in left else spec() for i in range(count)]
 
@@ -141,16 +141,12 @@
     return copies
 
 
-def stage_kernel(
-    in0, in1, in2, in3, own, to_right, to_left, labels, cond_x, cond_y, cond_z, sems
-):
-    copies = fetch(((in0, labels), (in1, cond_x), (in2, cond_y), (in3, cond_z)), sems)
+def stage_kernel(labels, cond_x, cond_y, cond_z, own, to_right, to_left):
     last_x = lax.axis_index("gx") == lax.axis_size("gx") - 1
     last_y = lax.axis_index("gy") == lax.axis_size("gy") - 1
     shape = (R0, 8, 128)
     row = lax.broadcasted_iota(jnp.int32, shape, 0)
     for a, ref in enumerate((labels, cond_x, cond_y, cond_z)):
-        copies[a].wait()
         for b in range(4):
             value = jnp.stack([ref[4 * s + b].astype(F32) for s in range(8)])
             value = jnp.swapaxes(value, 0, 1)
@@ -198,17 +194,26 @@
     ext, fx, fy, fz, d, g, f, va, vb, t, t1, ops1, d1, f1, va1, vb1, x2, y2, z2, e2, sems,
 ):
     lane = lanes((NZ, 128))
+    main, pairs = pl.ds(0, 128), []
     for a in range(4):
         skip, count = int(a > 1), H0 - (a > 0)
-        ext[a, skip:H0, :, 0:128] = behind[BEHIND[a] : BEHIND[a] + H0 - skip]
-        ext[a, H0 : H0 + R0, :, 0:128] = own[a]
-        ext[a, H0 + R0 : H0 + R0 + count, :, 0:128] = ahead[AHEAD[a] : AHEAD[a] + count]
+
+        def place(lo, size, a=a):
+            return ext.at[a, pl.ds(lo, size), :, main]
+
+        pairs.append((behind.at[pl.ds(BEHIND[a], H0 - skip)], place(skip, H0 - skip)))
+        pairs.append((own.at[a], place(H0, R0)))
+        pairs.append((ahead.at[pl.ds(AHEAD[a], count)], place(H0 + R0, count)))
+    copies = fetch(pairs, sems.at[pl.ds(8, 12)])
+    for a in range(4):
         for c in range(GROUPS):
             left, right = from_left[a, c], from_right[a, c]
             for k in range(8):
                 if 8 * c + k < N0:
                     both = jnp.where(lane // 16 == k, left, right)
                     ext[a, 8 * c + k, :, 128:256] = roll(both, -16 * k - 16, 1)
+    for copy in copies:
+        copy.wait()
 
     def cut(value, *kinds):
         for kind in kinds:
@@ -338,7 +343,8 @@
         for a, value in enumerate((x3[i + 1], y3[i], z3[i], d3)):
             spot = 32 * a + 16 * i
             total = jnp.where(lane // 16 == spot // 16, roll(value, spot - 8, 1), total)
-    own3[...] = total
+    for i in range(own3.shape[0]):
+        own3[i] = total
     for copy in copies:
         copy.wait()
 
@@ -557,11 +563,6 @@
         stage_kernel,
         (labels, conduct_x, conduct_y, conduct_z),
         [(4, R0, *side), (4 * H0 - 2, *side), (4 * H0 - 3, *side)],
-        [pltpu.VMEM(labels.shape, labels.dtype)]
-        + [pltpu.VMEM(labels.shape, conduct_x.dtype)] * 3
-        + [pltpu.SemaphoreType.DMA((4,))],
-        limit=58,
-        apart=(0, 1, 2, 3),
     )
     behind = shift(to_right, "gx", 1)
     ahead = shift(to_left, "gx", -1)
@@ -573,19 +574,20 @@
         (own, behind, ahead, from_left, from_right),
         [(6, 24, NZ, 256), (5, N1, *side), (N1, *side), (8, *side), (2, *side)]
         + [(11, *side)] * 2
-        + [side],
+        + [(count, *side)],
         [(4, N0, NZ, 256)]
         + [wide] * 9
         + [(4, N1, NZ, 256), (5, N1, *side)]
         + [(N1, *side)] * 4
         + [(5, *side)]
         + [(4, *side)] * 3
-        + [pltpu.SemaphoreType.DMA((8,))],
-        limit=44,
+        + [pltpu.SemaphoreType.DMA((20,))],
+        limit=28,
+        apart=(0, 1, 2),
         apart_outs=(0, 1, 2),
     )
-    all3 = lax.all_gather(own3, "gx")
     left, right = shift(to_right2, "gy", 1), shift(to_left2, "gy", -1)
+    all3 = lax.all_to_all(own3, "gx", 0, 0)
     joined2, joined1, to_right, to_left = call(
         join_kernel,
         (to_right2, own1, edge_f1, left, right),
@@ -627,7 +629,7 @@
         + [(11 + H1, *side), (10, *side), (5, *side), (8, *side)]
         + [(5, N1, *side), (6, 24, NZ, 256)]
         + [pltpu.SemaphoreType.DMA((11,))],
-        limit=58,
+        limit=18,
         apart=range(1, 12),
     )
     return out

time: 163 us -> 162 us (level)
  local copies, waits for them, and re-layouts: 4.96 us -> 17 us
  blocking collectives: 22.9 us -> 12.6 us
  Pallas kernels: 33.8 us -> 30.8 us
    all_gather x1 -> x0, blocking collectives: 22.9 us -> none  [body(): all3 = lax.all_gather(own3, 'gx')]
    all_to_all x0 -> x1, blocking collectives: none -> 12.6 us  [body(): all3 = lax.all_to_all(own3, 'gx', 0, 0)]
    unnamed x26 -> x42, local copies, waits for them, and re-layouts: 4.96 us -> 17 us
    pallas_call x8, Pallas kernels: 33.8 us -> 30.8 us  [call(): pl.pallas_call(kernel, out_shape=[jax.ShapeDtypeStruct(s, F32) for s in o...]
where the time goes in v4:
time: 162 us; the launch traced here: 159 us
  starting transfers between devices  65.6 us (40%)
  waiting for transfers between devices  32.7 us (20%)
  Pallas kernels  30.8 us (19%)
  local copies, waits for them, and re-layouts  17 us (10%)
  blocking collectives  12.6 us (8%)
    ppermute x16, starting transfers between devices, shift(): return lax.ppermute(value, axis, route)  57.4 us
    ppermute x16, waiting for transfers between devices, shift(): return lax.ppermute(value, axis, route)  32.7 us
    pallas_call x8, Pallas kernels, call(): pl.pallas_call(kernel, out_shape=[jax.ShapeDtypeStruct(s, F32) for s in o...  30.8 us
    unnamed x42, local copies, waits for them, and re-layouts  17 us
    all_to_all x1, blocking collectives, body(): all3 = lax.all_to_all(own3, 'gx', 0, 0)  12.6 us
    all_to_all x1, starting transfers between devices, body(): rhs3 = lax.all_to_all(rhs3, 'gx', 0, 0)  8.16 us
  transfers between devices with their start and end apart: 17, of which 8 were waited for; matrix products, arithmetic and copies ran while one was open for 0% of the time, Pallas kernels for 6%

profile of v4, /device:TPU:130, one launch (start us, length us, event | category | flops | bytes accessed | tf_op | source)
XLA Modules:
  0.0 159.2 jit_solution(4472235835704499919)
XLA Ops:
  4.0 3.5 %collective-permute-start = (f32[50,32,128]{2,1,0:T(8,128)S(1)}, f32[50,32,128]{2,1,0:T(8,128)S(1)}, u32[]{:S(2)}, u32[]{:S(2)}) collective-permute-start(f32[50,32,128]{2,1,0:T(8,128)S(1)} %get-tuple-element.29), channel_id=1, source_target_pairs={{0,16},{16,32},{32,48},{48,64},{64,80},{80,96},{96,112},{112,128},... | collective-permute-start | bytes 2457608 | tf_op jit(solution)/shard_map/ppermute | solution.py:555
  7.5 4.5 %collective-permute-start.1 = (f32[49,32,128]{2,1,0:T(8,128)S(1)}, f32[49,32,128]{2,1,0:T(8,128)S(1)}, u32[]{:S(2)}, u32[]{:S(2)}) collective-permute-start(f32[49,32,128]{2,1,0:T(8,128)S(1)} %get-tuple-element.30), channel_id=1, source_target_pairs={{16,0},{32,16},{48,32},{64,48},{80,64},{96,80},{112,96},{128,112},... | collective-permute-start | bytes 2408456 | tf_op jit(solution)/shard_map/ppermute | solution.py:555
  12.0 16.8 %collective-permute-done.1.ahead = f32[49,32,128]{2,1,0:T(8,128)S(1)} collective-permute-done((f32[49,32,128]{2,1,0:T(8,128)S(1)}, f32[49,32,128]{2,1,0:T(8,128)S(1)}, u32[]{:S(2)}, u32[]{:S(2)}) %collective-permute-start.1) | collective-permute-done | bytes 802848 | tf_op jit(solution)/shard_map/ppermute | solution.py:555
  29.5 1.9 %collective-permute-start.2 = (f32[4,6,32,128]{3,2,1,0:T(8,128)S(1)}, f32[4,6,32,128]{3,2,1,0:T(8,128)S(1)}, u32[]{:S(2)}, u32[]{:S(2)}) collective-permute-start(f32[4,6,32,128]{3,2,1,0:T(8,128)S(1)} %get-tuple-element.31), channel_id=1, source_target_pairs={{0,1},{1,2},{2,3},{3,4},{4,5},{5,6},{6,7},{7,8},{8,9},{9,10},{10,1... | collective-permute-start | bytes 1179656 | tf_op jit(solution)/shard_map/ppermute | solution.py:555
  31.5 4.9 %collective-permute-start.3 = (f32[4,6,32,128]{3,2,1,0:T(8,128)S(1)}, f32[4,6,32,128]{3,2,1,0:T(8,128)S(1)}, u32[]{:S(2)}, u32[]{:S(2)}) collective-permute-start(f32[4,6,32,128]{3,2,1,0:T(8,128)S(1)} %get-tuple-element.32), channel_id=1, source_target_pairs={{1,0},{2,1},{3,2},{4,3},{5,4},{6,5},{7,6},{8,7},{9,8},{10,9},{11,1... | collective-permute-start | bytes 1179656 | tf_op jit(solution)/shard_map/ppermute | solution.py:555
  36.3 3.5 %collective-permute-done.2.from_left = f32[4,6,32,128]{3,2,1,0:T(8,128)S(1)} collective-permute-done((f32[4,6,32,128]{3,2,1,0:T(8,128)S(1)}, f32[4,6,32,128]{3,2,1,0:T(8,128)S(1)}, u32[]{:S(2)}, u32[]{:S(2)}) %collective-permute-start.2) | collective-permute-done | bytes 393248 | tf_op jit(solution)/shard_map/ppermute | solution.py:555
  39.8 1.8 %collective-permute-done.3.from_right = f32[4,6,32,128]{3,2,1,0:T(8,128)S(1)} collective-permute-done((f32[4,6,32,128]{3,2,1,0:T(8,128)S(1)}, f32[4,6,32,128]{3,2,1,0:T(8,128)S(1)}, u32[]{:S(2)}, u32[]{:S(2)}) %collective-permute-start.3) | collective-permute-done | bytes 393248 | tf_op jit(solution)/shard_map/ppermute | solution.py:555
  41.6 11.7 %shard_map.48 = (f32[6,24,32,256]{3,2,1,0:T(8,128)S(1)}, f32[5,20,32,128]{3,2,1,0:T(8,128)S(1)}, f32[20,32,128]{2,1,0:T(8,128)S(1)}, f32[8,32,128]{2,1,0:T(8,128...) custom-call(f32[4,16,32,128]{3,2,1,0:T(8,128)S(1)} %get-tuple-elemen, ...), custom_call_target="tpu_custom_call" | custom-call | tf_op jit(solution)/shard_map/pallas_call | solution.py:33
  53.3 2.1 %copy-done = f32[6,24,32,256]{3,2,1,0:T(8,128)} copy-done((f32[6,24,32,256]{3,2,1,0:T(8,128)}, f32[6,24,32,256]{3,2,1,0:T(8,128)S(1)}, u32[]{:S(2)}) %copy-start) | copy-done | bytes 4718616
  55.5 5.0 %collective-permute-start.5 = (f32[11,32,128]{2,1,0:T(8,128)S(1)}, f32[11,32,128]{2,1,0:T(8,128)S(1)}, u32[]{:S(2)}, u32[]{:S(2)}) collective-permute-start(f32[11,32,128]{2,1,0:T(8,128)S(1)} %get-tuple-element.36), channel_id=1, source_target_pairs={{1,0},{2,1},{3,2},{4,3},{5,4},{6,5},{7,6},{8,7},{9,8},{10,9},{11,1... | collective-permute-start | bytes 540680 | tf_op jit(solution)/shard_map/ppermute | solution.py:555
  60.5 1.9 %collective-permute-start.4 = (f32[11,32,128]{2,1,0:T(8,128)S(1)}, f32[11,32,128]{2,1,0:T(8,128)S(1)}, u32[]{:S(2)}, u32[]{:S(2)}) collective-permute-start(f32[11,32,128]{2,1,0:T(8,128)S(1)} %get-tuple-element.33.own2), channel_id=1, source_target_pairs={{0,1},{1,2},{2,3},{3,4},{4,5},{5,6},{6,7},{7,8},{8,9},{9,10},{10,1... | collective-permute-start | bytes 540680 | tf_op jit(solution)/shard_map/ppermute | solution.py:555
  62.4 1.1 collective-permute-done.5.right
  63.5 5.0 %collective-permute-done.4.left = f32[11,32,128]{2,1,0:T(8,128)S(1)} collective-permute-done((f32[11,32,128]{2,1,0:T(8,128)S(1)}, f32[11,32,128]{2,1,0:T(8,128)S(1)}, u32[]{:S(2)}, u32[]{:S(2)}) %collective-permute-start.4) | collective-permute-done | bytes 180256 | tf_op jit(solution)/shard_map/ppermute | solution.py:555
  68.7 3.4 %collective-permute-start.6 = (f32[17,32,128]{2,1,0:T(8,128)S(1)}, f32[17,32,128]{2,1,0:T(8,128)S(1)}, u32[]{:S(2)}, u32[]{:S(2)}) collective-permute-start(f32[17,32,128]{2,1,0:T(8,128)S(1)} %get-tuple-element.37), channel_id=1, source_target_pairs={{0,16},{16,32},{32,48},{48,64},{64,80},{80,96},{96,112},{112,128},... | collective-permute-start | bytes 835592 | tf_op jit(solution)/shard_map/ppermute | solution.py:555
  72.2 5.0 %collective-permute-start.7 = (f32[17,32,128]{2,1,0:T(8,128)S(1)}, f32[17,32,128]{2,1,0:T(8,128)S(1)}, u32[]{:S(2)}, u32[]{:S(2)}) collective-permute-start(f32[17,32,128]{2,1,0:T(8,128)S(1)} %get-tuple-element.39), channel_id=1, source_target_pairs={{16,0},{32,16},{48,32},{64,48},{80,64},{96,80},{112,96},{128,112},... | collective-permute-start | bytes 835592 | tf_op jit(solution)/shard_map/ppermute | solution.py:555
  77.2 12.6 %all_to_all.10.ops3 = f32[16,32,128]{2,1,0:T(8,128)S(1)} all-to-all(f32[16,32,128]{2,1,0:T(8,128)S(1)} %get-tuple-element.40), channel_id=1, replica_groups=mesh['gx'=16,'gy'=16] {'gx'}, dimensions={0} | all-to-all | bytes 524288 | tf_op jit(solution)/shard_map/all_to_all | solution.py:590
  90.5 1.9 %collective-permute-start.9 = (f32[17,32,128]{2,1,0:T(8,128)S(1)}, f32[17,32,128]{2,1,0:T(8,128)S(1)}, u32[]{:S(2)}, u32[]{:S(2)}) collective-permute-start(f32[17,32,128]{2,1,0:T(8,128)S(1)} %get-tuple-element.41.own), channel_id=1, source_target_pairs={{1,0},{2,1},{3,2},{4,3},{5,4},{6,5},{7,6},{8,7},{9,8},{10,9},{11,1... | collective-permute-start | bytes 835592 | tf_op jit(solution)/shard_map/ppermute | solution.py:555
  92.4 2.4 %collective-permute-start.8 = (f32[17,32,128]{2,1,0:T(8,128)S(1)}, f32[17,32,128]{2,1,0:T(8,128)S(1)}, u32[]{:S(2)}, u32[]{:S(2)}) collective-permute-start(f32[17,32,128]{2,1,0:T(8,128)S(1)} %get-tuple-element.41.own), channel_id=1, source_target_pairs={{0,1},{1,2},{2,3},{3,4},{4,5},{5,6},{6,7},{7,8},{8,9},{9,10},{10,1... | collective-permute-start | bytes 835592 | tf_op jit(solution)/shard_map/ppermute | solution.py:555
  94.8 1.6 %collective-permute-done.9.right = f32[17,32,128]{2,1,0:T(8,128)S(1)} collective-permute-done((f32[17,32,128]{2,1,0:T(8,128)S(1)}, f32[17,32,128]{2,1,0:T(8,128)S(1)}, u32[]{:S(2)}, u32[]{:S(2)}) %collective-permute-start.9) | collective-permute-done | bytes 278560 | tf_op jit(solution)/shard_map/ppermute | solution.py:555
  96.5 5.0 %collective-permute-start.11 = (f32[17,32,128]{2,1,0:T(8,128)S(1)}, f32[17,32,128]{2,1,0:T(8,128)S(1)}, u32[]{:S(2)}, u32[]{:S(2)}) collective-permute-start(f32[17,32,128]{2,1,0:T(8,128)S(1)} %collective-permute-done.9.right), channel_id=1, source_target_pairs={{1,0},{2,1},{3,2},{4,3},{5,4},{6,5},{7,6},{8,7},{9,8},{10,9},{11,1... | collective-permute-start | bytes 835592 | tf_op jit(solution)/shard_map/ppermute | solution.py:555
  101.5 1.9 %collective-permute-start.10 = (f32[17,32,128]{2,1,0:T(8,128)S(1)}, f32[17,32,128]{2,1,0:T(8,128)S(1)}, u32[]{:S(2)}, u32[]{:S(2)}) collective-permute-start(f32[17,32,128]{2,1,0:T(8,128)S(1)} %collective-permute-done.8.left), channel_id=1, source_target_pairs={{0,1},{1,2},{2,3},{3,4},{4,5},{5,6},{6,7},{7,8},{8,9},{9,10},{10,1... | collective-permute-start | bytes 835592 | tf_op jit(solution)/shard_map/ppermute | solution.py:555
  103.4 2.3 %collective-permute-start.12 = (f32[10,32,128]{2,1,0:T(8,128)S(1)}, f32[10,32,128]{2,1,0:T(8,128)S(1)}, u32[]{:S(2)}, u32[]{:S(2)}) collective-permute-start(f32[10,32,128]{2,1,0:T(8,128)S(1)} %get-tuple-element.42), channel_id=1, source_target_pairs={{0,16},{16,32},{32,48},{48,64},{64,80},{80,96},{96,112},{112,128},... | collective-permute-start | bytes 491528 | tf_op jit(solution)/shard_map/ppermute | solution.py:555
  105.8 5.6 %collective-permute-start.13 = (f32[10,32,128]{2,1,0:T(8,128)S(1)}, f32[10,32,128]{2,1,0:T(8,128)S(1)}, u32[]{:S(2)}, u32[]{:S(2)}) collective-permute-start(f32[10,32,128]{2,1,0:T(8,128)S(1)} %get-tuple-element.43), channel_id=1, source_target_pairs={{16,0},{32,16},{48,32},{64,48},{80,64},{96,80},{112,96},{128,112},... | collective-permute-start | bytes 491528 | tf_op jit(solution)/shard_map/ppermute | solution.py:555
  111.4 1.4 collective-permute-done.12.behind2.in_behind2
  112.8 1.4 collective-permute-done.13.ahead2.in_ahead2
  117.6 8.2 %all-to-all-start.1 = ((f32[16,5,8,128]{3,2,1,0:T(8,128)}), f32[16,5,8,128]{3,2,1,0:T(8,128)S(1)}, u32[]{:S(2)}, u32[]{:S(2)}) async-start(f32[16,5,8,128]{3,2,1,0:T(8,128)} %copy-done.12), calls=%async_computation.1 | async-start | bytes 655360 | tf_op jit(solution)/shard_map/all_to_all | solution.py:612
  125.7 3.4 %collective-permute-start.14 = (f32[5,32,128]{2,1,0:T(8,128)}, f32[5,32,128]{2,1,0:T(8,128)}, u32[]{:S(2)}, u32[]{:S(2)}) collective-permute-start(f32[5,32,128]{2,1,0:T(8,128)} %copy-done.20), channel_id=1, source_target_pairs={{0,16},{16,32},{32,48},{48,64},{64,80},{80,96},{96,112},{112,128},... | collective-permute-start | bytes 245768 | tf_op jit(solution)/shard_map/ppermute | solution.py:555
  129.1 4.8 %collective-permute-start.15 = (f32[5,32,128]{2,1,0:T(8,128)}, f32[5,32,128]{2,1,0:T(8,128)}, u32[]{:S(2)}, u32[]{:S(2)}) collective-permute-start(f32[5,32,128]{2,1,0:T(8,128)} %copy-done.19), channel_id=1, source_target_pairs={{16,0},{32,16},{48,32},{64,48},{80,64},{96,80},{112,96},{128,112},... | collective-permute-start | bytes 245768 | tf_op jit(solution)/shard_map/ppermute | solution.py:555
  135.8 10.1 %shard_map.52.e3 = f32[10,32,128]{2,1,0:T(8,128)S(1)} custom-call(f32[16,5,8,128]{3,2,1,0:T(8,128)S(1)} %all-to-all-done.1.gathered, f32[17,32,128]{2,1,0:T(8,128)S(1)} %get-tuple-element.41.own, f32[17,32,128]{2,1,0:T(8,128)S(1)} %collective-permute-done.8.left, f32[17,32,128]{2,1,0:T(8,128)S(1)} %collective-permute-done.9.right, ...), custom_call_target="tpu_custom_call" | custom-call | tf_op jit(solution)/shard_map/pallas_call | solution.py:33
  145.9 2.3 %copy-done.1 = f32[6,24,32,256]{3,2,1,0:T(8,128)S(1)} copy-done((f32[6,24,32,256]{3,2,1,0:T(8,128)S(1)}, f32[6,24,32,256]{3,2,1,0:T(8,128)}, u32[]{:S(2)}) %copy-start.1) | copy-done | bytes 4718616
  150.1 1.0 copy-done.11
  152.0 7.0 %shard_map.53 = f32[32,16,128]{2,1,0:T(8,128)} custom-call(f32[10,32,128]{2,1,0:T(8,128)S(1)} %shard_map.52.e3, f32[5,32,128]{2,1,0:T(8,128)} %collective-permute-done.14.in_behind3, f32[10,32,128]{2,1,0:T(8,128)S(1)} %copy-done.7, f32[17,32,128]{2,1,0:T(8,128)S(1)} %collective-permute-done.6.behind.in_behind, ...), custom_call_target="tpu_custom_call" | custom-call | tf_op jit(solution)/shard_map/pallas_call | solution.py:33
  (53 shorter events, 13.6 us)
Async XLA Ops:
  0.0 0.9 copy-start.13
  1.0 0.9 copy-start.16
  1.9 0.9 copy-start.17
  2.8 0.9 copy-start.18
  4.0 24.8 %collective-permute-start = (f32[50,32,128]{2,1,0:T(8,128)S(1)}, f32[50,32,128]{2,1,0:T(8,128)S(1)}, u32[]{:S(2)}, u32[]{:S(2)}) collective-permute-start(f32[50,32,128]{2,1,0:T(8,128)S(1)} %get-tuple-element.29), channel_id=1, source_target_pairs={{0,16},{16,32},{32,48},{48,64},{64,80},{80,96},{96,112},{112,128},... | collective-permute-start | bytes 2457608 | tf_op jit(solution)/shard_map/ppermute | solution.py:555
  7.5 21.3 %collective-permute-start.1 = (f32[49,32,128]{2,1,0:T(8,128)S(1)}, f32[49,32,128]{2,1,0:T(8,128)S(1)}, u32[]{:S(2)}, u32[]{:S(2)}) collective-permute-start(f32[49,32,128]{2,1,0:T(8,128)S(1)} %get-tuple-element.30), channel_id=1, source_target_pairs={{16,0},{32,16},{48,32},{64,48},{80,64},{96,80},{112,96},{128,112},... | collective-permute-start | bytes 2408456 | tf_op jit(solution)/shard_map/ppermute | solution.py:555
  29.5 10.3 %collective-permute-start.2 = (f32[4,6,32,128]{3,2,1,0:T(8,128)S(1)}, f32[4,6,32,128]{3,2,1,0:T(8,128)S(1)}, u32[]{:S(2)}, u32[]{:S(2)}) collective-permute-start(f32[4,6,32,128]{3,2,1,0:T(8,128)S(1)} %get-tuple-element.31), channel_id=1, source_target_pairs={{0,1},{1,2},{2,3},{3,4},{4,5},{5,6},{6,7},{7,8},{8,9},{9,10},{10,1... | collective-permute-start | bytes 1179656 | tf_op jit(solution)/shard_map/ppermute | solution.py:555
  31.5 10.1 %collective-permute-start.3 = (f32[4,6,32,128]{3,2,1,0:T(8,128)S(1)}, f32[4,6,32,128]{3,2,1,0:T(8,128)S(1)}, u32[]{:S(2)}, u32[]{:S(2)}) collective-permute-start(f32[4,6,32,128]{3,2,1,0:T(8,128)S(1)} %get-tuple-element.32), channel_id=1, source_target_pairs={{1,0},{2,1},{3,2},{4,3},{5,4},{6,5},{7,6},{8,7},{9,8},{10,9},{11,1... | collective-permute-start | bytes 1179656 | tf_op jit(solution)/shard_map/ppermute | solution.py:555
  53.3 2.1 %copy-start = (f32[6,24,32,256]{3,2,1,0:T(8,128)}, f32[6,24,32,256]{3,2,1,0:T(8,128)S(1)}, u32[]{:S(2)}) copy-start(f32[6,24,32,256]{3,2,1,0:T(8,128)S(1)} %get-tuple-element.50.in_keep0) | copy-start | bytes 14155780
  55.5 58.8 %copy-start.10 = (f32[20,32,128]{2,1,0:T(8,128)}, f32[20,32,128]{2,1,0:T(8,128)S(1)}, u32[]{:S(2)}) copy-start(f32[20,32,128]{2,1,0:T(8,128)S(1)} %get-tuple-element.48.in_f1) | copy-start | bytes 983044
  55.5 8.0 %collective-permute-start.5 = (f32[11,32,128]{2,1,0:T(8,128)S(1)}, f32[11,32,128]{2,1,0:T(8,128)S(1)}, u32[]{:S(2)}, u32[]{:S(2)}) collective-permute-start(f32[11,32,128]{2,1,0:T(8,128)S(1)} %get-tuple-element.36), channel_id=1, source_target_pairs={{1,0},{2,1},{3,2},{4,3},{5,4},{6,5},{7,6},{8,7},{9,8},{10,9},{11,1... | collective-permute-start | bytes 540680 | tf_op jit(solution)/shard_map/ppermute | solution.py:555
  60.5 8.0 %collective-permute-start.4 = (f32[11,32,128]{2,1,0:T(8,128)S(1)}, f32[11,32,128]{2,1,0:T(8,128)S(1)}, u32[]{:S(2)}, u32[]{:S(2)}) collective-permute-start(f32[11,32,128]{2,1,0:T(8,128)S(1)} %get-tuple-element.33.own2), channel_id=1, source_target_pairs={{0,1},{1,2},{2,3},{3,4},{4,5},{5,6},{6,7},{7,8},{8,9},{9,10},{10,1... | collective-permute-start | bytes 540680 | tf_op jit(solution)/shard_map/ppermute | solution.py:555
  68.7 45.5 %copy-start.14 = (f32[8,32,128]{2,1,0:T(8,128)}, f32[8,32,128]{2,1,0:T(8,128)S(1)}, u32[]{:S(2)}) copy-start(f32[8,32,128]{2,1,0:T(8,128)S(1)} %get-tuple-element.47.in_joined1) | copy-start | bytes 393220
  68.7 21.1 %collective-permute-start.6 = (f32[17,32,128]{2,1,0:T(8,128)S(1)}, f32[17,32,128]{2,1,0:T(8,128)S(1)}, u32[]{:S(2)}, u32[]{:S(2)}) collective-permute-start(f32[17,32,128]{2,1,0:T(8,128)S(1)} %get-tuple-element.37), channel_id=1, source_target_pairs={{0,16},{16,32},{32,48},{48,64},{64,80},{80,96},{96,112},{112,128},... | collective-permute-start | bytes 835592 | tf_op jit(solution)/shard_map/ppermute | solution.py:555
  72.2 17.7 %collective-permute-start.7 = (f32[17,32,128]{2,1,0:T(8,128)S(1)}, f32[17,32,128]{2,1,0:T(8,128)S(1)}, u32[]{:S(2)}, u32[]{:S(2)}) collective-permute-start(f32[17,32,128]{2,1,0:T(8,128)S(1)} %get-tuple-element.39), channel_id=1, source_target_pairs={{16,0},{32,16},{48,32},{64,48},{80,64},{96,80},{112,96},{128,112},... | collective-permute-start | bytes 835592 | tf_op jit(solution)/shard_map/ppermute | solution.py:555
  90.5 6.0 %collective-permute-start.9 = (f32[17,32,128]{2,1,0:T(8,128)S(1)}, f32[17,32,128]{2,1,0:T(8,128)S(1)}, u32[]{:S(2)}, u32[]{:S(2)}) collective-permute-start(f32[17,32,128]{2,1,0:T(8,128)S(1)} %get-tuple-element.41.own), channel_id=1, source_target_pairs={{1,0},{2,1},{3,2},{4,3},{5,4},{6,5},{7,6},{8,7},{9,8},{10,9},{11,1... | collective-permute-start | bytes 835592 | tf_op jit(solution)/shard_map/ppermute | solution.py:555
  92.4 9.1 %collective-permute-start.8 = (f32[17,32,128]{2,1,0:T(8,128)S(1)}, f32[17,32,128]{2,1,0:T(8,128)S(1)}, u32[]{:S(2)}, u32[]{:S(2)}) collective-permute-start(f32[17,32,128]{2,1,0:T(8,128)S(1)} %get-tuple-element.41.own), channel_id=1, source_target_pairs={{0,1},{1,2},{2,3},{3,4},{4,5},{5,6},{6,7},{7,8},{8,9},{9,10},{10,1... | collective-permute-start | bytes 835592 | tf_op jit(solution)/shard_map/ppermute | solution.py:555
  96.5 17.7 %collective-permute-start.11 = (f32[17,32,128]{2,1,0:T(8,128)S(1)}, f32[17,32,128]{2,1,0:T(8,128)S(1)}, u32[]{:S(2)}, u32[]{:S(2)}) collective-permute-start(f32[17,32,128]{2,1,0:T(8,128)S(1)} %collective-permute-done.9.right), channel_id=1, source_target_pairs={{1,0},{2,1},{3,2},{4,3},{5,4},{6,5},{7,6},{8,7},{9,8},{10,9},{11,1... | collective-permute-start | bytes 835592 | tf_op jit(solution)/shard_map/ppermute | solution.py:555
  101.5 12.7 %collective-permute-start.10 = (f32[17,32,128]{2,1,0:T(8,128)S(1)}, f32[17,32,128]{2,1,0:T(8,128)S(1)}, u32[]{:S(2)}, u32[]{:S(2)}) collective-permute-start(f32[17,32,128]{2,1,0:T(8,128)S(1)} %collective-permute-done.8.left), channel_id=1, source_target_pairs={{0,1},{1,2},{2,3},{3,4},{4,5},{5,6},{6,7},{7,8},{8,9},{9,10},{10,1... | collective-permute-start | bytes 835592 | tf_op jit(solution)/shard_map/ppermute | solution.py:555
  103.4 9.4 %collective-permute-start.12 = (f32[10,32,128]{2,1,0:T(8,128)S(1)}, f32[10,32,128]{2,1,0:T(8,128)S(1)}, u32[]{:S(2)}, u32[]{:S(2)}) collective-permute-start(f32[10,32,128]{2,1,0:T(8,128)S(1)} %get-tuple-element.42), channel_id=1, source_target_pairs={{0,16},{16,32},{32,48},{48,64},{64,80},{80,96},{96,112},{112,128},... | collective-permute-start | bytes 491528 | tf_op jit(solution)/shard_map/ppermute | solution.py:555
  105.8 8.5 %collective-permute-start.13 = (f32[10,32,128]{2,1,0:T(8,128)S(1)}, f32[10,32,128]{2,1,0:T(8,128)S(1)}, u32[]{:S(2)}, u32[]{:S(2)}) collective-permute-start(f32[10,32,128]{2,1,0:T(8,128)S(1)} %get-tuple-element.43), channel_id=1, source_target_pairs={{16,0},{32,16},{48,32},{64,48},{80,64},{96,80},{112,96},{128,112},... | collective-permute-start | bytes 491528 | tf_op jit(solution)/shard_map/ppermute | solution.py:555
  112.8 1.5 copy-start.6
  114.2 3.4 %copy-start.2 = (f32[17,32,128]{2,1,0:T(8,128)}, f32[17,32,128]{2,1,0:T(8,128)S(1)}, u32[]{:S(2)}) copy-start(f32[17,32,128]{2,1,0:T(8,128)S(1)} %collective-permute-done.11.right_far) | copy-start | bytes 835588
  117.6 16.3 %all-to-all-start.1 = ((f32[16,5,8,128]{3,2,1,0:T(8,128)}), f32[16,5,8,128]{3,2,1,0:T(8,128)S(1)}, u32[]{:S(2)}, u32[]{:S(2)}) async-start(f32[16,5,8,128]{3,2,1,0:T(8,128)} %copy-done.12), calls=%async_computation.1 | async-start | bytes 655360 | tf_op jit(solution)/shard_map/all_to_all | solution.py:612
  125.7 20.2 %collective-permute-start.14 = (f32[5,32,128]{2,1,0:T(8,128)}, f32[5,32,128]{2,1,0:T(8,128)}, u32[]{:S(2)}, u32[]{:S(2)}) collective-permute-start(f32[5,32,128]{2,1,0:T(8,128)} %copy-done.20), channel_id=1, source_target_pairs={{0,16},{16,32},{32,48},{48,64},{64,80},{80,96},{96,112},{112,128},... | collective-permute-start | bytes 245768 | tf_op jit(solution)/shard_map/ppermute | solution.py:555
  129.1 16.8 %collective-permute-start.15 = (f32[5,32,128]{2,1,0:T(8,128)}, f32[5,32,128]{2,1,0:T(8,128)}, u32[]{:S(2)}, u32[]{:S(2)}) collective-permute-start(f32[5,32,128]{2,1,0:T(8,128)} %copy-done.19), channel_id=1, source_target_pairs={{16,0},{32,16},{48,32},{64,48},{80,64},{96,80},{112,96},{128,112},... | collective-permute-start | bytes 245768 | tf_op jit(solution)/shard_map/ppermute | solution.py:555
  133.9 1.0 copy-start.3
  134.8 1.0 copy-start.5
  145.9 2.3 %copy-start.1 = (f32[6,24,32,256]{3,2,1,0:T(8,128)S(1)}, f32[6,24,32,256]{3,2,1,0:T(8,128)}, u32[]{:S(2)}) copy-start(f32[6,24,32,256]{3,2,1,0:T(8,128)} %copy-done) | copy-start | bytes 14155780
  148.3 0.9 copy-start.7
  149.2 0.9 copy-start.9
  150.1 1.0 copy-start.11
  (6 other events, 4.3 us)

commit v5 on v4

--- a/solution.py
+++ b/solution.py
@@ -27,14 +27,17 @@
 
 
 def call(kernel, ins, outs, scratch=(), limit=10, apart=(), apart_outs=()):
-    def places(count, left):
-        return [pl.BlockSpec(memory_space=pl.ANY) if i in left else spec() for i in range(count)]
+    def places(count, left, space):
+        return [pl.BlockSpec(memory_space=space) if i in left else spec() for i in range(count)]
 
     return pl.pallas_call(
         kernel,
-        out_shape=[jax.ShapeDtypeStruct(s, F32) for s in outs],
-        in_specs=places(len(ins), apart),
-        out_specs=places(len(outs), apart_outs),
+        out_shape=[
+            pltpu.HBM(s, F32) if i in apart_outs else jax.ShapeDtypeStruct(s, F32)
+            for i, s in enumerate(outs)
+        ],
+        in_specs=places(len(ins), apart, pl.ANY),
+        out_specs=places(len(outs), apart_outs, pltpu.HBM),
         scratch_shapes=[pltpu.VMEM(s, F32) if isinstance(s, tuple) else s for s in scratch],
         compiler_params=pltpu.CompilerParams(vmem_limit_bytes=limit * 1024 * 1024),
     )(*ins)
@@ -407,14 +410,11 @@
     nearer[...] = ahead[0:10]
 
 
-def near_kernel(count, own, left, right, left_far, right_far, behind2, ahead2, out, further, nearer):
+def near_kernel(count, own, left, right, left_far, right_far, out):
     rhs = [ref[count, 0:8] for ref in (left_far, left, own, right, right_far)]
     for c in range(count):
         for s in range(5):
             out[c, s] = rhs[s]
-    for a in range(5):
-        further[a] = behind2[2 * a + 1]
-        nearer[a] = ahead2[2 * a]
 
 
 PAD3 = 8
@@ -478,14 +478,14 @@
         (in_joined1, joined1), (in_f1, f1), (in_ops1, ops1), (in_keep0, keep0),
     ]
     copies = fetch(pairs, sems)
-    sources = [(behind3, None)]
+    sources = [(behind3, 1)]
     sources += [(ref, h) for ref in (behind2, behind, own, ahead, ahead2) for h in range(2)]
-    sources += [(ahead3, None)]
+    sources += [(ahead3, 0)]
     for n, (source, h) in enumerate(sources):
         if n % 2 or n == 0:
             copies[(n + 1) // 2].wait()
         for a, ref in enumerate((f2, x2, y2, z2, d2)):
-            value = source[a if h is None else 2 * a + h]
+            value = source[2 * a + h]
             ref[2 * n] = value
             ref[2 * n + 1] = roll(value, 64, 1)
 
@@ -563,6 +563,7 @@
         stage_kernel,
         (labels, conduct_x, conduct_y, conduct_z),
         [(4, R0, *side), (4 * H0 - 2, *side), (4 * H0 - 3, *side)],
+        limit=10,
     )
     behind = shift(to_right, "gx", 1)
     ahead = shift(to_left, "gx", -1)
@@ -604,13 +605,9 @@
     behind2, ahead2 = shift(further, "gx", 1), shift(nearer, "gx", -1)
     left_far, right_far = shift(left, "gy", 1), shift(right, "gy", -1)
     near = (message, left, right, left_far, right_far)
-    rhs3, further, nearer = call(
-        functools.partial(near_kernel, count),
-        (*near, behind2, ahead2),
-        [(count, 5, 8, 128), (5, *side), (5, *side)],
-    )
+    (rhs3,) = call(functools.partial(near_kernel, count), near, [(count, 5, 8, 128)])
     rhs3 = lax.all_to_all(rhs3, "gx", 0, 0)
-    behind3, ahead3 = shift(further, "gx", 1), shift(nearer, "gx", -1)
+    behind3, ahead3 = shift(behind2, "gx", 1), shift(ahead2, "gx", -1)
     rows3 = 2 * count + 2 * PAD3
     (e3,) = call(
         functools.partial(solve_kernel, count),
@@ -618,6 +615,7 @@
         [(10, *side)],
         [(4, rows3, *side)] + [(rows3, *side)] * 3,
     )
+    keep0, ops1, f1 = (pltpu.with_memory_space_constraint(x, pltpu.HBM) for x in (keep0, ops1, f1))
     (out,) = call(
         up_kernel,
         (e3, behind3, behind2, behind, joined2, ahead, ahead2, ahead3, joined1, f1, ops1, keep0),
@@ -625,11 +623,11 @@
         [(24, *side)] * 8
         + [(N1, *side)] * 3
         + [(24, NZ, 256)] * 2
-        + [(5, *side), (10, *side), (11 + H1, *side), (10, *side)]
-        + [(11 + H1, *side), (10, *side), (5, *side), (8, *side)]
+        + [(10, *side), (10, *side), (11 + H1, *side), (10, *side)]
+        + [(11 + H1, *side), (10, *side), (10, *side), (8, *side)]
         + [(5, N1, *side), (6, 24, NZ, 256)]
         + [pltpu.SemaphoreType.DMA((11,))],
-        limit=18,
+        limit=17,
         apart=range(1, 12),
     )
     return out

time: 162 us -> 143 us (0.88)
  local copies, waits for them, and re-layouts: 17 us -> 3.66 us
  starting transfers between devices: 65.6 us -> 61.9 us
  waiting for transfers between devices: 32.7 us -> 29.9 us
    unnamed x42 -> x8, local copies, waits for them, and re-layouts: 17 us -> 3.66 us
    all_to_all x1, starting transfers between devices: 8.16 us -> 4.51 us  [body(): rhs3 = lax.all_to_all(rhs3, 'gx', 0, 0)]
    ppermute x16, waiting for transfers between devices: 32.7 us -> 29.9 us  [shift(): return lax.ppermute(value, axis, route)]
  transfers between devices with their start and end apart: 17 -> 17, of which waited for: 8 -> 6; matrix products, arithmetic and copies ran while one was open for 0% -> 0% of each run, Pallas kernels for 6% -> 8%
where the time goes in v5:
time: 143 us; the launch traced here: 141 us
  starting transfers between devices  61.9 us (43%)
  Pallas kernels  32 us (22%)
  waiting for transfers between devices  29.9 us (21%)
  blocking collectives  12.6 us (9%)
  local copies, waits for them, and re-layouts  3.66 us (3%)
    ppermute x16, starting transfers between devices, shift(): return lax.ppermute(value, axis, route)  57.4 us
    pallas_call x8, Pallas kernels, call(): pl.pallas_call(kernel, out_shape=[pltpu.HBM(s, F32) if i in apart_outs el...  32 us
    ppermute x16, waiting for transfers between devices, shift(): return lax.ppermute(value, axis, route)  29.9 us
    all_to_all x1, blocking collectives, body(): all3 = lax.all_to_all(own3, 'gx', 0, 0)  12.6 us
    all_to_all x1, starting transfers between devices, body(): rhs3 = lax.all_to_all(rhs3, 'gx', 0, 0)  4.51 us
    unnamed x8, local copies, waits for them, and re-layouts  3.66 us
  transfers between devices with their start and end apart: 17, of which 6 were waited for; matrix products, arithmetic and copies ran while one was open for 0% of the time, Pallas kernels for 8%

profile of v5, /device:TPU:130, one launch (start us, length us, event | category | flops | bytes accessed | tf_op | source)
XLA Modules:
  0.0 140.5 jit_solution(3178745437357788547)
XLA Ops:
  0.0 0.9 copy-done
  1.0 0.9 copy-done.1
  1.9 0.9 copy-done.2
  2.8 0.9 copy-done.3
  4.0 3.5 %collective-permute-start = (f32[50,32,128]{2,1,0:T(8,128)S(1)}, f32[50,32,128]{2,1,0:T(8,128)S(1)}, u32[]{:S(2)}, u32[]{:S(2)}) collective-permute-start(f32[50,32,128]{2,1,0:T(8,128)S(1)} %get-tuple-element.26), channel_id=1, source_target_pairs={{0,16},{16,32},{32,48},{48,64},{64,80},{80,96},{96,112},{112,128},... | collective-permute-start | bytes 2457608 | tf_op jit(solution)/shard_map/ppermute | solution.py:555
  7.5 4.5 %collective-permute-start.1 = (f32[49,32,128]{2,1,0:T(8,128)S(1)}, f32[49,32,128]{2,1,0:T(8,128)S(1)}, u32[]{:S(2)}, u32[]{:S(2)}) collective-permute-start(f32[49,32,128]{2,1,0:T(8,128)S(1)} %get-tuple-element.27), channel_id=1, source_target_pairs={{16,0},{32,16},{48,32},{64,48},{80,64},{96,80},{112,96},{128,112},... | collective-permute-start | bytes 2408456 | tf_op jit(solution)/shard_map/ppermute | solution.py:555
  12.0 16.8 %collective-permute-done.1.ahead = f32[49,32,128]{2,1,0:T(8,128)S(1)} collective-permute-done((f32[49,32,128]{2,1,0:T(8,128)S(1)}, f32[49,32,128]{2,1,0:T(8,128)S(1)}, u32[]{:S(2)}, u32[]{:S(2)}) %collective-permute-start.1) | collective-permute-done | bytes 802848 | tf_op jit(solution)/shard_map/ppermute | solution.py:555
  29.5 1.9 %collective-permute-start.2 = (f32[4,6,32,128]{3,2,1,0:T(8,128)S(1)}, f32[4,6,32,128]{3,2,1,0:T(8,128)S(1)}, u32[]{:S(2)}, u32[]{:S(2)}) collective-permute-start(f32[4,6,32,128]{3,2,1,0:T(8,128)S(1)} %get-tuple-element.28), channel_id=1, source_target_pairs={{0,1},{1,2},{2,3},{3,4},{4,5},{5,6},{6,7},{7,8},{8,9},{9,10},{10,1... | collective-permute-start | bytes 1179656 | tf_op jit(solution)/shard_map/ppermute | solution.py:555
  31.5 4.9 %collective-permute-start.3 = (f32[4,6,32,128]{3,2,1,0:T(8,128)S(1)}, f32[4,6,32,128]{3,2,1,0:T(8,128)S(1)}, u32[]{:S(2)}, u32[]{:S(2)}) collective-permute-start(f32[4,6,32,128]{3,2,1,0:T(8,128)S(1)} %get-tuple-element.29), channel_id=1, source_target_pairs={{1,0},{2,1},{3,2},{4,3},{5,4},{6,5},{7,6},{8,7},{9,8},{10,9},{11,1... | collective-permute-start | bytes 1179656 | tf_op jit(solution)/shard_map/ppermute | solution.py:555
  36.3 3.5 %collective-permute-done.2.from_left = f32[4,6,32,128]{3,2,1,0:T(8,128)S(1)} collective-permute-done((f32[4,6,32,128]{3,2,1,0:T(8,128)S(1)}, f32[4,6,32,128]{3,2,1,0:T(8,128)S(1)}, u32[]{:S(2)}, u32[]{:S(2)}) %collective-permute-start.2) | collective-permute-done | bytes 393248 | tf_op jit(solution)/shard_map/ppermute | solution.py:555
  39.8 1.8 %collective-permute-done.3.from_right = f32[4,6,32,128]{3,2,1,0:T(8,128)S(1)} collective-permute-done((f32[4,6,32,128]{3,2,1,0:T(8,128)S(1)}, f32[4,6,32,128]{3,2,1,0:T(8,128)S(1)}, u32[]{:S(2)}, u32[]{:S(2)}) %collective-permute-start.3) | collective-permute-done | bytes 393248 | tf_op jit(solution)/shard_map/ppermute | solution.py:555
  41.6 12.1 %shard_map.48 = (f32[6,24,32,256]{3,2,1,0:T(8,128)}, f32[5,20,32,128]{3,2,1,0:T(8,128)}, f32[20,32,128]{2,1,0:T(8,128)}, f32[8,32,128]{2,1,0:T(8,128)S(1)}, f32[...) custom-call(f32[4,16,32,128]{3,2,1,0:T(8,128)S(1)} %get-tuple-elemen, ...), custom_call_target="tpu_custom_call" | custom-call | tf_op jit(solution)/shard_map/pallas_call | solution.py:33
  53.7 5.0 %collective-permute-start.5 = (f32[11,32,128]{2,1,0:T(8,128)S(1)}, f32[11,32,128]{2,1,0:T(8,128)S(1)}, u32[]{:S(2)}, u32[]{:S(2)}) collective-permute-start(f32[11,32,128]{2,1,0:T(8,128)S(1)} %get-tuple-element.33), channel_id=1, source_target_pairs={{1,0},{2,1},{3,2},{4,3},{5,4},{6,5},{7,6},{8,7},{9,8},{10,9},{11,1... | collective-permute-start | bytes 540680 | tf_op jit(solution)/shard_map/ppermute | solution.py:555
  58.8 1.9 %collective-permute-start.4 = (f32[11,32,128]{2,1,0:T(8,128)S(1)}, f32[11,32,128]{2,1,0:T(8,128)S(1)}, u32[]{:S(2)}, u32[]{:S(2)}) collective-permute-start(f32[11,32,128]{2,1,0:T(8,128)S(1)} %get-tuple-element.30.own2), channel_id=1, source_target_pairs={{0,1},{1,2},{2,3},{3,4},{4,5},{5,6},{6,7},{7,8},{8,9},{9,10},{10,1... | collective-permute-start | bytes 540680 | tf_op jit(solution)/shard_map/ppermute | solution.py:555
  60.7 1.1 collective-permute-done.5.right
  61.8 5.0 %collective-permute-done.4.left = f32[11,32,128]{2,1,0:T(8,128)S(1)} collective-permute-done((f32[11,32,128]{2,1,0:T(8,128)S(1)}, f32[11,32,128]{2,1,0:T(8,128)S(1)}, u32[]{:S(2)}, u32[]{:S(2)}) %collective-permute-start.4) | collective-permute-done | bytes 180256 | tf_op jit(solution)/shard_map/ppermute | solution.py:555
  67.0 3.4 %collective-permute-start.6 = (f32[17,32,128]{2,1,0:T(8,128)S(1)}, f32[17,32,128]{2,1,0:T(8,128)S(1)}, u32[]{:S(2)}, u32[]{:S(2)}) collective-permute-start(f32[17,32,128]{2,1,0:T(8,128)S(1)} %get-tuple-element.34), channel_id=1, source_target_pairs={{0,16},{16,32},{32,48},{48,64},{64,80},{80,96},{96,112},{112,128},... | collective-permute-start | bytes 835592 | tf_op jit(solution)/shard_map/ppermute | solution.py:555
  70.4 5.0 %collective-permute-start.7 = (f32[17,32,128]{2,1,0:T(8,128)S(1)}, f32[17,32,128]{2,1,0:T(8,128)S(1)}, u32[]{:S(2)}, u32[]{:S(2)}) collective-permute-start(f32[17,32,128]{2,1,0:T(8,128)S(1)} %get-tuple-element.36), channel_id=1, source_target_pairs={{16,0},{32,16},{48,32},{64,48},{80,64},{96,80},{112,96},{128,112},... | collective-permute-start | bytes 835592 | tf_op jit(solution)/shard_map/ppermute | solution.py:555
  75.4 12.6 %all_to_all.10.ops3 = f32[16,32,128]{2,1,0:T(8,128)S(1)} all-to-all(f32[16,32,128]{2,1,0:T(8,128)S(1)} %get-tuple-element.37), channel_id=1, replica_groups=mesh['gx'=16,'gy'=16] {'gx'}, dimensions={0} | all-to-all | bytes 524288 | tf_op jit(solution)/shard_map/all_to_all | solution.py:591
  88.7 1.9 %collective-permute-start.9 = (f32[17,32,128]{2,1,0:T(8,128)S(1)}, f32[17,32,128]{2,1,0:T(8,128)S(1)}, u32[]{:S(2)}, u32[]{:S(2)}) collective-permute-start(f32[17,32,128]{2,1,0:T(8,128)S(1)} %get-tuple-element.38.own), channel_id=1, source_target_pairs={{1,0},{2,1},{3,2},{4,3},{5,4},{6,5},{7,6},{8,7},{9,8},{10,9},{11,1... | collective-permute-start | bytes 835592 | tf_op jit(solution)/shard_map/ppermute | solution.py:555
  90.7 2.4 %collective-permute-start.8 = (f32[17,32,128]{2,1,0:T(8,128)S(1)}, f32[17,32,128]{2,1,0:T(8,128)S(1)}, u32[]{:S(2)}, u32[]{:S(2)}) collective-permute-start(f32[17,32,128]{2,1,0:T(8,128)S(1)} %get-tuple-element.38.own), channel_id=1, source_target_pairs={{0,1},{1,2},{2,3},{3,4},{4,5},{5,6},{6,7},{7,8},{8,9},{9,10},{10,1... | collective-permute-start | bytes 835592 | tf_op jit(solution)/shard_map/ppermute | solution.py:555
  93.1 1.6 %collective-permute-done.9.right = f32[17,32,128]{2,1,0:T(8,128)S(1)} collective-permute-done((f32[17,32,128]{2,1,0:T(8,128)S(1)}, f32[17,32,128]{2,1,0:T(8,128)S(1)}, u32[]{:S(2)}, u32[]{:S(2)}) %collective-permute-start.9) | collective-permute-done | bytes 278560 | tf_op jit(solution)/shard_map/ppermute | solution.py:555
  94.7 5.0 %collective-permute-start.11 = (f32[17,32,128]{2,1,0:T(8,128)S(1)}, f32[17,32,128]{2,1,0:T(8,128)S(1)}, u32[]{:S(2)}, u32[]{:S(2)}) collective-permute-start(f32[17,32,128]{2,1,0:T(8,128)S(1)} %collective-permute-done.9.right), channel_id=1, source_target_pairs={{1,0},{2,1},{3,2},{4,3},{5,4},{6,5},{7,6},{8,7},{9,8},{10,9},{11,1... | collective-permute-start | bytes 835592 | tf_op jit(solution)/shard_map/ppermute | solution.py:555
  99.7 1.9 %collective-permute-start.10 = (f32[17,32,128]{2,1,0:T(8,128)S(1)}, f32[17,32,128]{2,1,0:T(8,128)S(1)}, u32[]{:S(2)}, u32[]{:S(2)}) collective-permute-start(f32[17,32,128]{2,1,0:T(8,128)S(1)} %collective-permute-done.8.left), channel_id=1, source_target_pairs={{0,1},{1,2},{2,3},{3,4},{4,5},{5,6},{6,7},{7,8},{8,9},{9,10},{10,1... | collective-permute-start | bytes 835592 | tf_op jit(solution)/shard_map/ppermute | solution.py:555
  101.7 2.3 %collective-permute-start.12 = (f32[10,32,128]{2,1,0:T(8,128)S(1)}, f32[10,32,128]{2,1,0:T(8,128)S(1)}, u32[]{:S(2)}, u32[]{:S(2)}) collective-permute-start(f32[10,32,128]{2,1,0:T(8,128)S(1)} %get-tuple-element.39), channel_id=1, source_target_pairs={{0,16},{16,32},{32,48},{48,64},{64,80},{80,96},{96,112},{112,128},... | collective-permute-start | bytes 491528 | tf_op jit(solution)/shard_map/ppermute | solution.py:555
  104.0 5.6 %collective-permute-start.14 = (f32[10,32,128]{2,1,0:T(8,128)S(1)}, f32[10,32,128]{2,1,0:T(8,128)S(1)}, u32[]{:S(2)}, u32[]{:S(2)}) collective-permute-start(f32[10,32,128]{2,1,0:T(8,128)S(1)} %get-tuple-element.40), channel_id=1, source_target_pairs={{16,0},{32,16},{48,32},{64,48},{80,64},{96,80},{112,96},{128,112},... | collective-permute-start | bytes 491528 | tf_op jit(solution)/shard_map/ppermute | solution.py:555
  109.7 0.8 shard_map.51
  110.4 4.5 %all-to-all-start.1 = ((f32[16,5,8,128]{3,2,1,0:T(8,128)}), f32[16,5,8,128]{3,2,1,0:T(8,128)S(1)}, u32[]{:S(2)}, u32[]{:S(2)}) async-start(f32[16,5,8,128]{3,2,1,0:T(8,128)} %shard_map.51), calls=%async_computation.1 | async-start | bytes 655360 | tf_op jit(solution)/shard_map/all_to_all | solution.py:609
  114.9 3.4 %collective-permute-start.13 = (f32[10,32,128]{2,1,0:T(8,128)S(1)}, f32[10,32,128]{2,1,0:T(8,128)S(1)}, u32[]{:S(2)}, u32[]{:S(2)}) collective-permute-start(f32[10,32,128]{2,1,0:T(8,128)S(1)} %collective-permute-done.12.in_behind2), channel_id=1, source_target_pairs={{0,16},{16,32},{32,48},{48,64},{64,80},{80,96},{96,112},{112,128},... | collective-permute-start | bytes 491528 | tf_op jit(solution)/shard_map/ppermute | solution.py:555
  118.3 4.8 %collective-permute-start.15 = (f32[10,32,128]{2,1,0:T(8,128)S(1)}, f32[10,32,128]{2,1,0:T(8,128)S(1)}, u32[]{:S(2)}, u32[]{:S(2)}) collective-permute-start(f32[10,32,128]{2,1,0:T(8,128)S(1)} %collective-permute-done.14.in_ahead2), channel_id=1, source_target_pairs={{16,0},{32,16},{48,32},{64,48},{80,64},{96,80},{112,96},{128,112},... | collective-permute-start | bytes 491528 | tf_op jit(solution)/shard_map/ppermute | solution.py:555
  123.1 10.1 %shard_map.52.e3 = f32[10,32,128]{2,1,0:T(8,128)S(1)} custom-call(f32[16,5,8,128]{3,2,1,0:T(8,128)S(1)} %all-to-all-done.1.gathered, f32[17,32,128]{2,1,0:T(8,128)S(1)} %get-tuple-element.38.own, f32[17,32,128]{2,1,0:T(8,128)S(1)} %collective-permute-done.8.left, f32[17,32,128]{2,1,0:T(8,128)S(1)} %collective-permute-done.9.right, ...), custom_call_target="tpu_custom_call" | custom-call | tf_op jit(solution)/shard_map/pallas_call | solution.py:33
  133.2 7.1 %shard_map.53 = f32[32,16,128]{2,1,0:T(8,128)} custom-call(f32[10,32,128]{2,1,0:T(8,128)S(1)} %shard_map.52.e3, f32[10,32,128]{2,1,0:T(8,128)S(1)} %collective-permute-done.13.in_behind3, f32[10,32,128]{2,1,0:T(8,128)S(1)} %collective-permute-done.12.in_behind2, f32[17,32,128]{2,1,0:T(8,128)S(1)} %collective-permute-done.6.behind.in_behind, ...), custom_call_target="tpu_custom_call" | custom-call | tf_op jit(solution)/shard_map/pallas_call | solution.py:33
  (19 shorter events, 1.9 us)
Async XLA Ops:
  0.0 0.9 copy-start
  1.0 0.9 copy-start.1
  1.9 0.9 copy-start.2
  2.8 0.9 copy-start.3
  4.0 24.8 %collective-permute-start = (f32[50,32,128]{2,1,0:T(8,128)S(1)}, f32[50,32,128]{2,1,0:T(8,128)S(1)}, u32[]{:S(2)}, u32[]{:S(2)}) collective-permute-start(f32[50,32,128]{2,1,0:T(8,128)S(1)} %get-tuple-element.26), channel_id=1, source_target_pairs={{0,16},{16,32},{32,48},{48,64},{64,80},{80,96},{96,112},{112,128},... | collective-permute-start | bytes 2457608 | tf_op jit(solution)/shard_map/ppermute | solution.py:555
  7.5 21.3 %collective-permute-start.1 = (f32[49,32,128]{2,1,0:T(8,128)S(1)}, f32[49,32,128]{2,1,0:T(8,128)S(1)}, u32[]{:S(2)}, u32[]{:S(2)}) collective-permute-start(f32[49,32,128]{2,1,0:T(8,128)S(1)} %get-tuple-element.27), channel_id=1, source_target_pairs={{16,0},{32,16},{48,32},{64,48},{80,64},{96,80},{112,96},{128,112},... | collective-permute-start | bytes 2408456 | tf_op jit(solution)/shard_map/ppermute | solution.py:555
  29.5 10.3 %collective-permute-start.2 = (f32[4,6,32,128]{3,2,1,0:T(8,128)S(1)}, f32[4,6,32,128]{3,2,1,0:T(8,128)S(1)}, u32[]{:S(2)}, u32[]{:S(2)}) collective-permute-start(f32[4,6,32,128]{3,2,1,0:T(8,128)S(1)} %get-tuple-element.28), channel_id=1, source_target_pairs={{0,1},{1,2},{2,3},{3,4},{4,5},{5,6},{6,7},{7,8},{8,9},{9,10},{10,1... | collective-permute-start | bytes 1179656 | tf_op jit(solution)/shard_map/ppermute | solution.py:555
  31.5 10.1 %collective-permute-start.3 = (f32[4,6,32,128]{3,2,1,0:T(8,128)S(1)}, f32[4,6,32,128]{3,2,1,0:T(8,128)S(1)}, u32[]{:S(2)}, u32[]{:S(2)}) collective-permute-start(f32[4,6,32,128]{3,2,1,0:T(8,128)S(1)} %get-tuple-element.29), channel_id=1, source_target_pairs={{1,0},{2,1},{3,2},{4,3},{5,4},{6,5},{7,6},{8,7},{9,8},{10,9},{11,1... | collective-permute-start | bytes 1179656 | tf_op jit(solution)/shard_map/ppermute | solution.py:555
  53.7 8.0 %collective-permute-start.5 = (f32[11,32,128]{2,1,0:T(8,128)S(1)}, f32[11,32,128]{2,1,0:T(8,128)S(1)}, u32[]{:S(2)}, u32[]{:S(2)}) collective-permute-start(f32[11,32,128]{2,1,0:T(8,128)S(1)} %get-tuple-element.33), channel_id=1, source_target_pairs={{1,0},{2,1},{3,2},{4,3},{5,4},{6,5},{7,6},{8,7},{9,8},{10,9},{11,1... | collective-permute-start | bytes 540680 | tf_op jit(solution)/shard_map/ppermute | solution.py:555
  58.8 8.0 %collective-permute-start.4 = (f32[11,32,128]{2,1,0:T(8,128)S(1)}, f32[11,32,128]{2,1,0:T(8,128)S(1)}, u32[]{:S(2)}, u32[]{:S(2)}) collective-permute-start(f32[11,32,128]{2,1,0:T(8,128)S(1)} %get-tuple-element.30.own2), channel_id=1, source_target_pairs={{0,1},{1,2},{2,3},{3,4},{4,5},{5,6},{6,7},{7,8},{8,9},{9,10},{10,1... | collective-permute-start | bytes 540680 | tf_op jit(solution)/shard_map/ppermute | solution.py:555
  67.0 21.1 %collective-permute-start.6 = (f32[17,32,128]{2,1,0:T(8,128)S(1)}, f32[17,32,128]{2,1,0:T(8,128)S(1)}, u32[]{:S(2)}, u32[]{:S(2)}) collective-permute-start(f32[17,32,128]{2,1,0:T(8,128)S(1)} %get-tuple-element.34), channel_id=1, source_target_pairs={{0,16},{16,32},{32,48},{48,64},{64,80},{80,96},{96,112},{112,128},... | collective-permute-start | bytes 835592 | tf_op jit(solution)/shard_map/ppermute | solution.py:555
  70.4 17.7 %collective-permute-start.7 = (f32[17,32,128]{2,1,0:T(8,128)S(1)}, f32[17,32,128]{2,1,0:T(8,128)S(1)}, u32[]{:S(2)}, u32[]{:S(2)}) collective-permute-start(f32[17,32,128]{2,1,0:T(8,128)S(1)} %get-tuple-element.36), channel_id=1, source_target_pairs={{16,0},{32,16},{48,32},{64,48},{80,64},{96,80},{112,96},{128,112},... | collective-permute-start | bytes 835592 | tf_op jit(solution)/shard_map/ppermute | solution.py:555
  88.7 6.0 %collective-permute-start.9 = (f32[17,32,128]{2,1,0:T(8,128)S(1)}, f32[17,32,128]{2,1,0:T(8,128)S(1)}, u32[]{:S(2)}, u32[]{:S(2)}) collective-permute-start(f32[17,32,128]{2,1,0:T(8,128)S(1)} %get-tuple-element.38.own), channel_id=1, source_target_pairs={{1,0},{2,1},{3,2},{4,3},{5,4},{6,5},{7,6},{8,7},{9,8},{10,9},{11,1... | collective-permute-start | bytes 835592 | tf_op jit(solution)/shard_map/ppermute | solution.py:555
  90.7 9.1 %collective-permute-start.8 = (f32[17,32,128]{2,1,0:T(8,128)S(1)}, f32[17,32,128]{2,1,0:T(8,128)S(1)}, u32[]{:S(2)}, u32[]{:S(2)}) collective-permute-start(f32[17,32,128]{2,1,0:T(8,128)S(1)} %get-tuple-element.38.own), channel_id=1, source_target_pairs={{0,1},{1,2},{2,3},{3,4},{4,5},{5,6},{6,7},{7,8},{8,9},{9,10},{10,1... | collective-permute-start | bytes 835592 | tf_op jit(solution)/shard_map/ppermute | solution.py:555
  94.7 14.9 %collective-permute-start.11 = (f32[17,32,128]{2,1,0:T(8,128)S(1)}, f32[17,32,128]{2,1,0:T(8,128)S(1)}, u32[]{:S(2)}, u32[]{:S(2)}) collective-permute-start(f32[17,32,128]{2,1,0:T(8,128)S(1)} %collective-permute-done.9.right), channel_id=1, source_target_pairs={{1,0},{2,1},{3,2},{4,3},{5,4},{6,5},{7,6},{8,7},{9,8},{10,9},{11,1... | collective-permute-start | bytes 835592 | tf_op jit(solution)/shard_map/ppermute | solution.py:555
  99.7 9.9 %collective-permute-start.10 = (f32[17,32,128]{2,1,0:T(8,128)S(1)}, f32[17,32,128]{2,1,0:T(8,128)S(1)}, u32[]{:S(2)}, u32[]{:S(2)}) collective-permute-start(f32[17,32,128]{2,1,0:T(8,128)S(1)} %collective-permute-done.8.left), channel_id=1, source_target_pairs={{0,1},{1,2},{2,3},{3,4},{4,5},{5,6},{6,7},{7,8},{8,9},{9,10},{10,1... | collective-permute-start | bytes 835592 | tf_op jit(solution)/shard_map/ppermute | solution.py:555
  101.7 13.3 %collective-permute-start.12 = (f32[10,32,128]{2,1,0:T(8,128)S(1)}, f32[10,32,128]{2,1,0:T(8,128)S(1)}, u32[]{:S(2)}, u32[]{:S(2)}) collective-permute-start(f32[10,32,128]{2,1,0:T(8,128)S(1)} %get-tuple-element.39), channel_id=1, source_target_pairs={{0,16},{16,32},{32,48},{48,64},{64,80},{80,96},{96,112},{112,128},... | collective-permute-start | bytes 491528 | tf_op jit(solution)/shard_map/ppermute | solution.py:555
  104.0 14.3 %collective-permute-start.14 = (f32[10,32,128]{2,1,0:T(8,128)S(1)}, f32[10,32,128]{2,1,0:T(8,128)S(1)}, u32[]{:S(2)}, u32[]{:S(2)}) collective-permute-start(f32[10,32,128]{2,1,0:T(8,128)S(1)} %get-tuple-element.40), channel_id=1, source_target_pairs={{16,0},{32,16},{48,32},{64,48},{80,64},{96,80},{112,96},{128,112},... | collective-permute-start | bytes 491528 | tf_op jit(solution)/shard_map/ppermute | solution.py:555
  110.4 12.7 %all-to-all-start.1 = ((f32[16,5,8,128]{3,2,1,0:T(8,128)}), f32[16,5,8,128]{3,2,1,0:T(8,128)S(1)}, u32[]{:S(2)}, u32[]{:S(2)}) async-start(f32[16,5,8,128]{3,2,1,0:T(8,128)} %shard_map.51), calls=%async_computation.1 | async-start | bytes 655360 | tf_op jit(solution)/shard_map/all_to_all | solution.py:609
  114.9 18.3 %collective-permute-start.13 = (f32[10,32,128]{2,1,0:T(8,128)S(1)}, f32[10,32,128]{2,1,0:T(8,128)S(1)}, u32[]{:S(2)}, u32[]{:S(2)}) collective-permute-start(f32[10,32,128]{2,1,0:T(8,128)S(1)} %collective-permute-done.12.in_behind2), channel_id=1, source_target_pairs={{0,16},{16,32},{32,48},{48,64},{64,80},{80,96},{96,112},{112,128},... | collective-permute-start | bytes 491528 | tf_op jit(solution)/shard_map/ppermute | solution.py:555
  118.3 14.9 %collective-permute-start.15 = (f32[10,32,128]{2,1,0:T(8,128)S(1)}, f32[10,32,128]{2,1,0:T(8,128)S(1)}, u32[]{:S(2)}, u32[]{:S(2)}) collective-permute-start(f32[10,32,128]{2,1,0:T(8,128)S(1)} %collective-permute-done.14.in_ahead2), channel_id=1, source_target_pairs={{16,0},{32,16},{48,32},{64,48},{80,64},{96,80},{112,96},{128,112},... | collective-permute-start | bytes 491528 | tf_op jit(solution)/shard_map/ppermute | solution.py:555

commit v6 on v5

--- a/solution.py
+++ b/solution.py
@@ -144,12 +144,16 @@
     return copies
 
 
-def stage_kernel(labels, cond_x, cond_y, cond_z, own, to_right, to_left):
+def stage_kernel(
+    in0, in1, in2, in3, own, to_right, to_left, labels, cond_x, cond_y, cond_z, sems
+):
+    copies = fetch(((in0, labels), (in1, cond_x), (in2, cond_y), (in3, cond_z)), sems)
     last_x = lax.axis_index("gx") == lax.axis_size("gx") - 1
     last_y = lax.axis_index("gy") == lax.axis_size("gy") - 1
     shape = (R0, 8, 128)
     row = lax.broadcasted_iota(jnp.int32, shape, 0)
     for a, ref in enumerate((labels, cond_x, cond_y, cond_z)):
+        copies[a].wait()
         for b in range(4):
             value = jnp.stack([ref[4 * s + b].astype(F32) for s in range(8)])
             value = jnp.swapaxes(value, 0, 1)
@@ -252,7 +256,7 @@
     planes(1, N0 - 1, operator0, 4)
     src, dst = va, vb
     for s in range(NU - 1):
-        sweep(src, dst, f, g, fx, fy, fz, 2 + s, N0 - 2 - s)
+        sweep(src, dst, f, g, fx, fy, fz, 2 + s, N0 - 2 - s, N0 // 2 - 2 - s)
         src, dst = dst, src
 
     part = pl.ds(H0 - 4, 24)
@@ -417,7 +421,7 @@
             out[c, s] = rhs[s]
 
 
-PAD3 = 8
+PAD3 = 16
 
 
 def turned(parts):
@@ -432,37 +436,59 @@
     return results
 
 
-def solve_kernel(
-    count, gathered, own, left, right, left_far, right_far, out, ops3, f3, va3, vb3
-):
-    rows = 2 * count
-    lo, hi = PAD3, PAD3 + rows
+def spread3_kernel(count, own, left, right, left_far, right_far, out, ops3, sems):
+    def unpack(i, carry):
+        values = turned([ref[i] for ref in (left_far, left, own, right, right_far)])
+        for m, value in enumerate(values):
+            ops3[m // 2, 2 * i + m % 2] = scale_of(value) if m >= 6 else value
+        return carry
+
+    lax.fori_loop(0, count, unpack, 0)
+    for copy in fetch(((ops3, out),), sems):
+        copy.wait()
+
+
+def solve_kernel(count, gathered, in_ops3, out, ops3, f3, va3, vb3, sems):
+    lo, hi = PAD3, PAD3 + 2 * count
+    inner = pl.ds(lo, 2 * count)
+    copies = fetch([(in_ops3.at[a], ops3.at[a, inner]) for a in range(4)], sems)
     x3, y3, z3, g3 = (ops3.at[a] for a in range(4))
-    for ref in (va3, vb3, x3):
+    for ref in (x3, y3, z3, g3, va3, vb3, f3):
         ref[0:lo] = jnp.zeros((PAD3, NZ, 128), F32)
         ref[hi : hi + PAD3] = jnp.zeros((PAD3, NZ, 128), F32)
 
     def unpack(i, carry):
         p = lo + 2 * i
-        for m, value in enumerate(turned([ref[i] for ref in (left_far, left, own, right, right_far)])):
-            ops3[m // 2, p + m % 2] = scale_of(value) if m >= 6 else value
         for m, value in enumerate(turned([gathered[i, s] for s in range(5)])):
             part = slice(8 * (m // 2), 8 * (m // 2) + 8)
             f3[p + m % 2, part] = value
-            va3[p + m % 2, part] = value * g3[p + m % 2, part]
         return carry
 
     lax.fori_loop(0, count, unpack, 0)
+    for copy in copies:
+        copy.wait()
+
+    def first(p):
+        va3[p] = g3[p] * f3[p]
+
+    planes(lo, hi, first)
 
     def two(i, carry):
         sweep(va3, vb3, f3, g3, x3, y3, z3, lo, hi, 32)
         sweep(vb3, va3, f3, g3, x3, y3, z3, lo, hi, 32)
         return carry
 
-    lax.fori_loop(0, (COARSE_SWEEPS - 1) // 2, two, 0)
-    sweep(va3, vb3, f3, g3, x3, y3, z3, lo, hi, 32)
+    last = 11
+    lax.fori_loop(0, (COARSE_SWEEPS - 1 - last) // 2, two, 0)
     start = lo + 2 * lax.axis_index("gx") - 4
-    out[...] = vb3[pl.ds(start, 10)]
+    src, dst = va3, vb3
+    for k in range(last - 1, -1, -1):
+        for i in range(10 + 2 * k):
+            p = start - k + i
+            v, s = neighbours(src, x3, y3, z3, p)
+            dst[p] = (1.0 - OMEGA) * v + g3[p] * (f3[p] + s)
+        src, dst = dst, src
+    out[...] = src[pl.ds(start, 10)]
 
 
 def up_kernel(
@@ -541,7 +567,7 @@
             va0[i] = v0[i] + jnp.where(g0[i] > 0.0, coarse[k // 2], 0.0)
     src, dst = va0, vb0
     for s in range(NU):
-        sweep(src, dst, f0, g0, x0, y0, z0, 1 + s, 23 - s)
+        sweep(src, dst, f0, g0, x0, y0, z0, 1 + s, 23 - s, 11 - s)
         src, dst = dst, src
     for b in range(4):
         value = jnp.swapaxes(src[4:20, 8 * b : 8 * b + 8, 0:128], 0, 1)
@@ -559,11 +585,13 @@
     count = lax.axis_size("gx")
     side = (NZ, 128)
     wide = (N0, NZ, 256)
+    fields = (labels, conduct_x, conduct_y, conduct_z)
     own, to_right, to_left = call(
         stage_kernel,
-        (labels, conduct_x, conduct_y, conduct_z),
+        [pltpu.with_memory_space_constraint(x, pltpu.HBM) for x in fields],
         [(4, R0, *side), (4 * H0 - 2, *side), (4 * H0 - 3, *side)],
-        limit=10,
+        [pltpu.VMEM(x.shape, x.dtype) for x in fields] + [pltpu.SemaphoreType.DMA((4,))],
+        apart=(0, 1, 2, 3),
     )
     behind = shift(to_right, "gx", 1)
     ahead = shift(to_left, "gx", -1)
@@ -609,11 +637,20 @@
     rhs3 = lax.all_to_all(rhs3, "gx", 0, 0)
     behind3, ahead3 = shift(behind2, "gx", 1), shift(ahead2, "gx", -1)
     rows3 = 2 * count + 2 * PAD3
+    (ops3,) = call(
+        functools.partial(spread3_kernel, count),
+        near,
+        [(4, 2 * count, *side)],
+        [(4, 2 * count, *side), pltpu.SemaphoreType.DMA((1,))],
+        apart_outs=(0,),
+    )
     (e3,) = call(
         functools.partial(solve_kernel, count),
-        (rhs3, *near),
+        (rhs3, pltpu.with_memory_space_constraint(ops3, pltpu.HBM)),
         [(10, *side)],
-        [(4, rows3, *side)] + [(rows3, *side)] * 3,
+        [(4, rows3, *side)] + [(rows3, *side)] * 3 + [pltpu.SemaphoreType.DMA((4,))],
+        limit=14,
+        apart=(1,),
     )
     keep0, ops1, f1 = (pltpu.with_memory_space_constraint(x, pltpu.HBM) for x in (keep0, ops1, f1))
     (out,) = call(

time: 143 us -> 141 us (0.986); the launches traced: 141 us -> 140 us
  Pallas kernels: 32 us -> 35.9 us
  local copies, waits for them, and re-layouts: 3.66 us -> 0 us
  waiting for transfers between devices: 29.9 us -> 27.4 us
  starting transfers between devices: 61.9 us -> 64.1 us
    pallas_call x8 -> x9, Pallas kernels: 32 us -> 35.9 us  [call(): pl.pallas_call(kernel, out_shape=[pltpu.HBM(s, F32) if i in apart_outs el...]
    unnamed x8 -> x0, local copies, waits for them, and re-layouts: 3.66 us -> none
    ppermute x16, waiting for transfers between devices: 29.9 us -> 27.4 us  [shift(): return lax.ppermute(value, axis, route)]
    ppermute x16, starting transfers between devices: 57.4 us -> 59.7 us  [shift(): return lax.ppermute(value, axis, route)]
  transfers between devices with their start and end apart: 17 -> 17, of which waited for: 6 -> 6; matrix products, arithmetic and copies ran while one was open for 0% -> 0% of each run, Pallas kernels for 8% -> 9%
where the time goes in v6:
time: 141 us; the launch traced here: 140 us
  starting transfers between devices  64.1 us (45%)
  Pallas kernels  35.9 us (25%)
  waiting for transfers between devices  27.4 us (19%)
  blocking collectives  12.6 us (9%)
    ppermute x16, starting transfers between devices, shift(): return lax.ppermute(value, axis, route)  59.7 us
    pallas_call x9, Pallas kernels, call(): pl.pallas_call(kernel, out_shape=[pltpu.HBM(s, F32) if i in apart_outs el...  35.9 us
    ppermute x16, waiting for transfers between devices, shift(): return lax.ppermute(value, axis, route)  27.4 us
    all_to_all x1, blocking collectives, body(): all3 = lax.all_to_all(own3, 'gx', 0, 0)  12.6 us
    all_to_all x1, starting transfers between devices, body(): rhs3 = lax.all_to_all(rhs3, 'gx', 0, 0)  4.39 us
  transfers between devices with their start and end apart: 17, of which 6 were waited for; matrix products, arithmetic and copies ran while one was open for 0% of the time, Pallas kernels for 9%

profile of v6, /device:TPU:130, one launch (start us, length us, event | category | flops | bytes accessed | tf_op | source)
XLA Modules:
  0.0 140.5 jit_solution(2492876058138597974)
XLA Ops:
  0.0 1.4 shard_map.46
  1.4 3.5 %collective-permute-start = (f32[50,32,128]{2,1,0:T(8,128)S(1)}, f32[50,32,128]{2,1,0:T(8,128)S(1)}, u32[]{:S(2)}, u32[]{:S(2)}) collective-permute-start(f32[50,32,128]{2,1,0:T(8,128)S(1)} %get-tuple-element.26), channel_id=1, source_target_pairs={{0,16},{16,32},{32,48},{48,64},{64,80},{80,96},{96,112},{112,128},... | collective-permute-start | bytes 2457608 | tf_op jit(solution)/shard_map/ppermute | solution.py:581
  4.9 4.5 %collective-permute-start.1 = (f32[49,32,128]{2,1,0:T(8,128)S(1)}, f32[49,32,128]{2,1,0:T(8,128)S(1)}, u32[]{:S(2)}, u32[]{:S(2)}) collective-permute-start(f32[49,32,128]{2,1,0:T(8,128)S(1)} %get-tuple-element.27), channel_id=1, source_target_pairs={{16,0},{32,16},{48,32},{64,48},{80,64},{96,80},{112,96},{128,112},... | collective-permute-start | bytes 2408456 | tf_op jit(solution)/shard_map/ppermute | solution.py:581
  9.4 16.8 %collective-permute-done.1.ahead = f32[49,32,128]{2,1,0:T(8,128)S(1)} collective-permute-done((f32[49,32,128]{2,1,0:T(8,128)S(1)}, f32[49,32,128]{2,1,0:T(8,128)S(1)}, u32[]{:S(2)}, u32[]{:S(2)}) %collective-permute-start.1) | collective-permute-done | bytes 802848 | tf_op jit(solution)/shard_map/ppermute | solution.py:581
  26.2 0.7 shard_map.47
  26.9 1.9 %collective-permute-start.2 = (f32[4,6,32,128]{3,2,1,0:T(8,128)S(1)}, f32[4,6,32,128]{3,2,1,0:T(8,128)S(1)}, u32[]{:S(2)}, u32[]{:S(2)}) collective-permute-start(f32[4,6,32,128]{3,2,1,0:T(8,128)S(1)} %get-tuple-element.28), channel_id=1, source_target_pairs={{0,1},{1,2},{2,3},{3,4},{4,5},{5,6},{6,7},{7,8},{8,9},{9,10},{10,1... | collective-permute-start | bytes 1179656 | tf_op jit(solution)/shard_map/ppermute | solution.py:581
  28.8 4.9 %collective-permute-start.3 = (f32[4,6,32,128]{3,2,1,0:T(8,128)S(1)}, f32[4,6,32,128]{3,2,1,0:T(8,128)S(1)}, u32[]{:S(2)}, u32[]{:S(2)}) collective-permute-start(f32[4,6,32,128]{3,2,1,0:T(8,128)S(1)} %get-tuple-element.29), channel_id=1, source_target_pairs={{1,0},{2,1},{3,2},{4,3},{5,4},{6,5},{7,6},{8,7},{9,8},{10,9},{11,1... | collective-permute-start | bytes 1179656 | tf_op jit(solution)/shard_map/ppermute | solution.py:581
  33.7 3.5 %collective-permute-done.2.from_left = f32[4,6,32,128]{3,2,1,0:T(8,128)S(1)} collective-permute-done((f32[4,6,32,128]{3,2,1,0:T(8,128)S(1)}, f32[4,6,32,128]{3,2,1,0:T(8,128)S(1)}, u32[]{:S(2)}, u32[]{:S(2)}) %collective-permute-start.2) | collective-permute-done | bytes 393248 | tf_op jit(solution)/shard_map/ppermute | solution.py:581
  37.2 1.8 %collective-permute-done.3.from_right = f32[4,6,32,128]{3,2,1,0:T(8,128)S(1)} collective-permute-done((f32[4,6,32,128]{3,2,1,0:T(8,128)S(1)}, f32[4,6,32,128]{3,2,1,0:T(8,128)S(1)}, u32[]{:S(2)}, u32[]{:S(2)}) %collective-permute-start.3) | collective-permute-done | bytes 393248 | tf_op jit(solution)/shard_map/ppermute | solution.py:581
  38.9 12.1 %shard_map.48 = (f32[6,24,32,256]{3,2,1,0:T(8,128)}, f32[5,20,32,128]{3,2,1,0:T(8,128)}, f32[20,32,128]{2,1,0:T(8,128)}, f32[8,32,128]{2,1,0:T(8,128)S(1)}, f32[...) custom-call(f32[4,16,32,128]{3,2,1,0:T(8,128)S(1)} %get-tuple-elemen, ...), custom_call_target="tpu_custom_call" | custom-call | tf_op jit(solution)/shard_map/pallas_call | solution.py:33
  51.0 2.0 %collective-permute-start.4 = (f32[11,32,128]{2,1,0:T(8,128)S(1)}, f32[11,32,128]{2,1,0:T(8,128)S(1)}, u32[]{:S(2)}, u32[]{:S(2)}) collective-permute-start(f32[11,32,128]{2,1,0:T(8,128)S(1)} %get-tuple-element.30.own2), channel_id=1, source_target_pairs={{0,1},{1,2},{2,3},{3,4},{4,5},{5,6},{6,7},{7,8},{8,9},{9,10},{10,1... | collective-permute-start | bytes 540680 | tf_op jit(solution)/shard_map/ppermute | solution.py:581
  53.0 5.0 %collective-permute-start.5 = (f32[11,32,128]{2,1,0:T(8,128)S(1)}, f32[11,32,128]{2,1,0:T(8,128)S(1)}, u32[]{:S(2)}, u32[]{:S(2)}) collective-permute-start(f32[11,32,128]{2,1,0:T(8,128)S(1)} %get-tuple-element.33), channel_id=1, source_target_pairs={{1,0},{2,1},{3,2},{4,3},{5,4},{6,5},{7,6},{8,7},{9,8},{10,9},{11,1... | collective-permute-start | bytes 540680 | tf_op jit(solution)/shard_map/ppermute | solution.py:581
  58.0 1.2 collective-permute-done.4.left
  59.2 1.8 %collective-permute-done.5.right = f32[11,32,128]{2,1,0:T(8,128)S(1)} collective-permute-done((f32[11,32,128]{2,1,0:T(8,128)S(1)}, f32[11,32,128]{2,1,0:T(8,128)S(1)}, u32[]{:S(2)}, u32[]{:S(2)}) %collective-permute-start.5) | collective-permute-done | bytes 180256 | tf_op jit(solution)/shard_map/ppermute | solution.py:581
  61.2 3.4 %collective-permute-start.6 = (f32[17,32,128]{2,1,0:T(8,128)S(1)}, f32[17,32,128]{2,1,0:T(8,128)S(1)}, u32[]{:S(2)}, u32[]{:S(2)}) collective-permute-start(f32[17,32,128]{2,1,0:T(8,128)S(1)} %get-tuple-element.34), channel_id=1, source_target_pairs={{0,16},{16,32},{32,48},{48,64},{64,80},{80,96},{96,112},{112,128},... | collective-permute-start | bytes 835592 | tf_op jit(solution)/shard_map/ppermute | solution.py:581
  64.6 5.0 %collective-permute-start.7 = (f32[17,32,128]{2,1,0:T(8,128)S(1)}, f32[17,32,128]{2,1,0:T(8,128)S(1)}, u32[]{:S(2)}, u32[]{:S(2)}) collective-permute-start(f32[17,32,128]{2,1,0:T(8,128)S(1)} %get-tuple-element.36), channel_id=1, source_target_pairs={{16,0},{32,16},{48,32},{64,48},{80,64},{96,80},{112,96},{128,112},... | collective-permute-start | bytes 835592 | tf_op jit(solution)/shard_map/ppermute | solution.py:581
  69.6 12.6 %all_to_all.10.ops3 = f32[16,32,128]{2,1,0:T(8,128)S(1)} all-to-all(f32[16,32,128]{2,1,0:T(8,128)S(1)} %get-tuple-element.37), channel_id=1, replica_groups=mesh['gx'=16,'gy'=16] {'gx'}, dimensions={0} | all-to-all | bytes 524288 | tf_op jit(solution)/shard_map/all_to_all | solution.py:619
  82.3 0.7 shard_map.50
  82.9 1.9 %collective-permute-start.8 = (f32[17,32,128]{2,1,0:T(8,128)S(1)}, f32[17,32,128]{2,1,0:T(8,128)S(1)}, u32[]{:S(2)}, u32[]{:S(2)}) collective-permute-start(f32[17,32,128]{2,1,0:T(8,128)S(1)} %get-tuple-element.38.own), channel_id=1, source_target_pairs={{0,1},{1,2},{2,3},{3,4},{4,5},{5,6},{6,7},{7,8},{8,9},{9,10},{10,1... | collective-permute-start | bytes 835592 | tf_op jit(solution)/shard_map/ppermute | solution.py:581
  84.9 4.9 %collective-permute-start.9 = (f32[17,32,128]{2,1,0:T(8,128)S(1)}, f32[17,32,128]{2,1,0:T(8,128)S(1)}, u32[]{:S(2)}, u32[]{:S(2)}) collective-permute-start(f32[17,32,128]{2,1,0:T(8,128)S(1)} %get-tuple-element.38.own), channel_id=1, source_target_pairs={{1,0},{2,1},{3,2},{4,3},{5,4},{6,5},{7,6},{8,7},{9,8},{10,9},{11,1... | collective-permute-start | bytes 835592 | tf_op jit(solution)/shard_map/ppermute | solution.py:581
  89.7 2.3 %collective-permute-done.8.left = f32[17,32,128]{2,1,0:T(8,128)S(1)} collective-permute-done((f32[17,32,128]{2,1,0:T(8,128)S(1)}, f32[17,32,128]{2,1,0:T(8,128)S(1)}, u32[]{:S(2)}, u32[]{:S(2)}) %collective-permute-start.8) | collective-permute-done | bytes 278560 | tf_op jit(solution)/shard_map/ppermute | solution.py:581
  92.0 1.9 %collective-permute-start.10 = (f32[17,32,128]{2,1,0:T(8,128)S(1)}, f32[17,32,128]{2,1,0:T(8,128)S(1)}, u32[]{:S(2)}, u32[]{:S(2)}) collective-permute-start(f32[17,32,128]{2,1,0:T(8,128)S(1)} %collective-permute-done.8.left), channel_id=1, source_target_pairs={{0,1},{1,2},{2,3},{3,4},{4,5},{5,6},{6,7},{7,8},{8,9},{9,10},{10,1... | collective-permute-start | bytes 835592 | tf_op jit(solution)/shard_map/ppermute | solution.py:581
  93.9 4.9 %collective-permute-start.11 = (f32[17,32,128]{2,1,0:T(8,128)S(1)}, f32[17,32,128]{2,1,0:T(8,128)S(1)}, u32[]{:S(2)}, u32[]{:S(2)}) collective-permute-start(f32[17,32,128]{2,1,0:T(8,128)S(1)} %collective-permute-done.9.right), channel_id=1, source_target_pairs={{1,0},{2,1},{3,2},{4,3},{5,4},{6,5},{7,6},{8,7},{9,8},{10,9},{11,1... | collective-permute-start | bytes 835592 | tf_op jit(solution)/shard_map/ppermute | solution.py:581
  98.8 2.3 %collective-permute-start.12 = (f32[10,32,128]{2,1,0:T(8,128)S(1)}, f32[10,32,128]{2,1,0:T(8,128)S(1)}, u32[]{:S(2)}, u32[]{:S(2)}) collective-permute-start(f32[10,32,128]{2,1,0:T(8,128)S(1)} %get-tuple-element.39), channel_id=1, source_target_pairs={{0,16},{16,32},{32,48},{48,64},{64,80},{80,96},{96,112},{112,128},... | collective-permute-start | bytes 491528 | tf_op jit(solution)/shard_map/ppermute | solution.py:581
  101.1 5.6 %collective-permute-start.14 = (f32[10,32,128]{2,1,0:T(8,128)S(1)}, f32[10,32,128]{2,1,0:T(8,128)S(1)}, u32[]{:S(2)}, u32[]{:S(2)}) collective-permute-start(f32[10,32,128]{2,1,0:T(8,128)S(1)} %get-tuple-element.40), channel_id=1, source_target_pairs={{16,0},{32,16},{48,32},{64,48},{80,64},{96,80},{112,96},{128,112},... | collective-permute-start | bytes 491528 | tf_op jit(solution)/shard_map/ppermute | solution.py:581
  106.8 0.8 shard_map.51
  107.6 4.4 %all-to-all-start.1 = ((f32[16,5,8,128]{3,2,1,0:T(8,128)}), f32[16,5,8,128]{3,2,1,0:T(8,128)S(1)}, u32[]{:S(2)}, u32[]{:S(2)}) async-start(f32[16,5,8,128]{3,2,1,0:T(8,128)} %shard_map.51), calls=%async_computation.1 | async-start | bytes 655360 | tf_op jit(solution)/shard_map/all_to_all | solution.py:637
  112.0 3.4 %collective-permute-start.13 = (f32[10,32,128]{2,1,0:T(8,128)S(1)}, f32[10,32,128]{2,1,0:T(8,128)S(1)}, u32[]{:S(2)}, u32[]{:S(2)}) collective-permute-start(f32[10,32,128]{2,1,0:T(8,128)S(1)} %collective-permute-done.12.in_behind2), channel_id=1, source_target_pairs={{0,16},{16,32},{32,48},{48,64},{64,80},{80,96},{96,112},{112,128},... | collective-permute-start | bytes 491528 | tf_op jit(solution)/shard_map/ppermute | solution.py:581
  115.3 4.8 %collective-permute-start.15 = (f32[10,32,128]{2,1,0:T(8,128)S(1)}, f32[10,32,128]{2,1,0:T(8,128)S(1)}, u32[]{:S(2)}, u32[]{:S(2)}) collective-permute-start(f32[10,32,128]{2,1,0:T(8,128)S(1)} %collective-permute-done.14.in_ahead2), channel_id=1, source_target_pairs={{16,0},{32,16},{48,32},{64,48},{80,64},{96,80},{112,96},{128,112},... | collective-permute-start | bytes 491528 | tf_op jit(solution)/shard_map/ppermute | solution.py:581
  120.1 4.2 %shard_map.52.in_ops3 = f32[4,32,32,128]{3,2,1,0:T(8,128)} custom-call(f32[17,32,128]{2,1,0:T(8,128)S(1)} %get-tuple-element.38.own, f32[17,32,128]{2,1,0:T(8,128)S(1)} %collective-permute-done.8.left, f32[17,32,128]{2,1,0:T(8,128)S(1)} %collective-permute-done.9.right, f32[17,32,128]{2,1,0:T(8,128)S(1)} %collective-permute-done.10.left_far, ...), custom_call_target="tpu_custom_call" | custom-call | tf_op jit(solution)/shard_map/pallas_call | solution.py:33
  124.3 8.3 %shard_map.53.e3 = f32[10,32,128]{2,1,0:T(8,128)S(1)} custom-call(f32[16,5,8,128]{3,2,1,0:T(8,128)S(1)} %all-to-all-done.1.gathered, f32[4,32,32,128]{3,2,1,0:T(8,128)} %shard_map.52.in_ops3), custom_call_target="tpu_custom_call" | custom-call | tf_op jit(solution)/shard_map/pallas_call | solution.py:33
  132.7 7.6 %shard_map.54 = f32[32,16,128]{2,1,0:T(8,128)} custom-call(f32[10,32,128]{2,1,0:T(8,128)S(1)} %shard_map.53.e3, f32[10,32,128]{2,1,0:T(8,128)S(1)} %collective-permute-done.13.in_behind3, f32[10,32,128]{2,1,0:T(8,128)S(1)} %collective-permute-done.12.in_behind2, f32[17,32,128]{2,1,0:T(8,128)S(1)} %collective-permute-done.6.behind.in_behind, ...), custom_call_target="tpu_custom_call" | custom-call | tf_op jit(solution)/shard_map/pallas_call | solution.py:33
  (12 shorter events, 0.2 us)
Async XLA Ops:
  1.4 24.8 %collective-permute-start = (f32[50,32,128]{2,1,0:T(8,128)S(1)}, f32[50,32,128]{2,1,0:T(8,128)S(1)}, u32[]{:S(2)}, u32[]{:S(2)}) collective-permute-start(f32[50,32,128]{2,1,0:T(8,128)S(1)} %get-tuple-element.26), channel_id=1, source_target_pairs={{0,16},{16,32},{32,48},{48,64},{64,80},{80,96},{96,112},{112,128},... | collective-permute-start | bytes 2457608 | tf_op jit(solution)/shard_map/ppermute | solution.py:581
  4.9 21.3 %collective-permute-start.1 = (f32[49,32,128]{2,1,0:T(8,128)S(1)}, f32[49,32,128]{2,1,0:T(8,128)S(1)}, u32[]{:S(2)}, u32[]{:S(2)}) collective-permute-start(f32[49,32,128]{2,1,0:T(8,128)S(1)} %get-tuple-element.27), channel_id=1, source_target_pairs={{16,0},{32,16},{48,32},{64,48},{80,64},{96,80},{112,96},{128,112},... | collective-permute-start | bytes 2408456 | tf_op jit(solution)/shard_map/ppermute | solution.py:581
  26.9 10.3 %collective-permute-start.2 = (f32[4,6,32,128]{3,2,1,0:T(8,128)S(1)}, f32[4,6,32,128]{3,2,1,0:T(8,128)S(1)}, u32[]{:S(2)}, u32[]{:S(2)}) collective-permute-start(f32[4,6,32,128]{3,2,1,0:T(8,128)S(1)} %get-tuple-element.28), channel_id=1, source_target_pairs={{0,1},{1,2},{2,3},{3,4},{4,5},{5,6},{6,7},{7,8},{8,9},{9,10},{10,1... | collective-permute-start | bytes 1179656 | tf_op jit(solution)/shard_map/ppermute | solution.py:581
  28.8 10.1 %collective-permute-start.3 = (f32[4,6,32,128]{3,2,1,0:T(8,128)S(1)}, f32[4,6,32,128]{3,2,1,0:T(8,128)S(1)}, u32[]{:S(2)}, u32[]{:S(2)}) collective-permute-start(f32[4,6,32,128]{3,2,1,0:T(8,128)S(1)} %get-tuple-element.29), channel_id=1, source_target_pairs={{1,0},{2,1},{3,2},{4,3},{5,4},{6,5},{7,6},{8,7},{9,8},{10,9},{11,1... | collective-permute-start | bytes 1179656 | tf_op jit(solution)/shard_map/ppermute | solution.py:581
  51.0 8.2 %collective-permute-start.4 = (f32[11,32,128]{2,1,0:T(8,128)S(1)}, f32[11,32,128]{2,1,0:T(8,128)S(1)}, u32[]{:S(2)}, u32[]{:S(2)}) collective-permute-start(f32[11,32,128]{2,1,0:T(8,128)S(1)} %get-tuple-element.30.own2), channel_id=1, source_target_pairs={{0,1},{1,2},{2,3},{3,4},{4,5},{5,6},{6,7},{7,8},{8,9},{9,10},{10,1... | collective-permute-start | bytes 540680 | tf_op jit(solution)/shard_map/ppermute | solution.py:581
  53.0 8.0 %collective-permute-start.5 = (f32[11,32,128]{2,1,0:T(8,128)S(1)}, f32[11,32,128]{2,1,0:T(8,128)S(1)}, u32[]{:S(2)}, u32[]{:S(2)}) collective-permute-start(f32[11,32,128]{2,1,0:T(8,128)S(1)} %get-tuple-element.33), channel_id=1, source_target_pairs={{1,0},{2,1},{3,2},{4,3},{5,4},{6,5},{7,6},{8,7},{9,8},{10,9},{11,1... | collective-permute-start | bytes 540680 | tf_op jit(solution)/shard_map/ppermute | solution.py:581
  61.2 21.1 %collective-permute-start.6 = (f32[17,32,128]{2,1,0:T(8,128)S(1)}, f32[17,32,128]{2,1,0:T(8,128)S(1)}, u32[]{:S(2)}, u32[]{:S(2)}) collective-permute-start(f32[17,32,128]{2,1,0:T(8,128)S(1)} %get-tuple-element.34), channel_id=1, source_target_pairs={{0,16},{16,32},{32,48},{48,64},{64,80},{80,96},{96,112},{112,128},... | collective-permute-start | bytes 835592 | tf_op jit(solution)/shard_map/ppermute | solution.py:581
  64.6 17.7 %collective-permute-start.7 = (f32[17,32,128]{2,1,0:T(8,128)S(1)}, f32[17,32,128]{2,1,0:T(8,128)S(1)}, u32[]{:S(2)}, u32[]{:S(2)}) collective-permute-start(f32[17,32,128]{2,1,0:T(8,128)S(1)} %get-tuple-element.36), channel_id=1, source_target_pairs={{16,0},{32,16},{48,32},{64,48},{80,64},{96,80},{112,96},{128,112},... | collective-permute-start | bytes 835592 | tf_op jit(solution)/shard_map/ppermute | solution.py:581
  82.9 9.1 %collective-permute-start.8 = (f32[17,32,128]{2,1,0:T(8,128)S(1)}, f32[17,32,128]{2,1,0:T(8,128)S(1)}, u32[]{:S(2)}, u32[]{:S(2)}) collective-permute-start(f32[17,32,128]{2,1,0:T(8,128)S(1)} %get-tuple-element.38.own), channel_id=1, source_target_pairs={{0,1},{1,2},{2,3},{3,4},{4,5},{5,6},{6,7},{7,8},{8,9},{9,10},{10,1... | collective-permute-start | bytes 835592 | tf_op jit(solution)/shard_map/ppermute | solution.py:581
  84.9 9.1 %collective-permute-start.9 = (f32[17,32,128]{2,1,0:T(8,128)S(1)}, f32[17,32,128]{2,1,0:T(8,128)S(1)}, u32[]{:S(2)}, u32[]{:S(2)}) collective-permute-start(f32[17,32,128]{2,1,0:T(8,128)S(1)} %get-tuple-element.38.own), channel_id=1, source_target_pairs={{1,0},{2,1},{3,2},{4,3},{5,4},{6,5},{7,6},{8,7},{9,8},{10,9},{11,1... | collective-permute-start | bytes 835592 | tf_op jit(solution)/shard_map/ppermute | solution.py:581
  92.0 14.8 %collective-permute-start.10 = (f32[17,32,128]{2,1,0:T(8,128)S(1)}, f32[17,32,128]{2,1,0:T(8,128)S(1)}, u32[]{:S(2)}, u32[]{:S(2)}) collective-permute-start(f32[17,32,128]{2,1,0:T(8,128)S(1)} %collective-permute-done.8.left), channel_id=1, source_target_pairs={{0,1},{1,2},{2,3},{3,4},{4,5},{5,6},{6,7},{7,8},{8,9},{9,10},{10,1... | collective-permute-start | bytes 835592 | tf_op jit(solution)/shard_map/ppermute | solution.py:581
  93.9 12.8 %collective-permute-start.11 = (f32[17,32,128]{2,1,0:T(8,128)S(1)}, f32[17,32,128]{2,1,0:T(8,128)S(1)}, u32[]{:S(2)}, u32[]{:S(2)}) collective-permute-start(f32[17,32,128]{2,1,0:T(8,128)S(1)} %collective-permute-done.9.right), channel_id=1, source_target_pairs={{1,0},{2,1},{3,2},{4,3},{5,4},{6,5},{7,6},{8,7},{9,8},{10,9},{11,1... | collective-permute-start | bytes 835592 | tf_op jit(solution)/shard_map/ppermute | solution.py:581
  98.8 13.2 %collective-permute-start.12 = (f32[10,32,128]{2,1,0:T(8,128)S(1)}, f32[10,32,128]{2,1,0:T(8,128)S(1)}, u32[]{:S(2)}, u32[]{:S(2)}) collective-permute-start(f32[10,32,128]{2,1,0:T(8,128)S(1)} %get-tuple-element.39), channel_id=1, source_target_pairs={{0,16},{16,32},{32,48},{48,64},{64,80},{80,96},{96,112},{112,128},... | collective-permute-start | bytes 491528 | tf_op jit(solution)/shard_map/ppermute | solution.py:581
  101.1 14.2 %collective-permute-start.14 = (f32[10,32,128]{2,1,0:T(8,128)S(1)}, f32[10,32,128]{2,1,0:T(8,128)S(1)}, u32[]{:S(2)}, u32[]{:S(2)}) collective-permute-start(f32[10,32,128]{2,1,0:T(8,128)S(1)} %get-tuple-element.40), channel_id=1, source_target_pairs={{16,0},{32,16},{48,32},{64,48},{80,64},{96,80},{112,96},{128,112},... | collective-permute-start | bytes 491528 | tf_op jit(solution)/shard_map/ppermute | solution.py:581
  107.6 16.8 %all-to-all-start.1 = ((f32[16,5,8,128]{3,2,1,0:T(8,128)}), f32[16,5,8,128]{3,2,1,0:T(8,128)S(1)}, u32[]{:S(2)}, u32[]{:S(2)}) async-start(f32[16,5,8,128]{3,2,1,0:T(8,128)} %shard_map.51), calls=%async_computation.1 | async-start | bytes 655360 | tf_op jit(solution)/shard_map/all_to_all | solution.py:637
  112.0 20.7 %collective-permute-start.13 = (f32[10,32,128]{2,1,0:T(8,128)S(1)}, f32[10,32,128]{2,1,0:T(8,128)S(1)}, u32[]{:S(2)}, u32[]{:S(2)}) collective-permute-start(f32[10,32,128]{2,1,0:T(8,128)S(1)} %collective-permute-done.12.in_behind2), channel_id=1, source_target_pairs={{0,16},{16,32},{32,48},{48,64},{64,80},{80,96},{96,112},{112,128},... | collective-permute-start | bytes 491528 | tf_op jit(solution)/shard_map/ppermute | solution.py:581
  115.3 17.3 %collective-permute-start.15 = (f32[10,32,128]{2,1,0:T(8,128)S(1)}, f32[10,32,128]{2,1,0:T(8,128)S(1)}, u32[]{:S(2)}, u32[]{:S(2)}) collective-permute-start(f32[10,32,128]{2,1,0:T(8,128)S(1)} %collective-permute-done.14.in_ahead2), channel_id=1, source_target_pairs={{16,0},{32,16},{48,32},{64,48},{80,64},{96,80},{112,96},{128,112},... | collective-permute-start | bytes 491528 | tf_op jit(solution)/shard_map/ppermute | solution.py:581

commit v7 on v6

--- a/solution.py
+++ b/solution.py
@@ -383,7 +383,7 @@
 
 
 def middle_kernel(
-    count, behind, own, ahead, ops3, message, further, nearer, f, fx, fy, fz, d, g, va, vb
+    count, behind, own, ahead, ops3, message, f, fx, fy, fz, d, g, va, vb
 ):
     for j in range(12):
         source = (behind, own, ahead)[j // 4]
@@ -410,8 +410,6 @@
     message[count, 8:] = jnp.zeros((NZ - 8, 128), F32)
     for i in range(count):
         message[i] = ops3[i]
-    further[...] = behind[0:10]
-    nearer[...] = ahead[0:10]
 
 
 def near_kernel(count, own, left, right, left_far, right_far, out):
@@ -492,28 +490,26 @@
 
 
 def up_kernel(
-    e3, in_behind3, in_behind2, in_behind, in_own, in_ahead, in_ahead2, in_ahead3,
-    in_joined1, in_f1, in_ops1, in_keep0,
+    e3, all2, in_behind, in_ahead, in_joined1, in_f1, in_ops1, in_keep0,
     out,
     f2, x2, y2, z2, d2, g2, va2, vb2, f1, va1, vb1, va0, vb0,
-    behind3, behind2, behind, own, ahead, ahead2, ahead3, joined1, ops1, keep0, sems,
+    wide2, behind, ahead, joined1, ops1, keep0, sems,
 ):
-    pairs = [
-        (in_behind3, behind3), (in_behind2, behind2), (in_behind, behind), (in_own, own),
-        (in_ahead, ahead), (in_ahead2, ahead2), (in_ahead3, ahead3),
-        (in_joined1, joined1), (in_f1, f1), (in_ops1, ops1), (in_keep0, keep0),
-    ]
+    me, ends = lax.axis_index("gx"), lax.axis_size("gx") - 1
+    pairs = [(all2.at[jnp.clip(me + n - 3, 0, ends)], wide2.at[n]) for n in range(7)]
+    pairs += [(in_behind, behind), (in_ahead, ahead), (in_joined1, joined1)]
+    pairs += [(in_f1, f1), (in_ops1, ops1), (in_keep0, keep0)]
     copies = fetch(pairs, sems)
-    sources = [(behind3, 1)]
-    sources += [(ref, h) for ref in (behind2, behind, own, ahead, ahead2) for h in range(2)]
-    sources += [(ahead3, 0)]
-    for n, (source, h) in enumerate(sources):
-        if n % 2 or n == 0:
-            copies[(n + 1) // 2].wait()
-        for a, ref in enumerate((f2, x2, y2, z2, d2)):
-            value = source[2 * a + h]
-            ref[2 * n] = value
-            ref[2 * n + 1] = roll(value, 64, 1)
+    for n in range(7):
+        copies[n].wait()
+        inside = (me + n - 3 >= 0) & (me + n - 3 <= ends)
+        for h in range(2):
+            j = 4 * n + 2 * h - 2
+            if 0 <= j < 24:
+                for a, ref in enumerate((f2, x2, y2, z2, d2)):
+                    value = jnp.where(inside, wide2[n, 2 * a + h], 0.0)
+                    ref[j] = value
+                    ref[j + 1] = roll(value, 64, 1)
 
     def operator2(j):
         g2[j] = scale_of(d2[j])
@@ -535,7 +531,7 @@
         sweep(src, dst, f2, g2, x2, y2, z2, 4 + s, 20 - s, 32)
         src, dst = dst, src
 
-    for copy in copies[7:10]:
+    for copy in copies[7:12]:
         copy.wait()
     x1, y1, z1, g1 = ops1.at[0], ops1.at[1], ops1.at[2], ops1.at[4]
     f1[1] = behind[10 + H1]
@@ -555,7 +551,7 @@
         sweep(src, dst, f1, g1, x1, y1, z1, 1 + s, N1 - 1 - s, 32)
         src, dst = dst, src
 
-    copies[10].wait()
+    copies[12].wait()
     v0, f0, g0, x0, y0, z0 = (keep0.at[a] for a in range(6))
     col = lax.broadcasted_iota(jnp.int32, (128, 256), 1)
     row = lax.broadcasted_iota(jnp.int32, (128, 256), 0)
@@ -573,6 +569,10 @@
         value = jnp.swapaxes(src[4:20, 8 * b : 8 * b + 8, 0:128], 0, 1)
         for s in range(8):
             out[4 * s + b] = value[s]
+
+
+def to_hbm(value):
+    return pltpu.with_memory_space_constraint(value, pltpu.HBM)
 
 
 def shift(value, axis, distance):
@@ -622,20 +622,19 @@
         (to_right2, own1, edge_f1, left, right),
         [(10, *side), (8, *side)] + [(11 + H1, *side)] * 2,
     )
+    all2 = lax.all_gather(joined2, "gx")
     behind, ahead = shift(to_right, "gx", 1), shift(to_left, "gx", -1)
-    message, further, nearer = call(
+    (message,) = call(
         functools.partial(middle_kernel, count),
         (behind, joined2, ahead, all3),
-        [(count + 1, *side)] + [(10, *side)] * 2,
+        [(count + 1, *side)],
         [(12, *side)] * 8,
     )
     left, right = shift(message, "gy", 1), shift(message, "gy", -1)
-    behind2, ahead2 = shift(further, "gx", 1), shift(nearer, "gx", -1)
     left_far, right_far = shift(left, "gy", 1), shift(right, "gy", -1)
     near = (message, left, right, left_far, right_far)
     (rhs3,) = call(functools.partial(near_kernel, count), near, [(count, 5, 8, 128)])
     rhs3 = lax.all_to_all(rhs3, "gx", 0, 0)
-    behind3, ahead3 = shift(behind2, "gx", 1), shift(ahead2, "gx", -1)
     rows3 = 2 * count + 2 * PAD3
     (ops3,) = call(
         functools.partial(spread3_kernel, count),
@@ -652,20 +651,20 @@
         limit=14,
         apart=(1,),
     )
-    keep0, ops1, f1 = (pltpu.with_memory_space_constraint(x, pltpu.HBM) for x in (keep0, ops1, f1))
+    kept = (all2, behind, ahead, joined1, f1, ops1, keep0)
+    in_hbm = [kept[i] if i in (1, 2, 3) else to_hbm(kept[i]) for i in range(7)]
     (out,) = call(
         up_kernel,
-        (e3, behind3, behind2, behind, joined2, ahead, ahead2, ahead3, joined1, f1, ops1, keep0),
+        (e3, *in_hbm),
         [(NZ, R0, 128)],
         [(24, *side)] * 8
         + [(N1, *side)] * 3
         + [(24, NZ, 256)] * 2
-        + [(10, *side), (10, *side), (11 + H1, *side), (10, *side)]
-        + [(11 + H1, *side), (10, *side), (10, *side), (8, *side)]
+        + [(7, 10, *side), (11 + H1, *side), (11 + H1, *side), (8, *side)]
         + [(5, N1, *side), (6, 24, NZ, 256)]
-        + [pltpu.SemaphoreType.DMA((11,))],
+        + [pltpu.SemaphoreType.DMA((13,))],
         limit=17,
-        apart=range(1, 12),
+        apart=range(1, 8),
     )
     return out
 

time: 141 us -> 151 us (1.071); the launches traced: 140 us -> 149 us
  starting transfers between devices: 64.1 us -> 49.6 us
  between operations: 0.4 us -> 13.6 us
  waiting for transfers between devices: 27.4 us -> 35.9 us
    ppermute x16 -> x12, starting transfers between devices: 59.7 us -> 43.6 us  [shift(): return lax.ppermute(value, axis, route)]
    all_to_all x1, waiting for transfers between devices: 0.01 us -> 4.4 us  [body(): rhs3 = lax.all_to_all(rhs3, 'gx', 0, 0)]
    ppermute x16 -> x12, waiting for transfers between devices: 27.4 us -> 31.5 us  [shift(): return lax.ppermute(value, axis, route)]
    all_to_all x1, starting transfers between devices: 4.39 us -> 5.98 us  [body(): rhs3 = lax.all_to_all(rhs3, 'gx', 0, 0)]
  transfers between devices with their start and end apart: 17 -> 14, of which waited for: 6 -> 9; matrix products, arithmetic and copies ran while one was open for 0% -> 0% of each run, Pallas kernels for 9% -> 10%
where the time goes in v7:
time: 151 us; the launch traced here: 149 us
  starting transfers between devices  49.6 us (33%)
  Pallas kernels  36.8 us (24%)
  waiting for transfers between devices  35.9 us (24%)
  between operations  13.6 us (9%)
  blocking collectives  12.8 us (8%)
    ppermute x12, starting transfers between devices, shift(): return lax.ppermute(value, axis, route)  43.6 us
    pallas_call x9, Pallas kernels, call(): pl.pallas_call(kernel, out_shape=[pltpu.HBM(s, F32) if i in apart_outs el...  36.8 us
    ppermute x12, waiting for transfers between devices, shift(): return lax.ppermute(value, axis, route)  31.5 us
    all_to_all x1, blocking collectives, body(): all3 = lax.all_to_all(own3, 'gx', 0, 0)  12.8 us
    all_to_all x1, starting transfers between devices, body(): rhs3 = lax.all_to_all(rhs3, 'gx', 0, 0)  5.98 us
    all_to_all x1, waiting for transfers between devices, body(): rhs3 = lax.all_to_all(rhs3, 'gx', 0, 0)  4.4 us
  transfers between devices with their start and end apart: 14, of which 9 were waited for; matrix products, arithmetic and copies ran while one was open for 0% of the time, Pallas kernels for 10%

profile of v7, /device:TPU:130, one launch (start us, length us, event | category | flops | bytes accessed | tf_op | source)
XLA Modules:
  0.0 148.7 jit_solution(9986885285344026906)
XLA Ops:
  6.5 1.4 shard_map.46
  7.9 3.5 %collective-permute-start = (f32[50,32,128]{2,1,0:T(8,128)S(1)}, f32[50,32,128]{2,1,0:T(8,128)S(1)}, u32[]{:S(2)}, u32[]{:S(2)}) collective-permute-start(f32[50,32,128]{2,1,0:T(8,128)S(1)} %get-tuple-element.23), channel_id=1, source_target_pairs={{0,16},{16,32},{32,48},{48,64},{64,80},{80,96},{96,112},{112,128},... | collective-permute-start | bytes 2457608 | tf_op jit(solution)/shard_map/ppermute | solution.py:581
  11.4 4.5 %collective-permute-start.1 = (f32[49,32,128]{2,1,0:T(8,128)S(1)}, f32[49,32,128]{2,1,0:T(8,128)S(1)}, u32[]{:S(2)}, u32[]{:S(2)}) collective-permute-start(f32[49,32,128]{2,1,0:T(8,128)S(1)} %get-tuple-element.24), channel_id=1, source_target_pairs={{16,0},{32,16},{48,32},{64,48},{80,64},{96,80},{112,96},{128,112},... | collective-permute-start | bytes 2408456 | tf_op jit(solution)/shard_map/ppermute | solution.py:581
  15.9 16.8 %collective-permute-done.1.ahead = f32[49,32,128]{2,1,0:T(8,128)S(1)} collective-permute-done((f32[49,32,128]{2,1,0:T(8,128)S(1)}, f32[49,32,128]{2,1,0:T(8,128)S(1)}, u32[]{:S(2)}, u32[]{:S(2)}) %collective-permute-start.1) | collective-permute-done | bytes 802848 | tf_op jit(solution)/shard_map/ppermute | solution.py:581
  32.7 0.7 shard_map.47
  33.4 1.9 %collective-permute-start.2 = (f32[4,6,32,128]{3,2,1,0:T(8,128)S(1)}, f32[4,6,32,128]{3,2,1,0:T(8,128)S(1)}, u32[]{:S(2)}, u32[]{:S(2)}) collective-permute-start(f32[4,6,32,128]{3,2,1,0:T(8,128)S(1)} %get-tuple-element.25), channel_id=1, source_target_pairs={{0,1},{1,2},{2,3},{3,4},{4,5},{5,6},{6,7},{7,8},{8,9},{9,10},{10,1... | collective-permute-start | bytes 1179656 | tf_op jit(solution)/shard_map/ppermute | solution.py:581
  35.3 4.9 %collective-permute-start.3 = (f32[4,6,32,128]{3,2,1,0:T(8,128)S(1)}, f32[4,6,32,128]{3,2,1,0:T(8,128)S(1)}, u32[]{:S(2)}, u32[]{:S(2)}) collective-permute-start(f32[4,6,32,128]{3,2,1,0:T(8,128)S(1)} %get-tuple-element.26), channel_id=1, source_target_pairs={{1,0},{2,1},{3,2},{4,3},{5,4},{6,5},{7,6},{8,7},{9,8},{10,9},{11,1... | collective-permute-start | bytes 1179656 | tf_op jit(solution)/shard_map/ppermute | solution.py:581
  40.2 3.5 %collective-permute-done.2.from_left = f32[4,6,32,128]{3,2,1,0:T(8,128)S(1)} collective-permute-done((f32[4,6,32,128]{3,2,1,0:T(8,128)S(1)}, f32[4,6,32,128]{3,2,1,0:T(8,128)S(1)}, u32[]{:S(2)}, u32[]{:S(2)}) %collective-permute-start.2) | collective-permute-done | bytes 393248 | tf_op jit(solution)/shard_map/ppermute | solution.py:581
  43.7 1.8 %collective-permute-done.3.from_right = f32[4,6,32,128]{3,2,1,0:T(8,128)S(1)} collective-permute-done((f32[4,6,32,128]{3,2,1,0:T(8,128)S(1)}, f32[4,6,32,128]{3,2,1,0:T(8,128)S(1)}, u32[]{:S(2)}, u32[]{:S(2)}) %collective-permute-start.3) | collective-permute-done | bytes 393248 | tf_op jit(solution)/shard_map/ppermute | solution.py:581
  45.5 12.0 %shard_map.48 = (f32[6,24,32,256]{3,2,1,0:T(8,128)}, f32[5,20,32,128]{3,2,1,0:T(8,128)}, f32[20,32,128]{2,1,0:T(8,128)}, f32[8,32,128]{2,1,0:T(8,128)S(1)}, f32[...) custom-call(f32[4,16,32,128]{3,2,1,0:T(8,128)S(1)} %get-tuple-elemen, ...), custom_call_target="tpu_custom_call" | custom-call | tf_op jit(solution)/shard_map/pallas_call | solution.py:33
  57.5 2.0 %collective-permute-start.4 = (f32[11,32,128]{2,1,0:T(8,128)S(1)}, f32[11,32,128]{2,1,0:T(8,128)S(1)}, u32[]{:S(2)}, u32[]{:S(2)}) collective-permute-start(f32[11,32,128]{2,1,0:T(8,128)S(1)} %get-tuple-element.27.own2), channel_id=1, source_target_pairs={{0,1},{1,2},{2,3},{3,4},{4,5},{5,6},{6,7},{7,8},{8,9},{9,10},{10,1... | collective-permute-start | bytes 540680 | tf_op jit(solution)/shard_map/ppermute | solution.py:581
  59.5 5.0 %collective-permute-start.5 = (f32[11,32,128]{2,1,0:T(8,128)S(1)}, f32[11,32,128]{2,1,0:T(8,128)S(1)}, u32[]{:S(2)}, u32[]{:S(2)}) collective-permute-start(f32[11,32,128]{2,1,0:T(8,128)S(1)} %get-tuple-element.30), channel_id=1, source_target_pairs={{1,0},{2,1},{3,2},{4,3},{5,4},{6,5},{7,6},{8,7},{9,8},{10,9},{11,1... | collective-permute-start | bytes 540680 | tf_op jit(solution)/shard_map/ppermute | solution.py:581
  64.4 1.2 collective-permute-done.4.left
  65.7 1.8 %collective-permute-done.5.right = f32[11,32,128]{2,1,0:T(8,128)S(1)} collective-permute-done((f32[11,32,128]{2,1,0:T(8,128)S(1)}, f32[11,32,128]{2,1,0:T(8,128)S(1)}, u32[]{:S(2)}, u32[]{:S(2)}) %collective-permute-start.5) | collective-permute-done | bytes 180256 | tf_op jit(solution)/shard_map/ppermute | solution.py:581
  67.4 0.8 shard_map.49
  68.3 3.4 %collective-permute-start.6 = (f32[17,32,128]{2,1,0:T(8,128)S(1)}, f32[17,32,128]{2,1,0:T(8,128)S(1)}, u32[]{:S(2)}, u32[]{:S(2)}) collective-permute-start(f32[17,32,128]{2,1,0:T(8,128)S(1)} %get-tuple-element.31), channel_id=1, source_target_pairs={{0,16},{16,32},{32,48},{48,64},{64,80},{80,96},{96,112},{112,128},... | collective-permute-start | bytes 835592 | tf_op jit(solution)/shard_map/ppermute | solution.py:581
  71.7 5.0 %collective-permute-start.7 = (f32[17,32,128]{2,1,0:T(8,128)S(1)}, f32[17,32,128]{2,1,0:T(8,128)S(1)}, u32[]{:S(2)}, u32[]{:S(2)}) collective-permute-start(f32[17,32,128]{2,1,0:T(8,128)S(1)} %get-tuple-element.33), channel_id=1, source_target_pairs={{16,0},{32,16},{48,32},{64,48},{80,64},{96,80},{112,96},{128,112},... | collective-permute-start | bytes 835592 | tf_op jit(solution)/shard_map/ppermute | solution.py:581
  76.7 12.8 %all_to_all.10.ops3 = f32[16,32,128]{2,1,0:T(8,128)S(1)} all-to-all(f32[16,32,128]{2,1,0:T(8,128)S(1)} %get-tuple-element.34), channel_id=1, replica_groups=mesh['gx'=16,'gy'=16] {'gx'}, dimensions={0} | all-to-all | bytes 524288 | tf_op jit(solution)/shard_map/all_to_all | solution.py:619
  89.5 1.6 %shard_map.50.own = f32[17,32,128]{2,1,0:T(8,128)S(1)} custom-call(f32[17,32,128]{2,1,0:T(8,128)S(1)} %collective-permute-done.6.behind.in_behind, f32[10,32,128]{2,1,0:T(8,128)} %get-tuple-element.32.own, f32[17,32,128]{2,1,0:T(8,128)S(1)} %collective-permute-done.7.ahead.in_ahead, f32[16,32,128]{2,1,0:T(8,128)S(1)} %all_to_all.10.ops3), custom_call_target="tpu_custom_call" | custom-call | tf_op jit(solution)/shard_map/pallas_call | solution.py:33
  91.1 1.9 %collective-permute-start.8 = (f32[17,32,128]{2,1,0:T(8,128)S(1)}, f32[17,32,128]{2,1,0:T(8,128)S(1)}, u32[]{:S(2)}, u32[]{:S(2)}) collective-permute-start(f32[17,32,128]{2,1,0:T(8,128)S(1)} %shard_map.50.own), channel_id=1, source_target_pairs={{0,1},{1,2},{2,3},{3,4},{4,5},{5,6},{6,7},{7,8},{8,9},{9,10},{10,1... | collective-permute-start | bytes 835592 | tf_op jit(solution)/shard_map/ppermute | solution.py:581
  93.1 4.9 %collective-permute-start.9 = (f32[17,32,128]{2,1,0:T(8,128)S(1)}, f32[17,32,128]{2,1,0:T(8,128)S(1)}, u32[]{:S(2)}, u32[]{:S(2)}) collective-permute-start(f32[17,32,128]{2,1,0:T(8,128)S(1)} %shard_map.50.own), channel_id=1, source_target_pairs={{1,0},{2,1},{3,2},{4,3},{5,4},{6,5},{7,6},{8,7},{9,8},{10,9},{11,1... | collective-permute-start | bytes 835592 | tf_op jit(solution)/shard_map/ppermute | solution.py:581
  97.9 2.3 %collective-permute-done.8.left = f32[17,32,128]{2,1,0:T(8,128)S(1)} collective-permute-done((f32[17,32,128]{2,1,0:T(8,128)S(1)}, f32[17,32,128]{2,1,0:T(8,128)S(1)}, u32[]{:S(2)}, u32[]{:S(2)}) %collective-permute-start.8) | collective-permute-done | bytes 278560 | tf_op jit(solution)/shard_map/ppermute | solution.py:581
  100.2 1.9 %collective-permute-start.10 = (f32[17,32,128]{2,1,0:T(8,128)S(1)}, f32[17,32,128]{2,1,0:T(8,128)S(1)}, u32[]{:S(2)}, u32[]{:S(2)}) collective-permute-start(f32[17,32,128]{2,1,0:T(8,128)S(1)} %collective-permute-done.8.left), channel_id=1, source_target_pairs={{0,1},{1,2},{2,3},{3,4},{4,5},{5,6},{6,7},{7,8},{8,9},{9,10},{10,1... | collective-permute-start | bytes 835592 | tf_op jit(solution)/shard_map/ppermute | solution.py:581
  102.1 4.9 %collective-permute-start.11 = (f32[17,32,128]{2,1,0:T(8,128)S(1)}, f32[17,32,128]{2,1,0:T(8,128)S(1)}, u32[]{:S(2)}, u32[]{:S(2)}) collective-permute-start(f32[17,32,128]{2,1,0:T(8,128)S(1)} %collective-permute-done.9.right), channel_id=1, source_target_pairs={{1,0},{2,1},{3,2},{4,3},{5,4},{6,5},{7,6},{8,7},{9,8},{10,9},{11,1... | collective-permute-start | bytes 835592 | tf_op jit(solution)/shard_map/ppermute | solution.py:581
  107.0 2.3 %collective-permute-done.10.left_far = f32[17,32,128]{2,1,0:T(8,128)S(1)} collective-permute-done((f32[17,32,128]{2,1,0:T(8,128)S(1)}, f32[17,32,128]{2,1,0:T(8,128)S(1)}, u32[]{:S(2)}, u32[]{:S(2)}) %collective-permute-start.10) | collective-permute-done | bytes 278560 | tf_op jit(solution)/shard_map/ppermute | solution.py:581
  109.3 1.8 %collective-permute-done.11.right_far = f32[17,32,128]{2,1,0:T(8,128)S(1)} collective-permute-done((f32[17,32,128]{2,1,0:T(8,128)S(1)}, f32[17,32,128]{2,1,0:T(8,128)S(1)}, u32[]{:S(2)}, u32[]{:S(2)}) %collective-permute-start.11) | collective-permute-done | bytes 278560 | tf_op jit(solution)/shard_map/ppermute | solution.py:581
  111.0 0.7 shard_map.51
  111.8 6.0 %all-to-all-start.1 = ((f32[16,5,8,128]{3,2,1,0:T(8,128)}), f32[16,5,8,128]{3,2,1,0:T(8,128)S(1)}, u32[]{:S(2)}, u32[]{:S(2)}) async-start(f32[16,5,8,128]{3,2,1,0:T(8,128)} %shard_map.51), calls=%async_computation.1 | async-start | bytes 655360 | tf_op jit(solution)/shard_map/all_to_all | solution.py:637
  117.8 4.3 %shard_map.52.in_ops3 = f32[4,32,32,128]{3,2,1,0:T(8,128)} custom-call(f32[17,32,128]{2,1,0:T(8,128)S(1)} %shard_map.50.own, f32[17,32,128]{2,1,0:T(8,128)S(1)} %collective-permute-done.8.left, f32[17,32,128]{2,1,0:T(8,128)S(1)} %collective-permute-done.9.right, f32[17,32,128]{2,1,0:T(8,128)S(1)} %collective-permute-done.10.left_far, ...), custom_call_target="tpu_custom_call" | custom-call | tf_op jit(solution)/shard_map/pallas_call | solution.py:33
  122.0 4.4 %all-to-all-done.1.gathered = f32[16,5,8,128]{3,2,1,0:T(8,128)S(1)} async-done(((f32[16,5,8,128]{3,2,1,0:T(8,128)}), f32[16,5,8,128]{3,2,1,0:T(8,128)S(1)}, u32[]{:S(2)}, u32[]{:S(2)}) %all-to-all-start.1) | async-done | bytes 327712 | tf_op jit(solution)/shard_map/all_to_all | solution.py:637
  126.4 8.3 %shard_map.53.e3 = f32[10,32,128]{2,1,0:T(8,128)S(1)} custom-call(f32[16,5,8,128]{3,2,1,0:T(8,128)S(1)} %all-to-all-done.1.gathered, f32[4,32,32,128]{3,2,1,0:T(8,128)} %shard_map.52.in_ops3), custom_call_target="tpu_custom_call" | custom-call | tf_op jit(solution)/shard_map/pallas_call | solution.py:33
  134.8 7.0 %shard_map.54 = f32[32,16,128]{2,1,0:T(8,128)} custom-call(f32[10,32,128]{2,1,0:T(8,128)S(1)} %shard_map.53.e3, f32[16,10,32,128]{3,2,1,0:T(8,128)} %bitcast.1, f32[17,32,128]{2,1,0:T(8,128)S(1)} %collective-permute-done.6.behind.in_behind, f32[17,32,128]{2,1,0:T(8,128)S(1)} %collective-permute-done.7.ahead.in_ahead, ...), custom_call_target="tpu_custom_call" | custom-call | tf_op jit(solution)/shard_map/pallas_call | solution.py:33
  (7 shorter events, 0.1 us)
Async XLA Ops:
  6.5 128.3 %all-gather.3.cloned.1.call-start = ((), (), s32[]{:S(2)}) async-start(), calls=%async_computation.2 | async-start | bytes 2785280 | tf_op jit(solution)/shard_map/all_gather | solution.py:625
  7.9 24.8 %collective-permute-start = (f32[50,32,128]{2,1,0:T(8,128)S(1)}, f32[50,32,128]{2,1,0:T(8,128)S(1)}, u32[]{:S(2)}, u32[]{:S(2)}) collective-permute-start(f32[50,32,128]{2,1,0:T(8,128)S(1)} %get-tuple-element.23), channel_id=1, source_target_pairs={{0,16},{16,32},{32,48},{48,64},{64,80},{80,96},{96,112},{112,128},... | collective-permute-start | bytes 2457608 | tf_op jit(solution)/shard_map/ppermute | solution.py:581
  11.4 21.3 %collective-permute-start.1 = (f32[49,32,128]{2,1,0:T(8,128)S(1)}, f32[49,32,128]{2,1,0:T(8,128)S(1)}, u32[]{:S(2)}, u32[]{:S(2)}) collective-permute-start(f32[49,32,128]{2,1,0:T(8,128)S(1)} %get-tuple-element.24), channel_id=1, source_target_pairs={{16,0},{32,16},{48,32},{64,48},{80,64},{96,80},{112,96},{128,112},... | collective-permute-start | bytes 2408456 | tf_op jit(solution)/shard_map/ppermute | solution.py:581
  33.4 10.3 %collective-permute-start.2 = (f32[4,6,32,128]{3,2,1,0:T(8,128)S(1)}, f32[4,6,32,128]{3,2,1,0:T(8,128)S(1)}, u32[]{:S(2)}, u32[]{:S(2)}) collective-permute-start(f32[4,6,32,128]{3,2,1,0:T(8,128)S(1)} %get-tuple-element.25), channel_id=1, source_target_pairs={{0,1},{1,2},{2,3},{3,4},{4,5},{5,6},{6,7},{7,8},{8,9},{9,10},{10,1... | collective-permute-start | bytes 1179656 | tf_op jit(solution)/shard_map/ppermute | solution.py:581
  35.3 10.1 %collective-permute-start.3 = (f32[4,6,32,128]{3,2,1,0:T(8,128)S(1)}, f32[4,6,32,128]{3,2,1,0:T(8,128)S(1)}, u32[]{:S(2)}, u32[]{:S(2)}) collective-permute-start(f32[4,6,32,128]{3,2,1,0:T(8,128)S(1)} %get-tuple-element.26), channel_id=1, source_target_pairs={{1,0},{2,1},{3,2},{4,3},{5,4},{6,5},{7,6},{8,7},{9,8},{10,9},{11,1... | collective-permute-start | bytes 1179656 | tf_op jit(solution)/shard_map/ppermute | solution.py:581
  57.5 8.2 %collective-permute-start.4 = (f32[11,32,128]{2,1,0:T(8,128)S(1)}, f32[11,32,128]{2,1,0:T(8,128)S(1)}, u32[]{:S(2)}, u32[]{:S(2)}) collective-permute-start(f32[11,32,128]{2,1,0:T(8,128)S(1)} %get-tuple-element.27.own2), channel_id=1, source_target_pairs={{0,1},{1,2},{2,3},{3,4},{4,5},{5,6},{6,7},{7,8},{8,9},{9,10},{10,1... | collective-permute-start | bytes 540680 | tf_op jit(solution)/shard_map/ppermute | solution.py:581
  59.5 8.0 %collective-permute-start.5 = (f32[11,32,128]{2,1,0:T(8,128)S(1)}, f32[11,32,128]{2,1,0:T(8,128)S(1)}, u32[]{:S(2)}, u32[]{:S(2)}) collective-permute-start(f32[11,32,128]{2,1,0:T(8,128)S(1)} %get-tuple-element.30), channel_id=1, source_target_pairs={{1,0},{2,1},{3,2},{4,3},{5,4},{6,5},{7,6},{8,7},{9,8},{10,9},{11,1... | collective-permute-start | bytes 540680 | tf_op jit(solution)/shard_map/ppermute | solution.py:581
  68.3 21.3 %collective-permute-start.6 = (f32[17,32,128]{2,1,0:T(8,128)S(1)}, f32[17,32,128]{2,1,0:T(8,128)S(1)}, u32[]{:S(2)}, u32[]{:S(2)}) collective-permute-start(f32[17,32,128]{2,1,0:T(8,128)S(1)} %get-tuple-element.31), channel_id=1, source_target_pairs={{0,16},{16,32},{32,48},{48,64},{64,80},{80,96},{96,112},{112,128},... | collective-permute-start | bytes 835592 | tf_op jit(solution)/shard_map/ppermute | solution.py:581
  71.7 17.9 %collective-permute-start.7 = (f32[17,32,128]{2,1,0:T(8,128)S(1)}, f32[17,32,128]{2,1,0:T(8,128)S(1)}, u32[]{:S(2)}, u32[]{:S(2)}) collective-permute-start(f32[17,32,128]{2,1,0:T(8,128)S(1)} %get-tuple-element.33), channel_id=1, source_target_pairs={{16,0},{32,16},{48,32},{64,48},{80,64},{96,80},{112,96},{128,112},... | collective-permute-start | bytes 835592 | tf_op jit(solution)/shard_map/ppermute | solution.py:581
  91.1 9.1 %collective-permute-start.8 = (f32[17,32,128]{2,1,0:T(8,128)S(1)}, f32[17,32,128]{2,1,0:T(8,128)S(1)}, u32[]{:S(2)}, u32[]{:S(2)}) collective-permute-start(f32[17,32,128]{2,1,0:T(8,128)S(1)} %shard_map.50.own), channel_id=1, source_target_pairs={{0,1},{1,2},{2,3},{3,4},{4,5},{5,6},{6,7},{7,8},{8,9},{9,10},{10,1... | collective-permute-start | bytes 835592 | tf_op jit(solution)/shard_map/ppermute | solution.py:581
  93.1 9.1 %collective-permute-start.9 = (f32[17,32,128]{2,1,0:T(8,128)S(1)}, f32[17,32,128]{2,1,0:T(8,128)S(1)}, u32[]{:S(2)}, u32[]{:S(2)}) collective-permute-start(f32[17,32,128]{2,1,0:T(8,128)S(1)} %shard_map.50.own), channel_id=1, source_target_pairs={{1,0},{2,1},{3,2},{4,3},{5,4},{6,5},{7,6},{8,7},{9,8},{10,9},{11,1... | collective-permute-start | bytes 835592 | tf_op jit(solution)/shard_map/ppermute | solution.py:581
  100.2 9.1 %collective-permute-start.10 = (f32[17,32,128]{2,1,0:T(8,128)S(1)}, f32[17,32,128]{2,1,0:T(8,128)S(1)}, u32[]{:S(2)}, u32[]{:S(2)}) collective-permute-start(f32[17,32,128]{2,1,0:T(8,128)S(1)} %collective-permute-done.8.left), channel_id=1, source_target_pairs={{0,1},{1,2},{2,3},{3,4},{4,5},{5,6},{6,7},{7,8},{8,9},{9,10},{10,1... | collective-permute-start | bytes 835592 | tf_op jit(solution)/shard_map/ppermute | solution.py:581
  102.1 8.9 %collective-permute-start.11 = (f32[17,32,128]{2,1,0:T(8,128)S(1)}, f32[17,32,128]{2,1,0:T(8,128)S(1)}, u32[]{:S(2)}, u32[]{:S(2)}) collective-permute-start(f32[17,32,128]{2,1,0:T(8,128)S(1)} %collective-permute-done.9.right), channel_id=1, source_target_pairs={{1,0},{2,1},{3,2},{4,3},{5,4},{6,5},{7,6},{8,7},{9,8},{10,9},{11,1... | collective-permute-start | bytes 835592 | tf_op jit(solution)/shard_map/ppermute | solution.py:581
  111.8 14.6 %all-to-all-start.1 = ((f32[16,5,8,128]{3,2,1,0:T(8,128)}), f32[16,5,8,128]{3,2,1,0:T(8,128)S(1)}, u32[]{:S(2)}, u32[]{:S(2)}) async-start(f32[16,5,8,128]{3,2,1,0:T(8,128)} %shard_map.51), calls=%async_computation.1 | async-start | bytes 655360 | tf_op jit(solution)/shard_map/all_to_all | solution.py:637
Sparse Core Ops, SparseCore 0:
  68.4 56.7 all-gather.2

commit v8 on v6

--- a/solution.py
+++ b/solution.py
@@ -437,13 +437,12 @@
 
 
 def spread3_kernel(count, own, left, right, left_far, right_far, out, ops3, sems):
-    def unpack(i, carry):
+    def unpack(i):
         values = turned([ref[i] for ref in (left_far, left, own, right, right_far)])
         for m, value in enumerate(values):
             ops3[m // 2, 2 * i + m % 2] = scale_of(value) if m >= 6 else value
-        return carry
-
-    lax.fori_loop(0, count, unpack, 0)
+
+    planes(0, count, unpack, 4)
     for copy in fetch(((ops3, out),), sems):
         copy.wait()
 
@@ -457,14 +456,13 @@
         ref[0:lo] = jnp.zeros((PAD3, NZ, 128), F32)
         ref[hi : hi + PAD3] = jnp.zeros((PAD3, NZ, 128), F32)
 
-    def unpack(i, carry):
+    def unpack(i):
         p = lo + 2 * i
         for m, value in enumerate(turned([gathered[i, s] for s in range(5)])):
             part = slice(8 * (m // 2), 8 * (m // 2) + 8)
             f3[p + m % 2, part] = value
-        return carry
-
-    lax.fori_loop(0, count, unpack, 0)
+
+    planes(0, count, unpack, 8)
     for copy in copies:
         copy.wait()
 

time: 141 us -> 139 us (0.986)
  Pallas kernels: 35.9 us -> 33.4 us
    pallas_call x9, Pallas kernels: 35.9 us -> 33.4 us  [call(): pl.pallas_call(kernel, out_shape=[pltpu.HBM(s, F32) if i in apart_outs el...]
  transfers between devices with their start and end apart: 17 -> 17, of which waited for: 6 -> 6; matrix products, arithmetic and copies ran while one was open for 0% -> 0% of each run, Pallas kernels for 9% -> 8%
where the time goes in v8:
time: 139 us; the launch traced here: 138 us
  starting transfers between devices  64.1 us (46%)
  Pallas kernels  33.4 us (24%)
  waiting for transfers between devices  27.4 us (20%)
  blocking collectives  12.6 us (9%)
    ppermute x16, starting transfers between devices, shift(): return lax.ppermute(value, axis, route)  59.7 us
    pallas_call x9, Pallas kernels, call(): pl.pallas_call(kernel, out_shape=[pltpu.HBM(s, F32) if i in apart_outs el...  33.4 us
    ppermute x16, waiting for transfers between devices, shift(): return lax.ppermute(value, axis, route)  27.4 us
    all_to_all x1, blocking collectives, body(): all3 = lax.all_to_all(own3, 'gx', 0, 0)  12.6 us
    all_to_all x1, starting transfers between devices, body(): rhs3 = lax.all_to_all(rhs3, 'gx', 0, 0)  4.39 us
  transfers between devices with their start and end apart: 17, of which 6 were waited for; matrix products, arithmetic and copies ran while one was open for 0% of the time, Pallas kernels for 8%

profile of v8, /device:TPU:130, one launch (start us, length us, event | category | flops | bytes accessed | tf_op | source)
XLA Modules:
  0.0 138.0 jit_solution(15970394665641070665)
XLA Ops:
  0.0 1.4 shard_map.46
  1.4 3.5 %collective-permute-start = (f32[50,32,128]{2,1,0:T(8,128)S(1)}, f32[50,32,128]{2,1,0:T(8,128)S(1)}, u32[]{:S(2)}, u32[]{:S(2)}) collective-permute-start(f32[50,32,128]{2,1,0:T(8,128)S(1)} %get-tuple-element.26), channel_id=1, source_target_pairs={{0,16},{16,32},{32,48},{48,64},{64,80},{80,96},{96,112},{112,128},... | collective-permute-start | bytes 2457608 | tf_op jit(solution)/shard_map/ppermute | solution.py:579
  4.9 4.5 %collective-permute-start.1 = (f32[49,32,128]{2,1,0:T(8,128)S(1)}, f32[49,32,128]{2,1,0:T(8,128)S(1)}, u32[]{:S(2)}, u32[]{:S(2)}) collective-permute-start(f32[49,32,128]{2,1,0:T(8,128)S(1)} %get-tuple-element.27), channel_id=1, source_target_pairs={{16,0},{32,16},{48,32},{64,48},{80,64},{96,80},{112,96},{128,112},... | collective-permute-start | bytes 2408456 | tf_op jit(solution)/shard_map/ppermute | solution.py:579
  9.4 16.8 %collective-permute-done.1.ahead = f32[49,32,128]{2,1,0:T(8,128)S(1)} collective-permute-done((f32[49,32,128]{2,1,0:T(8,128)S(1)}, f32[49,32,128]{2,1,0:T(8,128)S(1)}, u32[]{:S(2)}, u32[]{:S(2)}) %collective-permute-start.1) | collective-permute-done | bytes 802848 | tf_op jit(solution)/shard_map/ppermute | solution.py:579
  26.2 0.7 shard_map.47
  26.9 1.9 %collective-permute-start.2 = (f32[4,6,32,128]{3,2,1,0:T(8,128)S(1)}, f32[4,6,32,128]{3,2,1,0:T(8,128)S(1)}, u32[]{:S(2)}, u32[]{:S(2)}) collective-permute-start(f32[4,6,32,128]{3,2,1,0:T(8,128)S(1)} %get-tuple-element.28), channel_id=1, source_target_pairs={{0,1},{1,2},{2,3},{3,4},{4,5},{5,6},{6,7},{7,8},{8,9},{9,10},{10,1... | collective-permute-start | bytes 1179656 | tf_op jit(solution)/shard_map/ppermute | solution.py:579
  28.8 4.9 %collective-permute-start.3 = (f32[4,6,32,128]{3,2,1,0:T(8,128)S(1)}, f32[4,6,32,128]{3,2,1,0:T(8,128)S(1)}, u32[]{:S(2)}, u32[]{:S(2)}) collective-permute-start(f32[4,6,32,128]{3,2,1,0:T(8,128)S(1)} %get-tuple-element.29), channel_id=1, source_target_pairs={{1,0},{2,1},{3,2},{4,3},{5,4},{6,5},{7,6},{8,7},{9,8},{10,9},{11,1... | collective-permute-start | bytes 1179656 | tf_op jit(solution)/shard_map/ppermute | solution.py:579
  33.7 3.5 %collective-permute-done.2.from_left = f32[4,6,32,128]{3,2,1,0:T(8,128)S(1)} collective-permute-done((f32[4,6,32,128]{3,2,1,0:T(8,128)S(1)}, f32[4,6,32,128]{3,2,1,0:T(8,128)S(1)}, u32[]{:S(2)}, u32[]{:S(2)}) %collective-permute-start.2) | collective-permute-done | bytes 393248 | tf_op jit(solution)/shard_map/ppermute | solution.py:579
  37.2 1.8 %collective-permute-done.3.from_right = f32[4,6,32,128]{3,2,1,0:T(8,128)S(1)} collective-permute-done((f32[4,6,32,128]{3,2,1,0:T(8,128)S(1)}, f32[4,6,32,128]{3,2,1,0:T(8,128)S(1)}, u32[]{:S(2)}, u32[]{:S(2)}) %collective-permute-start.3) | collective-permute-done | bytes 393248 | tf_op jit(solution)/shard_map/ppermute | solution.py:579
  38.9 12.1 %shard_map.48 = (f32[6,24,32,256]{3,2,1,0:T(8,128)}, f32[5,20,32,128]{3,2,1,0:T(8,128)}, f32[20,32,128]{2,1,0:T(8,128)}, f32[8,32,128]{2,1,0:T(8,128)S(1)}, f32[...) custom-call(f32[4,16,32,128]{3,2,1,0:T(8,128)S(1)} %get-tuple-elemen, ...), custom_call_target="tpu_custom_call" | custom-call | tf_op jit(solution)/shard_map/pallas_call | solution.py:33
  51.0 2.0 %collective-permute-start.4 = (f32[11,32,128]{2,1,0:T(8,128)S(1)}, f32[11,32,128]{2,1,0:T(8,128)S(1)}, u32[]{:S(2)}, u32[]{:S(2)}) collective-permute-start(f32[11,32,128]{2,1,0:T(8,128)S(1)} %get-tuple-element.30.own2), channel_id=1, source_target_pairs={{0,1},{1,2},{2,3},{3,4},{4,5},{5,6},{6,7},{7,8},{8,9},{9,10},{10,1... | collective-permute-start | bytes 540680 | tf_op jit(solution)/shard_map/ppermute | solution.py:579
  53.0 5.0 %collective-permute-start.5 = (f32[11,32,128]{2,1,0:T(8,128)S(1)}, f32[11,32,128]{2,1,0:T(8,128)S(1)}, u32[]{:S(2)}, u32[]{:S(2)}) collective-permute-start(f32[11,32,128]{2,1,0:T(8,128)S(1)} %get-tuple-element.33), channel_id=1, source_target_pairs={{1,0},{2,1},{3,2},{4,3},{5,4},{6,5},{7,6},{8,7},{9,8},{10,9},{11,1... | collective-permute-start | bytes 540680 | tf_op jit(solution)/shard_map/ppermute | solution.py:579
  58.0 1.2 collective-permute-done.4.left
  59.2 1.8 %collective-permute-done.5.right = f32[11,32,128]{2,1,0:T(8,128)S(1)} collective-permute-done((f32[11,32,128]{2,1,0:T(8,128)S(1)}, f32[11,32,128]{2,1,0:T(8,128)S(1)}, u32[]{:S(2)}, u32[]{:S(2)}) %collective-permute-start.5) | collective-permute-done | bytes 180256 | tf_op jit(solution)/shard_map/ppermute | solution.py:579
  61.2 3.4 %collective-permute-start.6 = (f32[17,32,128]{2,1,0:T(8,128)S(1)}, f32[17,32,128]{2,1,0:T(8,128)S(1)}, u32[]{:S(2)}, u32[]{:S(2)}) collective-permute-start(f32[17,32,128]{2,1,0:T(8,128)S(1)} %get-tuple-element.34), channel_id=1, source_target_pairs={{0,16},{16,32},{32,48},{48,64},{64,80},{80,96},{96,112},{112,128},... | collective-permute-start | bytes 835592 | tf_op jit(solution)/shard_map/ppermute | solution.py:579
  64.6 5.0 %collective-permute-start.7 = (f32[17,32,128]{2,1,0:T(8,128)S(1)}, f32[17,32,128]{2,1,0:T(8,128)S(1)}, u32[]{:S(2)}, u32[]{:S(2)}) collective-permute-start(f32[17,32,128]{2,1,0:T(8,128)S(1)} %get-tuple-element.36), channel_id=1, source_target_pairs={{16,0},{32,16},{48,32},{64,48},{80,64},{96,80},{112,96},{128,112},... | collective-permute-start | bytes 835592 | tf_op jit(solution)/shard_map/ppermute | solution.py:579
  69.6 12.6 %all_to_all.10.ops3 = f32[16,32,128]{2,1,0:T(8,128)S(1)} all-to-all(f32[16,32,128]{2,1,0:T(8,128)S(1)} %get-tuple-element.37), channel_id=1, replica_groups=mesh['gx'=16,'gy'=16] {'gx'}, dimensions={0} | all-to-all | bytes 524288 | tf_op jit(solution)/shard_map/all_to_all | solution.py:617
  82.3 0.7 shard_map.50
  82.9 1.9 %collective-permute-start.8 = (f32[17,32,128]{2,1,0:T(8,128)S(1)}, f32[17,32,128]{2,1,0:T(8,128)S(1)}, u32[]{:S(2)}, u32[]{:S(2)}) collective-permute-start(f32[17,32,128]{2,1,0:T(8,128)S(1)} %get-tuple-element.38.own), channel_id=1, source_target_pairs={{0,1},{1,2},{2,3},{3,4},{4,5},{5,6},{6,7},{7,8},{8,9},{9,10},{10,1... | collective-permute-start | bytes 835592 | tf_op jit(solution)/shard_map/ppermute | solution.py:579
  84.9 4.9 %collective-permute-start.9 = (f32[17,32,128]{2,1,0:T(8,128)S(1)}, f32[17,32,128]{2,1,0:T(8,128)S(1)}, u32[]{:S(2)}, u32[]{:S(2)}) collective-permute-start(f32[17,32,128]{2,1,0:T(8,128)S(1)} %get-tuple-element.38.own), channel_id=1, source_target_pairs={{1,0},{2,1},{3,2},{4,3},{5,4},{6,5},{7,6},{8,7},{9,8},{10,9},{11,1... | collective-permute-start | bytes 835592 | tf_op jit(solution)/shard_map/ppermute | solution.py:579
  89.7 2.3 %collective-permute-done.8.left = f32[17,32,128]{2,1,0:T(8,128)S(1)} collective-permute-done((f32[17,32,128]{2,1,0:T(8,128)S(1)}, f32[17,32,128]{2,1,0:T(8,128)S(1)}, u32[]{:S(2)}, u32[]{:S(2)}) %collective-permute-start.8) | collective-permute-done | bytes 278560 | tf_op jit(solution)/shard_map/ppermute | solution.py:579
  92.0 1.9 %collective-permute-start.10 = (f32[17,32,128]{2,1,0:T(8,128)S(1)}, f32[17,32,128]{2,1,0:T(8,128)S(1)}, u32[]{:S(2)}, u32[]{:S(2)}) collective-permute-start(f32[17,32,128]{2,1,0:T(8,128)S(1)} %collective-permute-done.8.left), channel_id=1, source_target_pairs={{0,1},{1,2},{2,3},{3,4},{4,5},{5,6},{6,7},{7,8},{8,9},{9,10},{10,1... | collective-permute-start | bytes 835592 | tf_op jit(solution)/shard_map/ppermute | solution.py:579
  93.9 4.9 %collective-permute-start.11 = (f32[17,32,128]{2,1,0:T(8,128)S(1)}, f32[17,32,128]{2,1,0:T(8,128)S(1)}, u32[]{:S(2)}, u32[]{:S(2)}) collective-permute-start(f32[17,32,128]{2,1,0:T(8,128)S(1)} %collective-permute-done.9.right), channel_id=1, source_target_pairs={{1,0},{2,1},{3,2},{4,3},{5,4},{6,5},{7,6},{8,7},{9,8},{10,9},{11,1... | collective-permute-start | bytes 835592 | tf_op jit(solution)/shard_map/ppermute | solution.py:579
  98.8 2.3 %collective-permute-start.12 = (f32[10,32,128]{2,1,0:T(8,128)S(1)}, f32[10,32,128]{2,1,0:T(8,128)S(1)}, u32[]{:S(2)}, u32[]{:S(2)}) collective-permute-start(f32[10,32,128]{2,1,0:T(8,128)S(1)} %get-tuple-element.39), channel_id=1, source_target_pairs={{0,16},{16,32},{32,48},{48,64},{64,80},{80,96},{96,112},{112,128},... | collective-permute-start | bytes 491528 | tf_op jit(solution)/shard_map/ppermute | solution.py:579
  101.1 5.6 %collective-permute-start.14 = (f32[10,32,128]{2,1,0:T(8,128)S(1)}, f32[10,32,128]{2,1,0:T(8,128)S(1)}, u32[]{:S(2)}, u32[]{:S(2)}) collective-permute-start(f32[10,32,128]{2,1,0:T(8,128)S(1)} %get-tuple-element.40), channel_id=1, source_target_pairs={{16,0},{32,16},{48,32},{64,48},{80,64},{96,80},{112,96},{128,112},... | collective-permute-start | bytes 491528 | tf_op jit(solution)/shard_map/ppermute | solution.py:579
  106.8 0.8 shard_map.51
  107.6 4.4 %all-to-all-start.1 = ((f32[16,5,8,128]{3,2,1,0:T(8,128)}), f32[16,5,8,128]{3,2,1,0:T(8,128)S(1)}, u32[]{:S(2)}, u32[]{:S(2)}) async-start(f32[16,5,8,128]{3,2,1,0:T(8,128)} %shard_map.51), calls=%async_computation.1 | async-start | bytes 655360 | tf_op jit(solution)/shard_map/all_to_all | solution.py:635
  112.0 3.4 %collective-permute-start.13 = (f32[10,32,128]{2,1,0:T(8,128)S(1)}, f32[10,32,128]{2,1,0:T(8,128)S(1)}, u32[]{:S(2)}, u32[]{:S(2)}) collective-permute-start(f32[10,32,128]{2,1,0:T(8,128)S(1)} %collective-permute-done.12.in_behind2), channel_id=1, source_target_pairs={{0,16},{16,32},{32,48},{48,64},{64,80},{80,96},{96,112},{112,128},... | collective-permute-start | bytes 491528 | tf_op jit(solution)/shard_map/ppermute | solution.py:579
  115.3 4.8 %collective-permute-start.15 = (f32[10,32,128]{2,1,0:T(8,128)S(1)}, f32[10,32,128]{2,1,0:T(8,128)S(1)}, u32[]{:S(2)}, u32[]{:S(2)}) collective-permute-start(f32[10,32,128]{2,1,0:T(8,128)S(1)} %collective-permute-done.14.in_ahead2), channel_id=1, source_target_pairs={{16,0},{32,16},{48,32},{64,48},{80,64},{96,80},{112,96},{128,112},... | collective-permute-start | bytes 491528 | tf_op jit(solution)/shard_map/ppermute | solution.py:579
  120.1 2.8 %shard_map.52.in_ops3 = f32[4,32,32,128]{3,2,1,0:T(8,128)} custom-call(f32[17,32,128]{2,1,0:T(8,128)S(1)} %get-tuple-element.38.own, f32[17,32,128]{2,1,0:T(8,128)S(1)} %collective-permute-done.8.left, f32[17,32,128]{2,1,0:T(8,128)S(1)} %collective-permute-done.9.right, f32[17,32,128]{2,1,0:T(8,128)S(1)} %collective-permute-done.10.left_far, ...), custom_call_target="tpu_custom_call" | custom-call | tf_op jit(solution)/shard_map/pallas_call | solution.py:33
  122.9 7.2 %shard_map.53.e3 = f32[10,32,128]{2,1,0:T(8,128)S(1)} custom-call(f32[16,5,8,128]{3,2,1,0:T(8,128)S(1)} %all-to-all-done.1.gathered, f32[4,32,32,128]{3,2,1,0:T(8,128)} %shard_map.52.in_ops3), custom_call_target="tpu_custom_call" | custom-call | tf_op jit(solution)/shard_map/pallas_call | solution.py:33
  130.2 7.6 %shard_map.54 = f32[32,16,128]{2,1,0:T(8,128)} custom-call(f32[10,32,128]{2,1,0:T(8,128)S(1)} %shard_map.53.e3, f32[10,32,128]{2,1,0:T(8,128)S(1)} %collective-permute-done.13.in_behind3, f32[10,32,128]{2,1,0:T(8,128)S(1)} %collective-permute-done.12.in_behind2, f32[17,32,128]{2,1,0:T(8,128)S(1)} %collective-permute-done.6.behind.in_behind, ...), custom_call_target="tpu_custom_call" | custom-call | tf_op jit(solution)/shard_map/pallas_call | solution.py:33
  (12 shorter events, 0.2 us)
Async XLA Ops:
  1.4 24.8 %collective-permute-start = (f32[50,32,128]{2,1,0:T(8,128)S(1)}, f32[50,32,128]{2,1,0:T(8,128)S(1)}, u32[]{:S(2)}, u32[]{:S(2)}) collective-permute-start(f32[50,32,128]{2,1,0:T(8,128)S(1)} %get-tuple-element.26), channel_id=1, source_target_pairs={{0,16},{16,32},{32,48},{48,64},{64,80},{80,96},{96,112},{112,128},... | collective-permute-start | bytes 2457608 | tf_op jit(solution)/shard_map/ppermute | solution.py:579
  4.9 21.3 %collective-permute-start.1 = (f32[49,32,128]{2,1,0:T(8,128)S(1)}, f32[49,32,128]{2,1,0:T(8,128)S(1)}, u32[]{:S(2)}, u32[]{:S(2)}) collective-permute-start(f32[49,32,128]{2,1,0:T(8,128)S(1)} %get-tuple-element.27), channel_id=1, source_target_pairs={{16,0},{32,16},{48,32},{64,48},{80,64},{96,80},{112,96},{128,112},... | collective-permute-start | bytes 2408456 | tf_op jit(solution)/shard_map/ppermute | solution.py:579
  26.9 10.3 %collective-permute-start.2 = (f32[4,6,32,128]{3,2,1,0:T(8,128)S(1)}, f32[4,6,32,128]{3,2,1,0:T(8,128)S(1)}, u32[]{:S(2)}, u32[]{:S(2)}) collective-permute-start(f32[4,6,32,128]{3,2,1,0:T(8,128)S(1)} %get-tuple-element.28), channel_id=1, source_target_pairs={{0,1},{1,2},{2,3},{3,4},{4,5},{5,6},{6,7},{7,8},{8,9},{9,10},{10,1... | collective-permute-start | bytes 1179656 | tf_op jit(solution)/shard_map/ppermute | solution.py:579
  28.8 10.1 %collective-permute-start.3 = (f32[4,6,32,128]{3,2,1,0:T(8,128)S(1)}, f32[4,6,32,128]{3,2,1,0:T(8,128)S(1)}, u32[]{:S(2)}, u32[]{:S(2)}) collective-permute-start(f32[4,6,32,128]{3,2,1,0:T(8,128)S(1)} %get-tuple-element.29), channel_id=1, source_target_pairs={{1,0},{2,1},{3,2},{4,3},{5,4},{6,5},{7,6},{8,7},{9,8},{10,9},{11,1... | collective-permute-start | bytes 1179656 | tf_op jit(solution)/shard_map/ppermute | solution.py:579
  51.0 8.2 %collective-permute-start.4 = (f32[11,32,128]{2,1,0:T(8,128)S(1)}, f32[11,32,128]{2,1,0:T(8,128)S(1)}, u32[]{:S(2)}, u32[]{:S(2)}) collective-permute-start(f32[11,32,128]{2,1,0:T(8,128)S(1)} %get-tuple-element.30.own2), channel_id=1, source_target_pairs={{0,1},{1,2},{2,3},{3,4},{4,5},{5,6},{6,7},{7,8},{8,9},{9,10},{10,1... | collective-permute-start | bytes 540680 | tf_op jit(solution)/shard_map/ppermute | solution.py:579
  53.0 8.0 %collective-permute-start.5 = (f32[11,32,128]{2,1,0:T(8,128)S(1)}, f32[11,32,128]{2,1,0:T(8,128)S(1)}, u32[]{:S(2)}, u32[]{:S(2)}) collective-permute-start(f32[11,32,128]{2,1,0:T(8,128)S(1)} %get-tuple-element.33), channel_id=1, source_target_pairs={{1,0},{2,1},{3,2},{4,3},{5,4},{6,5},{7,6},{8,7},{9,8},{10,9},{11,1... | collective-permute-start | bytes 540680 | tf_op jit(solution)/shard_map/ppermute | solution.py:579
  61.2 21.1 %collective-permute-start.6 = (f32[17,32,128]{2,1,0:T(8,128)S(1)}, f32[17,32,128]{2,1,0:T(8,128)S(1)}, u32[]{:S(2)}, u32[]{:S(2)}) collective-permute-start(f32[17,32,128]{2,1,0:T(8,128)S(1)} %get-tuple-element.34), channel_id=1, source_target_pairs={{0,16},{16,32},{32,48},{48,64},{64,80},{80,96},{96,112},{112,128},... | collective-permute-start | bytes 835592 | tf_op jit(solution)/shard_map/ppermute | solution.py:579
  64.6 17.7 %collective-permute-start.7 = (f32[17,32,128]{2,1,0:T(8,128)S(1)}, f32[17,32,128]{2,1,0:T(8,128)S(1)}, u32[]{:S(2)}, u32[]{:S(2)}) collective-permute-start(f32[17,32,128]{2,1,0:T(8,128)S(1)} %get-tuple-element.36), channel_id=1, source_target_pairs={{16,0},{32,16},{48,32},{64,48},{80,64},{96,80},{112,96},{128,112},... | collective-permute-start | bytes 835592 | tf_op jit(solution)/shard_map/ppermute | solution.py:579
  82.9 9.1 %collective-permute-start.8 = (f32[17,32,128]{2,1,0:T(8,128)S(1)}, f32[17,32,128]{2,1,0:T(8,128)S(1)}, u32[]{:S(2)}, u32[]{:S(2)}) collective-permute-start(f32[17,32,128]{2,1,0:T(8,128)S(1)} %get-tuple-element.38.own), channel_id=1, source_target_pairs={{0,1},{1,2},{2,3},{3,4},{4,5},{5,6},{6,7},{7,8},{8,9},{9,10},{10,1... | collective-permute-start | bytes 835592 | tf_op jit(solution)/shard_map/ppermute | solution.py:579
  84.9 9.1 %collective-permute-start.9 = (f32[17,32,128]{2,1,0:T(8,128)S(1)}, f32[17,32,128]{2,1,0:T(8,128)S(1)}, u32[]{:S(2)}, u32[]{:S(2)}) collective-permute-start(f32[17,32,128]{2,1,0:T(8,128)S(1)} %get-tuple-element.38.own), channel_id=1, source_target_pairs={{1,0},{2,1},{3,2},{4,3},{5,4},{6,5},{7,6},{8,7},{9,8},{10,9},{11,1... | collective-permute-start | bytes 835592 | tf_op jit(solution)/shard_map/ppermute | solution.py:579
  92.0 14.8 %collective-permute-start.10 = (f32[17,32,128]{2,1,0:T(8,128)S(1)}, f32[17,32,128]{2,1,0:T(8,128)S(1)}, u32[]{:S(2)}, u32[]{:S(2)}) collective-permute-start(f32[17,32,128]{2,1,0:T(8,128)S(1)} %collective-permute-done.8.left), channel_id=1, source_target_pairs={{0,1},{1,2},{2,3},{3,4},{4,5},{5,6},{6,7},{7,8},{8,9},{9,10},{10,1... | collective-permute-start | bytes 835592 | tf_op jit(solution)/shard_map/ppermute | solution.py:579
  93.9 12.8 %collective-permute-start.11 = (f32[17,32,128]{2,1,0:T(8,128)S(1)}, f32[17,32,128]{2,1,0:T(8,128)S(1)}, u32[]{:S(2)}, u32[]{:S(2)}) collective-permute-start(f32[17,32,128]{2,1,0:T(8,128)S(1)} %collective-permute-done.9.right), channel_id=1, source_target_pairs={{1,0},{2,1},{3,2},{4,3},{5,4},{6,5},{7,6},{8,7},{9,8},{10,9},{11,1... | collective-permute-start | bytes 835592 | tf_op jit(solution)/shard_map/ppermute | solution.py:579
  98.8 13.2 %collective-permute-start.12 = (f32[10,32,128]{2,1,0:T(8,128)S(1)}, f32[10,32,128]{2,1,0:T(8,128)S(1)}, u32[]{:S(2)}, u32[]{:S(2)}) collective-permute-start(f32[10,32,128]{2,1,0:T(8,128)S(1)} %get-tuple-element.39), channel_id=1, source_target_pairs={{0,16},{16,32},{32,48},{48,64},{64,80},{80,96},{96,112},{112,128},... | collective-permute-start | bytes 491528 | tf_op jit(solution)/shard_map/ppermute | solution.py:579
  101.1 14.2 %collective-permute-start.14 = (f32[10,32,128]{2,1,0:T(8,128)S(1)}, f32[10,32,128]{2,1,0:T(8,128)S(1)}, u32[]{:S(2)}, u32[]{:S(2)}) collective-permute-start(f32[10,32,128]{2,1,0:T(8,128)S(1)} %get-tuple-element.40), channel_id=1, source_target_pairs={{16,0},{32,16},{48,32},{64,48},{80,64},{96,80},{112,96},{128,112},... | collective-permute-start | bytes 491528 | tf_op jit(solution)/shard_map/ppermute | solution.py:579
  107.6 15.4 %all-to-all-start.1 = ((f32[16,5,8,128]{3,2,1,0:T(8,128)}), f32[16,5,8,128]{3,2,1,0:T(8,128)S(1)}, u32[]{:S(2)}, u32[]{:S(2)}) async-start(f32[16,5,8,128]{3,2,1,0:T(8,128)} %shard_map.51), calls=%async_computation.1 | async-start | bytes 655360 | tf_op jit(solution)/shard_map/all_to_all | solution.py:635
  112.0 18.2 %collective-permute-start.13 = (f32[10,32,128]{2,1,0:T(8,128)S(1)}, f32[10,32,128]{2,1,0:T(8,128)S(1)}, u32[]{:S(2)}, u32[]{:S(2)}) collective-permute-start(f32[10,32,128]{2,1,0:T(8,128)S(1)} %collective-permute-done.12.in_behind2), channel_id=1, source_target_pairs={{0,16},{16,32},{32,48},{48,64},{64,80},{80,96},{96,112},{112,128},... | collective-permute-start | bytes 491528 | tf_op jit(solution)/shard_map/ppermute | solution.py:579
  115.3 14.9 %collective-permute-start.15 = (f32[10,32,128]{2,1,0:T(8,128)S(1)}, f32[10,32,128]{2,1,0:T(8,128)S(1)}, u32[]{:S(2)}, u32[]{:S(2)}) collective-permute-start(f32[10,32,128]{2,1,0:T(8,128)S(1)} %collective-permute-done.14.in_ahead2), channel_id=1, source_target_pairs={{16,0},{32,16},{48,32},{64,48},{80,64},{96,80},{112,96},{128,112},... | collective-permute-start | bytes 491528 | tf_op jit(solution)/shard_map/ppermute | solution.py:579

commit v9 on v8

--- a/solution.py
+++ b/solution.py
@@ -253,7 +253,7 @@
         va[p] = scale * rhs
         t[p] = cut(extra, free)
 
-    planes(1, N0 - 1, operator0, 4)
+    planes(1, N0 - 1, operator0, 8)
     src, dst = va, vb
     for s in range(NU - 1):
         sweep(src, dst, f, g, fx, fy, fz, 2 + s, N0 - 2 - s, N0 // 2 - 2 - s)
@@ -275,7 +275,7 @@
         t1[2, q] = fz[p] + fz[p + 1]
         t1[3, q] = t[p] + t[p + 1]
 
-    planes(0, N1, coarsen1, 4)
+    planes(0, N1, coarsen1, 10)
     for a in range(4):
         for c in range(0, N1, 4):
             value = t1[a, c : c + 4].reshape(4 * NZ, 256)

time: 139 us -> 138 us (level)
  no operation moved by 1% of the time
where the time goes in v9:
time: 138 us
  starting transfers between devices  64.1 us (46%)
  Pallas kernels  33.2 us (24%)
  waiting for transfers between devices  27.4 us (20%)
  blocking collectives  12.6 us (9%)
    ppermute x16, starting transfers between devices, shift(): return lax.ppermute(value, axis, route)  59.7 us
    pallas_call x9, Pallas kernels, call(): pl.pallas_call(kernel, out_shape=[pltpu.HBM(s, F32) if i in apart_outs el...  33.2 us
    ppermute x16, waiting for transfers between devices, shift(): return lax.ppermute(value, axis, route)  27.4 us
    all_to_all x1, blocking collectives, body(): all3 = lax.all_to_all(own3, 'gx', 0, 0)  12.6 us
    all_to_all x1, starting transfers between devices, body(): rhs3 = lax.all_to_all(rhs3, 'gx', 0, 0)  4.39 us
  transfers between devices with their start and end apart: 17, of which 6 were waited for; matrix products, arithmetic and copies ran while one was open for 0% of the time, Pallas kernels for 8%

profile of v9, /device:TPU:130, one launch (start us, length us, event | category | flops | bytes accessed | tf_op | source)
XLA Modules:
  0.0 137.8 jit_solution(15464484753873621377)
XLA Ops:
  0.0 1.4 %shard_map.46 = (f32[4,16,32,128]{3,2,1,0:T(8,128)S(1)}, f32[50,32,128]{2,1,0:T(8,128)S(1)}, f32[49,32,128]{2,1,0:T(8,128)S(1)}) custom-call(s32[32,16,128]{2,1,0:T(8,128)} %in0.1, bf16[32,16,128]{2,1,0:T(8,128)(2,1)} %in1.1, bf16[32,16,128]{2,1,0:T(8,128)(2,1)} %in2.1, bf16[32,16,128]{2,1,0:T(8,128)(2,1)} %in3.1), custom_call_target="tpu_custom_call" | custom-call | tf_op jit(solution)/shard_map/pallas_call | solution.py:33
  1.4 3.5 %collective-permute-start = (f32[50,32,128]{2,1,0:T(8,128)S(1)}, f32[50,32,128]{2,1,0:T(8,128)S(1)}, u32[]{:S(2)}, u32[]{:S(2)}) collective-permute-start(f32[50,32,128]{2,1,0:T(8,128)S(1)} %get-tuple-element.26), channel_id=1, source_target_pairs={{0,16},{16,32},{32,48},{48,64},{64,80},{80,96},{96,112},{112,128},... | collective-permute-start | bytes 2457608 | tf_op jit(solution)/shard_map/ppermute | solution.py:579
  4.9 4.5 %collective-permute-start.1 = (f32[49,32,128]{2,1,0:T(8,128)S(1)}, f32[49,32,128]{2,1,0:T(8,128)S(1)}, u32[]{:S(2)}, u32[]{:S(2)}) collective-permute-start(f32[49,32,128]{2,1,0:T(8,128)S(1)} %get-tuple-element.27), channel_id=1, source_target_pairs={{16,0},{32,16},{48,32},{64,48},{80,64},{96,80},{112,96},{128,112},... | collective-permute-start | bytes 2408456 | tf_op jit(solution)/shard_map/ppermute | solution.py:579
  9.4 16.8 %collective-permute-done.1.ahead = f32[49,32,128]{2,1,0:T(8,128)S(1)} collective-permute-done((f32[49,32,128]{2,1,0:T(8,128)S(1)}, f32[49,32,128]{2,1,0:T(8,128)S(1)}, u32[]{:S(2)}, u32[]{:S(2)}) %collective-permute-start.1) | collective-permute-done | bytes 802848 | tf_op jit(solution)/shard_map/ppermute | solution.py:579
  26.2 0.7 shard_map.47
  26.9 1.9 %collective-permute-start.2 = (f32[4,6,32,128]{3,2,1,0:T(8,128)S(1)}, f32[4,6,32,128]{3,2,1,0:T(8,128)S(1)}, u32[]{:S(2)}, u32[]{:S(2)}) collective-permute-start(f32[4,6,32,128]{3,2,1,0:T(8,128)S(1)} %get-tuple-element.28), channel_id=1, source_target_pairs={{0,1},{1,2},{2,3},{3,4},{4,5},{5,6},{6,7},{7,8},{8,9},{9,10},{10,1... | collective-permute-start | bytes 1179656 | tf_op jit(solution)/shard_map/ppermute | solution.py:579
  28.8 4.9 %collective-permute-start.3 = (f32[4,6,32,128]{3,2,1,0:T(8,128)S(1)}, f32[4,6,32,128]{3,2,1,0:T(8,128)S(1)}, u32[]{:S(2)}, u32[]{:S(2)}) collective-permute-start(f32[4,6,32,128]{3,2,1,0:T(8,128)S(1)} %get-tuple-element.29), channel_id=1, source_target_pairs={{1,0},{2,1},{3,2},{4,3},{5,4},{6,5},{7,6},{8,7},{9,8},{10,9},{11,1... | collective-permute-start | bytes 1179656 | tf_op jit(solution)/shard_map/ppermute | solution.py:579
  33.7 3.5 %collective-permute-done.2.from_left = f32[4,6,32,128]{3,2,1,0:T(8,128)S(1)} collective-permute-done((f32[4,6,32,128]{3,2,1,0:T(8,128)S(1)}, f32[4,6,32,128]{3,2,1,0:T(8,128)S(1)}, u32[]{:S(2)}, u32[]{:S(2)}) %collective-permute-start.2) | collective-permute-done | bytes 393248 | tf_op jit(solution)/shard_map/ppermute | solution.py:579
  37.2 1.8 %collective-permute-done.3.from_right = f32[4,6,32,128]{3,2,1,0:T(8,128)S(1)} collective-permute-done((f32[4,6,32,128]{3,2,1,0:T(8,128)S(1)}, f32[4,6,32,128]{3,2,1,0:T(8,128)S(1)}, u32[]{:S(2)}, u32[]{:S(2)}) %collective-permute-start.3) | collective-permute-done | bytes 393248 | tf_op jit(solution)/shard_map/ppermute | solution.py:579
  38.9 11.9 %shard_map.48 = (f32[6,24,32,256]{3,2,1,0:T(8,128)}, f32[5,20,32,128]{3,2,1,0:T(8,128)}, f32[20,32,128]{2,1,0:T(8,128)}, f32[8,32,128]{2,1,0:T(8,128)S(1)}, f32[...) custom-call(f32[4,16,32,128]{3,2,1,0:T(8,128)S(1)} %get-tuple-elemen, ...), custom_call_target="tpu_custom_call" | custom-call | tf_op jit(solution)/shard_map/pallas_call | solution.py:33
  50.8 2.0 %collective-permute-start.4 = (f32[11,32,128]{2,1,0:T(8,128)S(1)}, f32[11,32,128]{2,1,0:T(8,128)S(1)}, u32[]{:S(2)}, u32[]{:S(2)}) collective-permute-start(f32[11,32,128]{2,1,0:T(8,128)S(1)} %get-tuple-element.30.own2), channel_id=1, source_target_pairs={{0,1},{1,2},{2,3},{3,4},{4,5},{5,6},{6,7},{7,8},{8,9},{9,10},{10,1... | collective-permute-start | bytes 540680 | tf_op jit(solution)/shard_map/ppermute | solution.py:579
  52.8 5.0 %collective-permute-start.5 = (f32[11,32,128]{2,1,0:T(8,128)S(1)}, f32[11,32,128]{2,1,0:T(8,128)S(1)}, u32[]{:S(2)}, u32[]{:S(2)}) collective-permute-start(f32[11,32,128]{2,1,0:T(8,128)S(1)} %get-tuple-element.33), channel_id=1, source_target_pairs={{1,0},{2,1},{3,2},{4,3},{5,4},{6,5},{7,6},{8,7},{9,8},{10,9},{11,1... | collective-permute-start | bytes 540680 | tf_op jit(solution)/shard_map/ppermute | solution.py:579
  57.8 1.2 collective-permute-done.4.left
  59.0 1.8 %collective-permute-done.5.right = f32[11,32,128]{2,1,0:T(8,128)S(1)} collective-permute-done((f32[11,32,128]{2,1,0:T(8,128)S(1)}, f32[11,32,128]{2,1,0:T(8,128)S(1)}, u32[]{:S(2)}, u32[]{:S(2)}) %collective-permute-start.5) | collective-permute-done | bytes 180256 | tf_op jit(solution)/shard_map/ppermute | solution.py:579
  61.0 3.4 %collective-permute-start.6 = (f32[17,32,128]{2,1,0:T(8,128)S(1)}, f32[17,32,128]{2,1,0:T(8,128)S(1)}, u32[]{:S(2)}, u32[]{:S(2)}) collective-permute-start(f32[17,32,128]{2,1,0:T(8,128)S(1)} %get-tuple-element.34), channel_id=1, source_target_pairs={{0,16},{16,32},{32,48},{48,64},{64,80},{80,96},{96,112},{112,128},... | collective-permute-start | bytes 835592 | tf_op jit(solution)/shard_map/ppermute | solution.py:579
  64.4 5.0 %collective-permute-start.7 = (f32[17,32,128]{2,1,0:T(8,128)S(1)}, f32[17,32,128]{2,1,0:T(8,128)S(1)}, u32[]{:S(2)}, u32[]{:S(2)}) collective-permute-start(f32[17,32,128]{2,1,0:T(8,128)S(1)} %get-tuple-element.36), channel_id=1, source_target_pairs={{16,0},{32,16},{48,32},{64,48},{80,64},{96,80},{112,96},{128,112},... | collective-permute-start | bytes 835592 | tf_op jit(solution)/shard_map/ppermute | solution.py:579
  69.4 12.6 %all_to_all.10.ops3 = f32[16,32,128]{2,1,0:T(8,128)S(1)} all-to-all(f32[16,32,128]{2,1,0:T(8,128)S(1)} %get-tuple-element.37), channel_id=1, replica_groups=mesh['gx'=16,'gy'=16] {'gx'}, dimensions={0} | all-to-all | bytes 524288 | tf_op jit(solution)/shard_map/all_to_all | solution.py:617
  82.1 0.7 shard_map.50
  82.7 1.9 %collective-permute-start.8 = (f32[17,32,128]{2,1,0:T(8,128)S(1)}, f32[17,32,128]{2,1,0:T(8,128)S(1)}, u32[]{:S(2)}, u32[]{:S(2)}) collective-permute-start(f32[17,32,128]{2,1,0:T(8,128)S(1)} %get-tuple-element.38.own), channel_id=1, source_target_pairs={{0,1},{1,2},{2,3},{3,4},{4,5},{5,6},{6,7},{7,8},{8,9},{9,10},{10,1... | collective-permute-start | bytes 835592 | tf_op jit(solution)/shard_map/ppermute | solution.py:579
  84.7 4.9 %collective-permute-start.9 = (f32[17,32,128]{2,1,0:T(8,128)S(1)}, f32[17,32,128]{2,1,0:T(8,128)S(1)}, u32[]{:S(2)}, u32[]{:S(2)}) collective-permute-start(f32[17,32,128]{2,1,0:T(8,128)S(1)} %get-tuple-element.38.own), channel_id=1, source_target_pairs={{1,0},{2,1},{3,2},{4,3},{5,4},{6,5},{7,6},{8,7},{9,8},{10,9},{11,1... | collective-permute-start | bytes 835592 | tf_op jit(solution)/shard_map/ppermute | solution.py:579
  89.5 2.3 %collective-permute-done.8.left = f32[17,32,128]{2,1,0:T(8,128)S(1)} collective-permute-done((f32[17,32,128]{2,1,0:T(8,128)S(1)}, f32[17,32,128]{2,1,0:T(8,128)S(1)}, u32[]{:S(2)}, u32[]{:S(2)}) %collective-permute-start.8) | collective-permute-done | bytes 278560 | tf_op jit(solution)/shard_map/ppermute | solution.py:579
  91.8 1.9 %collective-permute-start.10 = (f32[17,32,128]{2,1,0:T(8,128)S(1)}, f32[17,32,128]{2,1,0:T(8,128)S(1)}, u32[]{:S(2)}, u32[]{:S(2)}) collective-permute-start(f32[17,32,128]{2,1,0:T(8,128)S(1)} %collective-permute-done.8.left), channel_id=1, source_target_pairs={{0,1},{1,2},{2,3},{3,4},{4,5},{5,6},{6,7},{7,8},{8,9},{9,10},{10,1... | collective-permute-start | bytes 835592 | tf_op jit(solution)/shard_map/ppermute | solution.py:579
  93.7 4.9 %collective-permute-start.11 = (f32[17,32,128]{2,1,0:T(8,128)S(1)}, f32[17,32,128]{2,1,0:T(8,128)S(1)}, u32[]{:S(2)}, u32[]{:S(2)}) collective-permute-start(f32[17,32,128]{2,1,0:T(8,128)S(1)} %collective-permute-done.9.right), channel_id=1, source_target_pairs={{1,0},{2,1},{3,2},{4,3},{5,4},{6,5},{7,6},{8,7},{9,8},{10,9},{11,1... | collective-permute-start | bytes 835592 | tf_op jit(solution)/shard_map/ppermute | solution.py:579
  98.6 2.3 %collective-permute-start.12 = (f32[10,32,128]{2,1,0:T(8,128)S(1)}, f32[10,32,128]{2,1,0:T(8,128)S(1)}, u32[]{:S(2)}, u32[]{:S(2)}) collective-permute-start(f32[10,32,128]{2,1,0:T(8,128)S(1)} %get-tuple-element.39), channel_id=1, source_target_pairs={{0,16},{16,32},{32,48},{48,64},{64,80},{80,96},{96,112},{112,128},... | collective-permute-start | bytes 491528 | tf_op jit(solution)/shard_map/ppermute | solution.py:579
  100.9 5.6 %collective-permute-start.14 = (f32[10,32,128]{2,1,0:T(8,128)S(1)}, f32[10,32,128]{2,1,0:T(8,128)S(1)}, u32[]{:S(2)}, u32[]{:S(2)}) collective-permute-start(f32[10,32,128]{2,1,0:T(8,128)S(1)} %get-tuple-element.40), channel_id=1, source_target_pairs={{16,0},{32,16},{48,32},{64,48},{80,64},{96,80},{112,96},{128,112},... | collective-permute-start | bytes 491528 | tf_op jit(solution)/shard_map/ppermute | solution.py:579
  106.6 0.8 shard_map.51
  107.4 4.4 %all-to-all-start.1 = ((f32[16,5,8,128]{3,2,1,0:T(8,128)}), f32[16,5,8,128]{3,2,1,0:T(8,128)S(1)}, u32[]{:S(2)}, u32[]{:S(2)}) async-start(f32[16,5,8,128]{3,2,1,0:T(8,128)} %shard_map.51), calls=%async_computation.1 | async-start | bytes 655360 | tf_op jit(solution)/shard_map/all_to_all | solution.py:635
  111.8 3.4 %collective-permute-start.13 = (f32[10,32,128]{2,1,0:T(8,128)S(1)}, f32[10,32,128]{2,1,0:T(8,128)S(1)}, u32[]{:S(2)}, u32[]{:S(2)}) collective-permute-start(f32[10,32,128]{2,1,0:T(8,128)S(1)} %collective-permute-done.12.in_behind2), channel_id=1, source_target_pairs={{0,16},{16,32},{32,48},{48,64},{64,80},{80,96},{96,112},{112,128},... | collective-permute-start | bytes 491528 | tf_op jit(solution)/shard_map/ppermute | solution.py:579
  115.2 4.8 %collective-permute-start.15 = (f32[10,32,128]{2,1,0:T(8,128)S(1)}, f32[10,32,128]{2,1,0:T(8,128)S(1)}, u32[]{:S(2)}, u32[]{:S(2)}) collective-permute-start(f32[10,32,128]{2,1,0:T(8,128)S(1)} %collective-permute-done.14.in_ahead2), channel_id=1, source_target_pairs={{16,0},{32,16},{48,32},{64,48},{80,64},{96,80},{112,96},{128,112},... | collective-permute-start | bytes 491528 | tf_op jit(solution)/shard_map/ppermute | solution.py:579
  119.9 2.8 %shard_map.52.in_ops3 = f32[4,32,32,128]{3,2,1,0:T(8,128)} custom-call(f32[17,32,128]{2,1,0:T(8,128)S(1)} %get-tuple-element.38.own, f32[17,32,128]{2,1,0:T(8,128)S(1)} %collective-permute-done.8.left, f32[17,32,128]{2,1,0:T(8,128)S(1)} %collective-permute-done.9.right, f32[17,32,128]{2,1,0:T(8,128)S(1)} %collective-permute-done.10.left_far, ...), custom_call_target="tpu_custom_call" | custom-call | tf_op jit(solution)/shard_map/pallas_call | solution.py:33
  122.7 7.2 %shard_map.53.e3 = f32[10,32,128]{2,1,0:T(8,128)S(1)} custom-call(f32[16,5,8,128]{3,2,1,0:T(8,128)S(1)} %all-to-all-done.1.gathered, f32[4,32,32,128]{3,2,1,0:T(8,128)} %shard_map.52.in_ops3), custom_call_target="tpu_custom_call" | custom-call | tf_op jit(solution)/shard_map/pallas_call | solution.py:33
  130.0 7.6 %shard_map.54 = f32[32,16,128]{2,1,0:T(8,128)} custom-call(f32[10,32,128]{2,1,0:T(8,128)S(1)} %shard_map.53.e3, f32[10,32,128]{2,1,0:T(8,128)S(1)} %collective-permute-done.13.in_behind3, f32[10,32,128]{2,1,0:T(8,128)S(1)} %collective-permute-done.12.in_behind2, f32[17,32,128]{2,1,0:T(8,128)S(1)} %collective-permute-done.6.behind.in_behind, ...), custom_call_target="tpu_custom_call" | custom-call | tf_op jit(solution)/shard_map/pallas_call | solution.py:33
  (12 shorter events, 0.2 us)
Async XLA Ops:
  1.4 24.8 %collective-permute-start = (f32[50,32,128]{2,1,0:T(8,128)S(1)}, f32[50,32,128]{2,1,0:T(8,128)S(1)}, u32[]{:S(2)}, u32[]{:S(2)}) collective-permute-start(f32[50,32,128]{2,1,0:T(8,128)S(1)} %get-tuple-element.26), channel_id=1, source_target_pairs={{0,16},{16,32},{32,48},{48,64},{64,80},{80,96},{96,112},{112,128},... | collective-permute-start | bytes 2457608 | tf_op jit(solution)/shard_map/ppermute | solution.py:579
  4.9 21.3 %collective-permute-start.1 = (f32[49,32,128]{2,1,0:T(8,128)S(1)}, f32[49,32,128]{2,1,0:T(8,128)S(1)}, u32[]{:S(2)}, u32[]{:S(2)}) collective-permute-start(f32[49,32,128]{2,1,0:T(8,128)S(1)} %get-tuple-element.27), channel_id=1, source_target_pairs={{16,0},{32,16},{48,32},{64,48},{80,64},{96,80},{112,96},{128,112},... | collective-permute-start | bytes 2408456 | tf_op jit(solution)/shard_map/ppermute | solution.py:579
  26.9 10.3 %collective-permute-start.2 = (f32[4,6,32,128]{3,2,1,0:T(8,128)S(1)}, f32[4,6,32,128]{3,2,1,0:T(8,128)S(1)}, u32[]{:S(2)}, u32[]{:S(2)}) collective-permute-start(f32[4,6,32,128]{3,2,1,0:T(8,128)S(1)} %get-tuple-element.28), channel_id=1, source_target_pairs={{0,1},{1,2},{2,3},{3,4},{4,5},{5,6},{6,7},{7,8},{8,9},{9,10},{10,1... | collective-permute-start | bytes 1179656 | tf_op jit(solution)/shard_map/ppermute | solution.py:579
  28.8 10.1 %collective-permute-start.3 = (f32[4,6,32,128]{3,2,1,0:T(8,128)S(1)}, f32[4,6,32,128]{3,2,1,0:T(8,128)S(1)}, u32[]{:S(2)}, u32[]{:S(2)}) collective-permute-start(f32[4,6,32,128]{3,2,1,0:T(8,128)S(1)} %get-tuple-element.29), channel_id=1, source_target_pairs={{1,0},{2,1},{3,2},{4,3},{5,4},{6,5},{7,6},{8,7},{9,8},{10,9},{11,1... | collective-permute-start | bytes 1179656 | tf_op jit(solution)/shard_map/ppermute | solution.py:579
  50.8 8.2 %collective-permute-start.4 = (f32[11,32,128]{2,1,0:T(8,128)S(1)}, f32[11,32,128]{2,1,0:T(8,128)S(1)}, u32[]{:S(2)}, u32[]{:S(2)}) collective-permute-start(f32[11,32,128]{2,1,0:T(8,128)S(1)} %get-tuple-element.30.own2), channel_id=1, source_target_pairs={{0,1},{1,2},{2,3},{3,4},{4,5},{5,6},{6,7},{7,8},{8,9},{9,10},{10,1... | collective-permute-start | bytes 540680 | tf_op jit(solution)/shard_map/ppermute | solution.py:579
  52.8 8.0 %collective-permute-start.5 = (f32[11,32,128]{2,1,0:T(8,128)S(1)}, f32[11,32,128]{2,1,0:T(8,128)S(1)}, u32[]{:S(2)}, u32[]{:S(2)}) collective-permute-start(f32[11,32,128]{2,1,0:T(8,128)S(1)} %get-tuple-element.33), channel_id=1, source_target_pairs={{1,0},{2,1},{3,2},{4,3},{5,4},{6,5},{7,6},{8,7},{9,8},{10,9},{11,1... | collective-permute-start | bytes 540680 | tf_op jit(solution)/shard_map/ppermute | solution.py:579
  61.0 21.1 %collective-permute-start.6 = (f32[17,32,128]{2,1,0:T(8,128)S(1)}, f32[17,32,128]{2,1,0:T(8,128)S(1)}, u32[]{:S(2)}, u32[]{:S(2)}) collective-permute-start(f32[17,32,128]{2,1,0:T(8,128)S(1)} %get-tuple-element.34), channel_id=1, source_target_pairs={{0,16},{16,32},{32,48},{48,64},{64,80},{80,96},{96,112},{112,128},... | collective-permute-start | bytes 835592 | tf_op jit(solution)/shard_map/ppermute | solution.py:579
  64.4 17.7 %collective-permute-start.7 = (f32[17,32,128]{2,1,0:T(8,128)S(1)}, f32[17,32,128]{2,1,0:T(8,128)S(1)}, u32[]{:S(2)}, u32[]{:S(2)}) collective-permute-start(f32[17,32,128]{2,1,0:T(8,128)S(1)} %get-tuple-element.36), channel_id=1, source_target_pairs={{16,0},{32,16},{48,32},{64,48},{80,64},{96,80},{112,96},{128,112},... | collective-permute-start | bytes 835592 | tf_op jit(solution)/shard_map/ppermute | solution.py:579
  82.7 9.1 %collective-permute-start.8 = (f32[17,32,128]{2,1,0:T(8,128)S(1)}, f32[17,32,128]{2,1,0:T(8,128)S(1)}, u32[]{:S(2)}, u32[]{:S(2)}) collective-permute-start(f32[17,32,128]{2,1,0:T(8,128)S(1)} %get-tuple-element.38.own), channel_id=1, source_target_pairs={{0,1},{1,2},{2,3},{3,4},{4,5},{5,6},{6,7},{7,8},{8,9},{9,10},{10,1... | collective-permute-start | bytes 835592 | tf_op jit(solution)/shard_map/ppermute | solution.py:579
  84.7 9.1 %collective-permute-start.9 = (f32[17,32,128]{2,1,0:T(8,128)S(1)}, f32[17,32,128]{2,1,0:T(8,128)S(1)}, u32[]{:S(2)}, u32[]{:S(2)}) collective-permute-start(f32[17,32,128]{2,1,0:T(8,128)S(1)} %get-tuple-element.38.own), channel_id=1, source_target_pairs={{1,0},{2,1},{3,2},{4,3},{5,4},{6,5},{7,6},{8,7},{9,8},{10,9},{11,1... | collective-permute-start | bytes 835592 | tf_op jit(solution)/shard_map/ppermute | solution.py:579
  91.8 14.8 %collective-permute-start.10 = (f32[17,32,128]{2,1,0:T(8,128)S(1)}, f32[17,32,128]{2,1,0:T(8,128)S(1)}, u32[]{:S(2)}, u32[]{:S(2)}) collective-permute-start(f32[17,32,128]{2,1,0:T(8,128)S(1)} %collective-permute-done.8.left), channel_id=1, source_target_pairs={{0,1},{1,2},{2,3},{3,4},{4,5},{5,6},{6,7},{7,8},{8,9},{9,10},{10,1... | collective-permute-start | bytes 835592 | tf_op jit(solution)/shard_map/ppermute | solution.py:579
  93.7 12.8 %collective-permute-start.11 = (f32[17,32,128]{2,1,0:T(8,128)S(1)}, f32[17,32,128]{2,1,0:T(8,128)S(1)}, u32[]{:S(2)}, u32[]{:S(2)}) collective-permute-start(f32[17,32,128]{2,1,0:T(8,128)S(1)} %collective-permute-done.9.right), channel_id=1, source_target_pairs={{1,0},{2,1},{3,2},{4,3},{5,4},{6,5},{7,6},{8,7},{9,8},{10,9},{11,1... | collective-permute-start | bytes 835592 | tf_op jit(solution)/shard_map/ppermute | solution.py:579
  98.6 13.2 %collective-permute-start.12 = (f32[10,32,128]{2,1,0:T(8,128)S(1)}, f32[10,32,128]{2,1,0:T(8,128)S(1)}, u32[]{:S(2)}, u32[]{:S(2)}) collective-permute-start(f32[10,32,128]{2,1,0:T(8,128)S(1)} %get-tuple-element.39), channel_id=1, source_target_pairs={{0,16},{16,32},{32,48},{48,64},{64,80},{80,96},{96,112},{112,128},... | collective-permute-start | bytes 491528 | tf_op jit(solution)/shard_map/ppermute | solution.py:579
  100.9 14.2 %collective-permute-start.14 = (f32[10,32,128]{2,1,0:T(8,128)S(1)}, f32[10,32,128]{2,1,0:T(8,128)S(1)}, u32[]{:S(2)}, u32[]{:S(2)}) collective-permute-start(f32[10,32,128]{2,1,0:T(8,128)S(1)} %get-tuple-element.40), channel_id=1, source_target_pairs={{16,0},{32,16},{48,32},{64,48},{80,64},{96,80},{112,96},{128,112},... | collective-permute-start | bytes 491528 | tf_op jit(solution)/shard_map/ppermute | solution.py:579
  107.4 15.4 %all-to-all-start.1 = ((f32[16,5,8,128]{3,2,1,0:T(8,128)}), f32[16,5,8,128]{3,2,1,0:T(8,128)S(1)}, u32[]{:S(2)}, u32[]{:S(2)}) async-start(f32[16,5,8,128]{3,2,1,0:T(8,128)} %shard_map.51), calls=%async_computation.1 | async-start | bytes 655360 | tf_op jit(solution)/shard_map/all_to_all | solution.py:635
  111.8 18.2 %collective-permute-start.13 = (f32[10,32,128]{2,1,0:T(8,128)S(1)}, f32[10,32,128]{2,1,0:T(8,128)S(1)}, u32[]{:S(2)}, u32[]{:S(2)}) collective-permute-start(f32[10,32,128]{2,1,0:T(8,128)S(1)} %collective-permute-done.12.in_behind2), channel_id=1, source_target_pairs={{0,16},{16,32},{32,48},{48,64},{64,80},{80,96},{96,112},{112,128},... | collective-permute-start | bytes 491528 | tf_op jit(solution)/shard_map/ppermute | solution.py:579
  115.2 14.9 %collective-permute-start.15 = (f32[10,32,128]{2,1,0:T(8,128)S(1)}, f32[10,32,128]{2,1,0:T(8,128)S(1)}, u32[]{:S(2)}, u32[]{:S(2)}) collective-permute-start(f32[10,32,128]{2,1,0:T(8,128)S(1)} %collective-permute-done.14.in_ahead2), channel_id=1, source_target_pairs={{16,0},{32,16},{48,32},{64,48},{80,64},{96,80},{112,96},{128,112},... | collective-permute-start | bytes 491528 | tf_op jit(solution)/shard_map/ppermute | solution.py:579
